TPU v7x, 32 devices: a whole 2x2x4 slice. The times are simulated.
32 devices in a mesh: dp: 4 (over z), fsdp: 8 (over y, x, core).
Axes of the slice: x: 2, y: 2, z: 4, core: 2. Of those that a mesh axis runs over, the one named last changes fastest.
Arguments:
- tokens: bfloat16 [64, 1024, 512], P(('dp', 'fsdp')), may hold values from -6 to 6
- flat_params: float32 [2699264], P(('dp', 'fsdp')), may hold values from -4 to 4, as said below
- segments: int32 [64, 1024], P(('dp', 'fsdp')), may hold values from 0 to 31, never falling along the last dimension, each value on 1 to 64 neighbouring positions
- experts: int32 [64, 1024, 2], P(('dp', 'fsdp')), may hold values from 0 to 7, all different within a row
- counts: int32 [64], P(('dp', 'fsdp')), may hold values from 512 to 1024, as said below
- cotangent: bfloat16 [64, 1024, 512], P(('dp', 'fsdp')), may hold values from -6 to 6
Outputs:
- output: bfloat16 [64, 1024, 512], P(('dp', 'fsdp'))
- grad_tokens: bfloat16 [64, 1024, 512], P(('dp', 'fsdp'))
- grad_flat: float32 [2699264], P(('dp', 'fsdp'))
Inputs may be any that keep to these rules, and one draw needn't show every extreme that they name: `flat_params`: packed parameters in the order of the first step. `counts`: positions from this count on are padding; some row has exactly 1024 real tokens and another exactly 512. For each token slot, its 2 entries along the last dimension name different experts; across the token slots of a packed row the same experts recur freely.
All inputs are finite; a program needn't handle non-finite values.
Results may differ from a plain program's by a relative error of at most 0.0074.
Values may be sent and summed in bfloat16 or wider, within the bound.
No kernel may reach another device: no remote copies, remote signals or barrier semaphores. Data moves between devices by JAX's collectives and lax.ppermute only.
A program may use at most 192 MiB of HBM per device.

v0:
```python
from functools import partial
import math

import jax
import jax.numpy as jnp
from jax import lax
from jax.sharding import PartitionSpec as P

D = 512
FF = 2048
EXPERTS = 8
HEAD = 64


EPS = 1e-05
NEG = -1e30


def split_params(flat):
    shapes = [
        (D, EXPERTS * HEAD),
        (D, HEAD),
        (D, HEAD),
        (EXPERTS * HEAD, D),
        (D, FF),
        (FF, D),
        (D, EXPERTS),
        (FF,),
        (D,),
        (D,),
        (D,),
        (D,),
        (D,),
    ]
    pieces = []
    offset = 0
    for target in shapes:
        amount = math.prod(target)
        pieces.append(flat[offset : offset + amount].reshape(target))
        offset = offset + amount
    return pieces


def norm_parts(source):
    center = source - jnp.mean(source, axis=-1, keepdims=True)
    scaler = lax.rsqrt(jnp.mean(center * center, axis=-1, keepdims=True) + EPS)
    return (center * scaler, scaler)


def norm_back(grad_out, normal, scaler, gain):
    grad_normal = grad_out * gain
    grad_in = scaler * (
        grad_normal
        - jnp.mean(grad_normal, axis=-1, keepdims=True)
        - normal * jnp.mean(grad_normal * normal, axis=-1, keepdims=True)
    )
    return (grad_in, jnp.sum(grad_out * normal, axis=0), jnp.sum(grad_out, axis=0))


def row_allowed(segment_row, validity_row, first_row, last_row):
    places = jnp.arange(segment_row.shape[0], dtype=jnp.int32)
    allowed = (
        (segment_row[first_row:last_row, None] == segment_row[None, :])
        & validity_row[first_row:last_row, None]
        & validity_row[None, :]
    )
    return allowed | (places[first_row:last_row, None] == places[None, :])


def attend_row(inputs_row):
    queries, key_rows, value_rows, segment_row, validity_row = inputs_row
    length = queries.shape[0]
    block_rows = min(512, length)
    factor = HEAD ** (-0.5)
    outputs = []
    totals = []
    for first_row in range(0, length, block_rows):
        last_row = first_row + block_rows
        scores = (
            jnp.einsum(
                "qeh,kh->eqk",
                queries[first_row:last_row],
                key_rows,
                preferred_element_type=jnp.float32,
            )
            * factor
        )
        scores = jnp.where(
            row_allowed(segment_row, validity_row, first_row, last_row)[None], scores, NEG
        )
        peak = jnp.max(scores, axis=-1, keepdims=True)
        expd = jnp.exp(scores - peak)
        summed = jnp.sum(expd, axis=-1, keepdims=True)
        weights_soft = (expd / summed).astype(jnp.bfloat16)
        outputs.append(
            jnp.einsum("eqk,kh->qeh", weights_soft, value_rows, preferred_element_type=jnp.float32)
        )
        totals.append((peak + jnp.log(summed))[:, :, 0])
    return (jnp.concatenate(outputs, axis=0), jnp.concatenate(totals, axis=1))


def attend_back(inputs_row):
    queries, key_rows, value_rows, grad_att, log_total, segment_row, validity_row = inputs_row
    length = queries.shape[0]
    block_rows = min(512, length)
    factor = HEAD ** (-0.5)
    grad_key = jnp.zeros(key_rows.shape, jnp.float32)
    grad_value = jnp.zeros(value_rows.shape, jnp.float32)
    grad_queries = []
    for first_row in range(0, length, block_rows):
        last_row = first_row + block_rows
        query_block = queries[first_row:last_row]
        grad_block = grad_att[first_row:last_row]
        scores = (
            jnp.einsum("qeh,kh->eqk", query_block, key_rows, preferred_element_type=jnp.float32)
            * factor
        )
        scores = jnp.where(
            row_allowed(segment_row, validity_row, first_row, last_row)[None], scores, NEG
        )
        weights_soft = jnp.exp(scores - log_total[:, first_row:last_row, None])
        grad_soft = jnp.einsum(
            "qeh,kh->eqk", grad_block, value_rows, preferred_element_type=jnp.float32
        )
        grad_value = grad_value + jnp.einsum(
            "eqk,qeh->kh",
            weights_soft.astype(jnp.bfloat16),
            grad_block,
            preferred_element_type=jnp.float32,
        )
        grad_scores = weights_soft * (
            grad_soft - jnp.sum(weights_soft * grad_soft, axis=-1, keepdims=True)
        )
        grad_scores = grad_scores.astype(jnp.bfloat16)
        grad_queries.append(
            jnp.einsum("eqk,kh->qeh", grad_scores, key_rows, preferred_element_type=jnp.float32)
            * factor
        )
        grad_key = (
            grad_key
            + jnp.einsum(
                "eqk,qeh->kh", grad_scores, query_block, preferred_element_type=jnp.float32
            )
            * factor
        )
    return (jnp.concatenate(grad_queries, axis=0), grad_key, grad_value)


def local(tokens, flat_params, segments, experts, counts, cotangent):
    row_count, length = (tokens.shape[0], tokens.shape[1])
    tok_count = row_count * length
    source = tokens.reshape(tok_count, D).astype(jnp.float32)
    valid_rows = jnp.arange(length, dtype=jnp.int32)[None, :] < counts[:, None]
    validity = valid_rows.reshape(tok_count, 1).astype(jnp.float32)
    low_params = flat_params.astype(jnp.bfloat16)
    gathered = lax.all_gather(low_params, ("dp", "fsdp"), axis=0, tiled=True)
    (
        w_query,
        w_key,
        w_value,
        w_out,
        w_up,
        w_down,
        w_router,
        bias_up,
        gain_one,
        shift_one,
        gain_two,
        shift_two,
        bias_down,
    ) = split_params(gathered)
    normal_one, scaler_one = norm_parts(source)
    normed = (normal_one * gain_one.astype(jnp.float32) + shift_one.astype(jnp.float32)).astype(
        jnp.bfloat16
    )
    logits = jnp.dot(normed, w_router, preferred_element_type=jnp.float32)
    shifted = jnp.exp(logits - jnp.max(logits, axis=-1, keepdims=True))
    router_prob = shifted / jnp.sum(shifted, axis=-1, keepdims=True)
    expert_rows = experts.reshape(tok_count, 2)
    expert_ids = jnp.arange(EXPERTS, dtype=jnp.int32)[None, :]
    chosen = ((expert_rows[:, 0:1] == expert_ids) | (expert_rows[:, 1:2] == expert_ids)).astype(
        jnp.float32
    )
    gating = router_prob * chosen
    queries = jnp.dot(normed, w_query, preferred_element_type=jnp.float32).astype(jnp.bfloat16)
    key_rows = jnp.dot(normed, w_key, preferred_element_type=jnp.float32).astype(jnp.bfloat16)
    value_rows = jnp.dot(normed, w_value, preferred_element_type=jnp.float32).astype(jnp.bfloat16)
    query_rows = queries.reshape(row_count, length, EXPERTS, HEAD)
    key_by_row = key_rows.reshape(row_count, length, HEAD)
    value_by_row = value_rows.reshape(row_count, length, HEAD)
    attended, log_total = lax.map(
        attend_row, (query_rows, key_by_row, value_by_row, segments, valid_rows)
    )
    attended = attended.reshape(tok_count, EXPERTS, HEAD)
    mixed_heads = (
        (gating[:, :, None] * attended).astype(jnp.bfloat16).reshape(tok_count, EXPERTS * HEAD)
    )
    middle = source + jnp.dot(mixed_heads, w_out, preferred_element_type=jnp.float32)
    normal_two, scaler_two = norm_parts(middle)
    normed_two = (normal_two * gain_two.astype(jnp.float32) + shift_two.astype(jnp.float32)).astype(
        jnp.bfloat16
    )
    hidden_pre = jnp.dot(normed_two, w_up, preferred_element_type=jnp.float32) + bias_up.astype(
        jnp.float32
    )
    hidden = jax.nn.gelu(hidden_pre, approximate=True).astype(jnp.bfloat16)
    result = jnp.dot(hidden, w_down, preferred_element_type=jnp.float32) + bias_down.astype(
        jnp.float32
    )
    output = (validity * (middle + result)).astype(jnp.bfloat16).reshape(row_count, length, D)
    back_params = lax.all_gather(low_params, ("dp", "fsdp"), axis=0, tiled=True)
    (
        b_query,
        b_key,
        b_value,
        b_out,
        b_up,
        b_down,
        b_router,
        unused_up,
        b_gain_one,
        unused_one,
        b_gain_two,
        unused_two,
        unused_down,
    ) = split_params(back_params)
    grad_out = cotangent.reshape(tok_count, D).astype(jnp.float32) * validity
    grad_res = grad_out.astype(jnp.bfloat16)
    grad_w_down = jnp.einsum("tf,td->fd", hidden, grad_res, preferred_element_type=jnp.float32)
    grad_b_down = jnp.sum(grad_res.astype(jnp.float32), axis=0)
    grad_hidden = jnp.einsum("td,fd->tf", grad_res, b_down, preferred_element_type=jnp.float32)
    unused_value, gelu_pull = jax.vjp(partial(jax.nn.gelu, approximate=True), hidden_pre)
    grad_pre = gelu_pull(grad_hidden)[0].astype(jnp.bfloat16)
    grad_w_up = jnp.einsum("td,tf->df", normed_two, grad_pre, preferred_element_type=jnp.float32)
    grad_b_up = jnp.sum(grad_pre.astype(jnp.float32), axis=0)
    grad_normed_two = jnp.einsum("tf,df->td", grad_pre, b_up, preferred_element_type=jnp.float32)
    grad_mid_norm, grad_gain_two, grad_shift_two = norm_back(
        grad_normed_two, normal_two, scaler_two, b_gain_two.astype(jnp.float32)
    )
    grad_middle = grad_out + grad_mid_norm
    grad_branch = grad_middle.astype(jnp.bfloat16)
    grad_w_out = jnp.einsum(
        "tc,td->cd", mixed_heads, grad_branch, preferred_element_type=jnp.float32
    )
    grad_mixed = jnp.einsum(
        "td,cd->tc", grad_branch, b_out, preferred_element_type=jnp.float32
    ).reshape(tok_count, EXPERTS, HEAD)
    grad_gating = jnp.sum(grad_mixed * attended, axis=-1)
    grad_att = (grad_mixed * gating[:, :, None]).astype(jnp.bfloat16)
    grad_prob = grad_gating * chosen
    grad_logits = (
        router_prob * (grad_prob - jnp.sum(router_prob * grad_prob, axis=-1, keepdims=True))
    ).astype(jnp.bfloat16)
    grad_q, grad_k, grad_v = lax.map(
        attend_back,
        (
            query_rows,
            key_by_row,
            value_by_row,
            grad_att.reshape(row_count, length, EXPERTS, HEAD),
            log_total,
            segments,
            valid_rows,
        ),
    )
    grad_query = grad_q.astype(jnp.bfloat16).reshape(tok_count, EXPERTS * HEAD)
    grad_key = grad_k.astype(jnp.bfloat16).reshape(tok_count, HEAD)
    grad_value = grad_v.astype(jnp.bfloat16).reshape(tok_count, HEAD)
    grad_w_query = jnp.einsum("td,tc->dc", normed, grad_query, preferred_element_type=jnp.float32)
    grad_w_key = jnp.einsum("td,tc->dc", normed, grad_key, preferred_element_type=jnp.float32)
    grad_w_value = jnp.einsum("td,tc->dc", normed, grad_value, preferred_element_type=jnp.float32)
    grad_w_router = jnp.einsum("td,tc->dc", normed, grad_logits, preferred_element_type=jnp.float32)
    grad_normed = jnp.einsum("tc,dc->td", grad_query, b_query, preferred_element_type=jnp.float32)
    grad_normed = grad_normed + jnp.einsum(
        "tc,dc->td", grad_key, b_key, preferred_element_type=jnp.float32
    )
    grad_normed = grad_normed + jnp.einsum(
        "tc,dc->td", grad_value, b_value, preferred_element_type=jnp.float32
    )
    grad_normed = grad_normed + jnp.einsum(
        "tc,dc->td", grad_logits, b_router, preferred_element_type=jnp.float32
    )
    grad_in_norm, grad_gain_one, grad_shift_one = norm_back(
        grad_normed, normal_one, scaler_one, b_gain_one.astype(jnp.float32)
    )
    grad_input = (grad_middle + grad_in_norm).astype(jnp.bfloat16).reshape(row_count, length, D)
    grad_pieces = [
        grad_w_query,
        grad_w_key,
        grad_w_value,
        grad_w_out,
        grad_w_up,
        grad_w_down,
        grad_w_router,
        grad_b_up,
        grad_gain_one,
        grad_shift_one,
        grad_gain_two,
        grad_shift_two,
        grad_b_down,
    ]
    local_grads = jnp.concatenate([piece.reshape(-1) for piece in grad_pieces])
    local_grads = jnp.concatenate(
        [local_grads, jnp.zeros((gathered.shape[0] - local_grads.shape[0],), jnp.float32)]
    )
    grad_shard = lax.psum_scatter(local_grads, ("dp", "fsdp"), scatter_dimension=0, tiled=True)
    return (output, grad_input, grad_shard)


def solution(mesh):
    return jax.shard_map(
        local,
        mesh=mesh,
        in_specs=(
            P(("dp", "fsdp"), None, None),
            P(("dp", "fsdp")),
            P(("dp", "fsdp"), None),
            P(("dp", "fsdp"), None, None),
            P(("dp", "fsdp")),
            P(("dp", "fsdp"), None, None),
        ),
        out_specs=(P(("dp", "fsdp"), None, None), P(("dp", "fsdp"), None, None), P(("dp", "fsdp"))),
        check_vma=False,
    )
```

profile of v0, /device:TPU:0, one launch (start us, length us, event | category | flops | bytes accessed | tf_op | source)
XLA Modules:
  0.0 908.6 jit_solution(16997537187070233372)
XLA Ops:
  16.8 85.4 %all-gather.3.cloned.1.call-done = bf16[32,1,84352]{2,1,0:T(2,128)(2,1)} async-done(((bf16[1,1,84352]{2,1,0:T(2,128)(2,1)}), bf16[32,1,84352]{2,1,0:T(2,128)(2,1)}) %all-gather.3.cloned.1.call-update) | async-done | bytes 5398544 | tf_op jit(solution)/shard_map/all_gather | solution.py:156
  102.2 99.3 %reduce.9 = bf16[32,84352]{1,0:T(8,128)(2,1)} reduce(bf16[32,1,84352]{2,1,0:T(2,128)(2,1)} %all-gather.3.cloned.1.call-done, bf16[]{:T(256)} %constant.101), dimensions={1}, to_apply=%all-gather.reduce_sub_computation | reduce | bytes 10797058 | tf_op jit(solution)/shard_map/all_gather | solution.py:156
  201.5 10.6 %reshape.720 = bf16[2699264]{0:T(1024)(128)(2,1)} reshape(bf16[32,84352]{1,0:T(8,128)(2,1)} %reduce.9) | data formatting | bytes 10797056
  252.4 151.4 %while.26 = (s32[]{:T(128)}, f32[2,1024,8,64]{1,0,3,2:T(2,128)}, f32[2,8,1024]{2,1,0:T(8,128)S(1)}, bf16[2,1024,64]{1,2,0:T(8,128)(2,1)S(1)}, s32[2,1024]{1,0:T(...) while((s32[]{:T(128)}, f32[2,1024,8,64]{1,0,3,2:T(2,128)}, ...), condition=%wide.region_9.10_spmd, body=%wide.region_4.9_spmd.sunk | while | flops 2253914112 | bytes 121492128 | solution.py:191
  266.5 9.8 %fusion.225 = (f32[8,512]{1,0:T(8,128)S(1)}, f32[8,512]{1,0:T(8,128)S(1)}) fusion(f32[1024,512,8]{1,0,2:T(8,128)} %get-tuple-element.409, f32[8,512]{1,0:T(8,128)S(1)} %get-tuple-element.410, pred[512,1024]{0,1:T(8,128)(4,1)S(1)} %get-tuple-element.408, f32[8,512]{1,0:T(8,128)S(1)} %get-tuple-element.411, f32[1024,512,8]{1,0,2:T(8,128)S(1)} %get-tuple-element.407, ...), kind=kLoop, calls=%fused_computation.6.clone.1 | loop fusion | flops 33546240 | bytes 34668544 | tf_op jit(solution)/shard_map/while/body/eval_jaxpr/reduce_sum | solution.py:93
  291.8 36.4 %dynamic_update_slice.28 = f32[2,1024,8,64]{1,0,3,2:T(2,128)} dynamic-update-slice(f32[2,1024,8,64]{1,0,3,2:T(2,128)} %get-tuple-element.449, f32[1,1024,8,64]{1,0,3,2:T(1,128)S(1)} %copy.130, s32[]{:T(128)S(6)} %copy.139, s32[]{:T(128)} %constant.80.clone.1..sunk, s32[]{:T(128)} %constant.80.clone.1..sunk, s32[]{:T(128)} %constant.80.clone.1..sunk) | dynamic-update-slice | bytes 4194308 | tf_op jit(solution)/shard_map/while/body/jit(dynamic_update_index_in_dim)/dynamic_update_slice | solution.py:191
  341.9 9.8 %fusion.225 = (f32[8,512]{1,0:T(8,128)S(1)}, f32[8,512]{1,0:T(8,128)S(1)}) fusion(f32[1024,512,8]{1,0,2:T(8,128)} %get-tuple-element.409, f32[8,512]{1,0:T(8,128)S(1)} %get-tuple-element.410, pred[512,1024]{0,1:T(8,128)(4,1)S(1)} %get-tuple-element.408, f32[8,512]{1,0:T(8,128)S(1)} %get-tuple-element.411, f32[1024,512,8]{1,0,2:T(8,128)S(1)} %get-tuple-element.407, ...), kind=kLoop, calls=%fused_computation.6.clone.1 | loop fusion | flops 33546240 | bytes 34668544 | tf_op jit(solution)/shard_map/while/body/eval_jaxpr/reduce_sum | solution.py:93
  367.2 36.4 %dynamic_update_slice.28 = f32[2,1024,8,64]{1,0,3,2:T(2,128)} dynamic-update-slice(f32[2,1024,8,64]{1,0,3,2:T(2,128)} %get-tuple-element.449, f32[1,1024,8,64]{1,0,3,2:T(1,128)S(1)} %copy.130, s32[]{:T(128)S(6)} %copy.139, s32[]{:T(128)} %constant.80.clone.1..sunk, s32[]{:T(128)} %constant.80.clone.1..sunk, s32[]{:T(128)} %constant.80.clone.1..sunk) | dynamic-update-slice | bytes 4194308 | tf_op jit(solution)/shard_map/while/body/jit(dynamic_update_index_in_dim)/dynamic_update_slice | solution.py:191
  420.8 12.3 %multiply_convert_fusion = (bf16[2048,2048]{1,0:T(8,128)(2,1)}, f32[2048,2048]{1,0:T(8,128)}) fusion(f32[2048]{0:T(1024)S(1)} %copy-done.69, bf16[512,2048]{1,0:T(8,128)(2,1)S(1)} %copy-done.27, f32[2048,512]{1,0:T(8,128)S(1)} %get-tuple-element.262, f32[512]{0:T(512)S(1)} %copy-done.72, f32[512]{0:T(512)S(1)} %copy-done.67, f32[2048]{0:T(1024)S(1)} %add_rsqrt_fusion, ...), kind=kOutput, calls=%fused_computation.133 | convolution fusion | flops 4342153216 | bytes 31485952 | tf_op jit(solution)/shard_map/dot_general | solution.py:203
  433.1 19.9 %convert_reduce_fusion = (f32[2048]{0:T(1024)}, bf16[2048,2048]{1,0:T(8,128)(2,1)}) fusion(f32[2048,2048]{1,0:T(8,128)} %get-tuple-element.264, f32[2048]{0:T(1024)S(1)} %copy-done.69, bf16[2048,512]{1,0:T(8,128)(2,1)S(1)} %copy-done.23, bf16[2048,512]{1,0:T(8,128)(2,1)S(1)} %copy-done.21), kind=kOutput, calls=%fused_computation.132 | convolution fusion | flops 4391434240 | bytes 29376512 | tf_op jit(solution)/shard_map/td,fd->tf/dot_general | solution.py:231
  453.0 10.1 %multiply_reduce_fusion = (f32[512]{0:T(512)}, f32[2048]{0:T(1024)S(1)}, f32[2048]{0:T(1024)S(1)}, f32[512]{0:T(512)}, f32[2048,512]{1,0:T(8,128)S(1)}) fusion(f32[2048,512]{1,0:T(8,128)S(1)} %get-tuple-element.262, f32[2048]{0:T(1024)S(1)} %add_rsqrt_fusion, f32[2048]{0:T(1024)S(1)} %broadcast_multiply_fusion.4, f32[512]{0:T(512)S(1)} %copy-done.67, ...), kind=kOutput, calls=%fused_computation.162 | convolution fusion | flops 4304399360 | bytes 18913280 | tf_op jit(solution)/shard_map/tf,df->td/dot_general | solution.py:236
  479.1 148.8 %while.27 = (s32[]{:T(128)}, bf16[2,1024,8,64]{1,3,2,0:T(8,128)(2,1)}, bf16[2,1024,64]{1,2,0:T(8,128)(2,1)}, bf16[2,1024,64]{1,2,0:T(8,128)(2,1)}, bf16[2,1024,6...) while((s32[]{:T(128)}, ...), condition=%wide.region_17.18_spmd, body=%wide.region_14.17_spmd.sunk | while | flops 5452783616 | bytes 309880768 | solution.py:254
  483.5 10.2 %fusion.242 = (f32[8,512]{1,0:T(8,128)S(1)}, f32[8,512,1024]{1,2,0:T(8,128)}) fusion(f32[1024,512,8]{1,0,2:T(8,128)S(1)} %fusion.239, f32[8,512]{1,0:T(8,128)S(1)} %get-tuple-element.425, bf16[2,1024,8,64]{1,3,2,0:T(8,128)(2,1)} %get-tuple-element.505, s32[]{:T(128)S(6)} %copy.149, s32[]{:T(128)S(6)} %add.233, ...), kind=kOutput, calls=%fused_computation.50.clone.1 | convolution fusion | flops 557838336 | bytes 34768384 | tf_op jit(solution)/shard_map/while/body/eval_jaxpr/qeh,kh->eqk/dot_general | solution.py:115
  508.8 10.2 %fusion.246 = (f32[8,512]{1,0:T(8,128)S(1)}, f32[8,512,1024]{1,2,0:T(8,128)}) fusion(f32[1024,512,8]{1,0,2:T(8,128)S(1)} %fusion.245, f32[8,512]{1,0:T(8,128)S(1)} %get-tuple-element.433, bf16[2,1024,8,64]{1,3,2,0:T(8,128)(2,1)} %get-tuple-element.505, s32[]{:T(128)S(6)} %copy.149, bf16[2,1024,64]{1,2,0:T(8,128)(2,1)S(1)} %get-tuple-element.502, ...), kind=kOutput, calls=%fused_computation.58.clone.1 | convolution fusion | flops 557838336 | bytes 34767872 | tf_op jit(solution)/shard_map/while/body/eval_jaxpr/qeh,kh->eqk/dot_general | solution.py:115
  519.0 10.2 %fusion.247 = bf16[8,512,1024]{1,2,0:T(8,128)(2,1)} fusion(f32[8,512,1024]{1,2,0:T(8,128)} %get-tuple-element.435, f32[1024,512,8]{1,0,2:T(8,128)S(1)} %fusion.245, f32[8,512]{1,0:T(8,128)S(1)} %get-tuple-element.436), kind=kLoop, calls=%fused_computation.60.clone.1 | loop fusion | flops 12582912 | bytes 41959424 | tf_op jit(solution)/shard_map/while/body/eval_jaxpr/convert_element_type | solution.py:134
  529.2 8.6 fusion.251
  537.8 8.6 fusion.252
  557.6 10.2 %fusion.242 = (f32[8,512]{1,0:T(8,128)S(1)}, f32[8,512,1024]{1,2,0:T(8,128)}) fusion(f32[1024,512,8]{1,0,2:T(8,128)S(1)} %fusion.239, f32[8,512]{1,0:T(8,128)S(1)} %get-tuple-element.425, bf16[2,1024,8,64]{1,3,2,0:T(8,128)(2,1)} %get-tuple-element.505, s32[]{:T(128)S(6)} %copy.149, s32[]{:T(128)S(6)} %add.233, ...), kind=kOutput, calls=%fused_computation.50.clone.1 | convolution fusion | flops 557838336 | bytes 34768384 | tf_op jit(solution)/shard_map/while/body/eval_jaxpr/qeh,kh->eqk/dot_general | solution.py:115
  583.0 10.2 %fusion.246 = (f32[8,512]{1,0:T(8,128)S(1)}, f32[8,512,1024]{1,2,0:T(8,128)}) fusion(f32[1024,512,8]{1,0,2:T(8,128)S(1)} %fusion.245, f32[8,512]{1,0:T(8,128)S(1)} %get-tuple-element.433, bf16[2,1024,8,64]{1,3,2,0:T(8,128)(2,1)} %get-tuple-element.505, s32[]{:T(128)S(6)} %copy.149, bf16[2,1024,64]{1,2,0:T(8,128)(2,1)S(1)} %get-tuple-element.502, ...), kind=kOutput, calls=%fused_computation.58.clone.1 | convolution fusion | flops 557838336 | bytes 34767872 | tf_op jit(solution)/shard_map/while/body/eval_jaxpr/qeh,kh->eqk/dot_general | solution.py:115
  593.2 10.2 %fusion.247 = bf16[8,512,1024]{1,2,0:T(8,128)(2,1)} fusion(f32[8,512,1024]{1,2,0:T(8,128)} %get-tuple-element.435, f32[1024,512,8]{1,0,2:T(8,128)S(1)} %fusion.245, f32[8,512]{1,0:T(8,128)S(1)} %get-tuple-element.436), kind=kLoop, calls=%fused_computation.60.clone.1 | loop fusion | flops 12582912 | bytes 41959424 | tf_op jit(solution)/shard_map/while/body/eval_jaxpr/convert_element_type | solution.py:134
  603.3 8.6 fusion.251
  611.9 8.6 fusion.252
  692.4 9.4 %multiply_convert_fusion.3 = bf16[2048,512]{1,0:T(8,128)(2,1)} fusion(f32[2048,512]{1,0:T(8,128)S(1)} %copy-done.4, bf16[2048,2048]{1,0:T(8,128)(2,1)} %get-tuple-element.263, bf16[2048,512]{1,0:T(8,128)(2,1)S(1)} %copy-done.22, f32[512]{0:T(512)S(1)} %copy-done.71, f32[2048]{0:T(1024)S(1)} %bitcast.468), kind=kOutput, calls=%fused_computation.168 | convolution fusion | flops 4299161600 | bytes 16787456 | tf_op jit(solution)/shard_map/dot_general | solution.py:207
  701.9 197.8 %all-reduce.3.cloned.1.call-done = f32[2699264]{0:T(1024)} async-done(((f32[2699264]{0:T(1024)}), f32[2699264]{0:T(1024)}) %all-reduce.3.cloned.1.call-update) | async-done | bytes 10797072
  (354 shorter events, 258.9 us)
Async XLA Ops:
  7.2 7.2 copy-start.66
  7.2 95.0 %all-gather.3.cloned.1.call-start = ((), (), s32[]{:S(2)}) async-start(), calls=%async_computation | async-start | bytes 11134464 | tf_op jit(solution)/shard_map/all_gather | solution.py:156
  9.3 890.4 %all-reduce.3.cloned.1.call-start = ((), (), s32[]{:S(2)}) async-start(), calls=%async_computation.1 | async-start | bytes 21594112
  13.3 225.8 %copy-start.57 = (f32[2048]{0:T(1024)}, f32[2048]{0:T(1024)S(1)}, u32[]{:S(2)}) copy-start(f32[2048]{0:T(1024)S(1)} %get-tuple-element.269) | copy-start | bytes 24580
  13.3 225.8 %copy-start.59 = (f32[2048]{0:T(1024)}, f32[2048]{0:T(1024)S(1)}, u32[]{:S(2)}) copy-start(f32[2048]{0:T(1024)S(1)} %get-tuple-element.270) | copy-start | bytes 24580
  214.7 24.4 %copy-start.64 = (f32[512]{0:T(512)}, f32[512]{0:T(512)S(1)}, u32[]{:S(2)}) copy-start(f32[512]{0:T(512)S(1)} %get-tuple-element.241) | copy-start | bytes 6148
  224.5 15.5 %copy-start.30 = (bf16[512,8]{1,0:T(8,128)(2,1)}, bf16[512,8]{1,0:T(8,128)(2,1)S(1)}, u32[]{:S(2)}) copy-start(bf16[512,8]{1,0:T(8,128)(2,1)S(1)} %slice.211) | copy-start | bytes 24580
  226.6 15.4 %copy-start.18 = (bf16[512,512]{1,0:T(8,128)(2,1)}, bf16[512,512]{1,0:T(8,128)(2,1)S(1)}, u32[]{:S(2)}) copy-start(bf16[512,512]{1,0:T(8,128)(2,1)S(1)} %slice.215) | copy-start | bytes 1572868
  417.7 52.4 %copy-start.3 = (f32[2048,512]{1,0:T(8,128)}, f32[2048,512]{1,0:T(8,128)S(1)}, u32[]{:S(2)}) copy-start(f32[2048,512]{1,0:T(8,128)S(1)} %get-tuple-element.262) | copy-start | bytes 12582916
  420.8 12.4 %copy-start.21 = (bf16[2048,512]{1,0:T(8,128)(2,1)S(1)}, bf16[2048,512]{1,0:T(8,128)(2,1)}, u32[]{:S(2)}) copy-start(bf16[2048,512]{1,0:T(8,128)(2,1)} %slice.224) | copy-start | bytes 6291460
  420.8 12.4 %copy-start.23 = (bf16[2048,512]{1,0:T(8,128)(2,1)S(1)}, bf16[2048,512]{1,0:T(8,128)(2,1)}, u32[]{:S(2)}) copy-start(bf16[2048,512]{1,0:T(8,128)(2,1)} %fusion.118) | copy-start | bytes 6291460
  453.0 10.1 %copy-start.75 = (bf16[2048,2048]{1,0:T(8,128)(2,1)S(1)}, bf16[2048,2048]{1,0:T(8,128)(2,1)}, u32[]{:S(2)}) copy-start(bf16[2048,2048]{1,0:T(8,128)(2,1)} %get-tuple-element.268) | copy-start | bytes 25165828
  463.1 7.0 copy-start.62
  529.2 8.6 copy-start.41
  529.2 17.2 %slice-start = ((s8[8388608]{0:T(1024)(128)(4,1)}), s8[4194304]{0:T(1024)(128)(4,1)S(1)}, s32[]{:S(2)}) async-start(s8[8388608]{0:T(1024)(128)(4,1)} %bitcast.431), calls=%async_computation.2 | async-start | bytes 8388608 | tf_op jit(solution)/shard_map/while
  537.8 8.6 slice-start.1
  537.8 8.6 copy-start.44
  603.3 8.6 copy-start.41
  603.3 17.2 %slice-start = ((s8[8388608]{0:T(1024)(128)(4,1)}), s8[4194304]{0:T(1024)(128)(4,1)S(1)}, s32[]{:S(2)}) async-start(s8[8388608]{0:T(1024)(128)(4,1)} %bitcast.431), calls=%async_computation.2 | async-start | bytes 8388608 | tf_op jit(solution)/shard_map/while
  611.9 8.6 slice-start.1
  611.9 8.6 copy-start.44
  653.5 7.1 copy-start.35
  673.7 8.2 copy-start.73
  673.7 9.5 %copy-start.68 = (f32[512]{0:T(512)S(1)}, f32[512]{0:T(512)}, u32[]{:S(2)}) copy-start(f32[512]{0:T(512)} %convert_reduce_fusion.2) | copy-start | bytes 6148
  (67 other events, 264.2 us)
Sparse Core Ops, SparseCore 0:
  11.5 90.6 all-gather.2
  686.0 213.6 all-reduce.2
where the time goes:
time: 925 us; the launch traced here: 909 us
  waiting for transfers between devices  283 us (31%)
  matrix products  247 us (27%)
  other arithmetic  183 us (20%)
  local copies, waits for them, and re-layouts  178 us (19%)
  between operations  15.3 us (2%)
    unnamed x3, waiting for transfers between devices  198 us
    all_gather x1, other arithmetic, local(): gathered = lax.all_gather(low_params, ('dp', 'fsdp'), axis=0, tiled=True)  99.3 us
    all_gather x1, waiting for transfers between devices, local(): gathered = lax.all_gather(low_params, ('dp', 'fsdp'), axis=0, tiled=True)  85.4 us
    dynamic_update_slice x4, local copies, waits for them, and re-layouts, local(): lax.map(attend_row, (query_rows, key_by_row, value_by_row, segments, vali...  77 us
    unnamed x167, local copies, waits for them, and re-layouts  50.9 us
    dot_general x4, matrix products, attend_back(): jnp.einsum('qeh,kh->eqk', query_block, key_rows, preferred_element_type=j...  40.7 us
    convert_element_type x4, other arithmetic, attend_back(): grad_scores = grad_scores.astype(jnp.bfloat16)  35.5 us
    dot_general x4, matrix products, attend_back(): jnp.einsum('eqk,qeh->kh', weights_soft.astype(jnp.bfloat16), grad_block,...  34.3 us
  transfers between devices with their start and end apart: 2, of which 2 were waited for; matrix products, arithmetic and copies ran while one was open for 2% of the time, Pallas kernels for 0%

commit v1 on v0

v1 whole, which is shorter than its diff:
```python
from functools import partial

import jax
import jax.numpy as jnp
from jax import lax
from jax.experimental import pallas as pl
from jax.experimental.pallas import tpu as pltpu
from jax.sharding import PartitionSpec as P

D = 512
FF = 2048
EXPERTS = 8
HEAD = 64
EPS = 1e-05
NEG = -1e30
F32 = jnp.float32
BF16 = jnp.bfloat16
AXES = ("dp", "fsdp")

ROW_K = 512
ROW_V = 576
ROW_O = 640
ROW_U = 1152
ROW_D = 3200
ROW_S = 5248
SMALL = 32
ROWS_ALL = ROW_S + SMALL
T_R = 512
T_K = 528
T_V = 592
T_ALL = 656

QB = 128
KB = 256

NN = ((1,), (0,))
NT = ((1,), (1,))
TN = ((0,), (0,))

VMEM_MIB = 56


def dot(left, right, dims):
    return lax.dot_general(left, right, (dims, ((), ())), preferred_element_type=F32)


def cost(micros):
    return pl.CostEstimate(flops=int(micros * 1.1e9), bytes_accessed=int(micros * 1e5), transcendentals=0)


def after(value, *others):
    return lax.optimization_barrier((value, *others))[0]


def params(mib=VMEM_MIB):
    return pltpu.CompilerParams(vmem_limit_bytes=mib << 20)


def iota(shape, dim):
    return lax.broadcasted_iota(jnp.int32, shape, dim)


class Plan:
    def __init__(self, devices, shard):
        self.devices = devices
        self.lanes = shard // 128
        reach = max((self.lanes * d) % 64 for d in range(devices)) + self.lanes
        self.rows = -(-reach // 64) * 16

    def first(self, d):
        return (self.lanes * d) // 64

    def last(self, d):
        return (self.lanes * (d + 1) - 1) // 64


def window_kernel(plan, at_ref, shard_ref, out_ref, pad_ref):
    pad_ref[...] = jnp.zeros_like(pad_ref)
    pad_ref[64 : 64 + plan.lanes, :] = shard_ref[...]
    start = 64 - at_ref[0]
    for j in range(4):
        out_ref[:, 128 * j : 128 * (j + 1)] = pad_ref[
            pl.ds(start + j, plan.rows, stride=4), :
        ].astype(BF16)


def make_window(plan, at, shard):
    return pl.pallas_call(
        partial(window_kernel, plan),
        grid_spec=pltpu.PrefetchScalarGridSpec(
            num_scalar_prefetch=1,
            grid=(1,),
            in_specs=[pl.BlockSpec((plan.lanes, 128), lambda i, at: (0, 0))],
            out_specs=pl.BlockSpec((plan.rows, D), lambda i, at: (0, 0)),
            scratch_shapes=[pltpu.VMEM((plan.rows * 4 + 128, 128), F32)],
        ),
        out_shape=jax.ShapeDtypeStruct((plan.rows, D), BF16),
        compiler_params=params(),
    )(at, shard.reshape(plan.lanes, 128))


def row_pieces(plan, low, high):
    direct, shared = [], []
    for d in range(plan.devices):
        first, last = plan.first(d), plan.last(d)
        start = first
        if d > 0 and plan.last(d - 1) == first:
            start = first + 1
            if low <= first * 16 < high:
                shared.append((d, 0, first * 16 - low))
        begin, end = max(start * 16, low), min((last + 1) * 16, high)
        if begin < end:
            direct.append((d, begin - first * 16, begin - low, end - begin))
    return direct, shared


def start_rows(plan, source, low, high, dst_ref, tmp_ref, sem):
    direct, shared = row_pieces(plan, low, high)
    for d, at, to, amount in direct:
        pltpu.make_async_copy(
            source(d).at[pl.ds(at, amount), :], dst_ref.at[pl.ds(to, amount), :], sem.at[0]
        ).start()
    for slot, (d, at, _) in enumerate(shared):
        pltpu.make_async_copy(
            source(d).at[pl.ds(at, 16), :], tmp_ref.at[pl.ds(16 * slot, 16), :], sem.at[1]
        ).start()


def end_rows(plan, low, high, dst_ref, tmp_ref, sem):
    _, shared = row_pieces(plan, low, high)
    pltpu.make_async_copy(dst_ref, dst_ref, sem.at[0]).wait()
    if shared:
        part = tmp_ref.at[pl.ds(0, 16 * len(shared)), :]
        pltpu.make_async_copy(part, part, sem.at[1]).wait()
        for slot, (_, _, to) in enumerate(shared):
            dst_ref[to : to + 16, :] = (
                dst_ref[to : to + 16, :].astype(F32)
                + tmp_ref[16 * slot : 16 * slot + 16, :].astype(F32)
            ).astype(BF16)


def shared_rows(plan, low, high):
    return max(16, 16 * len(row_pieces(plan, low, high)[1]))


class Gathered:
    def __init__(self, plan, lanes, head, rest, whole):
        self.plan, self.lanes = plan, lanes
        self.head, self.rest, self.whole = head, rest, whole
        self.small_at = ROW_S - 16 * plan.first(plan.devices - 1)

    def arrays(self, need_head, need_rest):
        if self.whole is not None:
            return [self.whole]
        return (self.head if need_head else []) + (self.rest if need_rest else [])

    def fetch(self, place_ref, refs, need_head, start):
        if self.whole is not None:
            last = self.plan.devices - 1
            start(lambda d: refs[0].at[d], refs[0].at[last, pl.ds(self.small_at, SMALL), :])
            return
        head = refs[: self.lanes] if need_head else None
        rest = refs[self.lanes :] if need_head else refs
        for place in range(self.lanes):

            def source(d, place=place):
                plane, lane = divmod(d, self.lanes)
                if plane == 0:
                    return head[lane ^ place]
                return rest[lane ^ place].at[plane - 1]

            small = None
            if need_head:
                small = head[(self.lanes - 1) ^ place].at[pl.ds(self.plan.rows, SMALL), :]
            pl.when(place_ref[0] == place)(partial(start, source, small))


def spread(j):
    return (iota((64, D), 1) == 8 * iota((64, D), 0) + j).astype(BF16)


def narrow_transposed(flat):
    out = jnp.zeros((64, D), F32)
    for j in range(8):
        out = out + dot(flat[:, 64 * j : 64 * (j + 1)], spread(j), TN)
    return out


def narrow_flat(turned):
    return jnp.concatenate([dot(spread(j), turned, NT) for j in range(8)], axis=1)


def router_transposed(flat):
    lane = iota((8, D), 1) % 8
    at = iota((8, D), 0)
    pick = (iota((D, 64), 0) // 8 == iota((D, 64), 1)).astype(BF16)
    pieces = []
    for r in range(8):
        row = jnp.broadcast_to(flat[r : r + 1, :], (8, D))
        pieces.append(dot(jnp.where(lane == at, row, 0.0).astype(BF16), pick, NN))
    return jnp.concatenate(pieces, axis=1)


def router_flat(turned):
    lane = iota((8, D), 1) % 8
    at = iota((8, D), 0)
    pick = (iota((64, D), 1) // 8 == iota((64, D), 0)).astype(BF16)
    rows = []
    for r in range(8):
        full = dot(turned[:, 64 * r : 64 * (r + 1)].astype(BF16), pick, NN)
        rows.append(jnp.sum(jnp.where(lane == at, full, 0.0), axis=0, keepdims=True))
    return jnp.concatenate(rows, axis=0)


def norm(source):
    center = source - jnp.mean(source, axis=-1, keepdims=True)
    scaler = lax.rsqrt(jnp.mean(center * center, axis=-1, keepdims=True) + EPS)
    return center * scaler, scaler


def norm_back(grad_normal, normal, scaler):
    return scaler * (
        grad_normal
        - jnp.mean(grad_normal, axis=-1, keepdims=True)
        - normal * jnp.mean(grad_normal * normal, axis=-1, keepdims=True)
    )


def two_heads(ref, pair, q0):
    return jnp.concatenate(
        [
            ref[0, 128 * pair : 128 * pair + 64, pl.ds(q0, QB)],
            ref[0, 128 * pair + 64 : 128 * pair + 128, pl.ds(q0, QB)],
        ],
        axis=1,
    )


def block_bias(code_ref, column_ref, q0, w0):
    row = code_ref[0, :, pl.ds(q0, QB)]
    bias = jnp.where(column_ref[pl.ds(w0, KB), :] == row, 0.0, NEG)
    return jnp.concatenate([bias, bias], axis=1)


def set_columns(code_ref, column_ref):
    length = code_ref.shape[2]
    column_ref[...] = jnp.broadcast_to(code_ref[0], (QB, length)).T


def block_places(block, length):
    q0 = pl.multiple_of(block * QB, QB)
    w0 = pl.multiple_of(jnp.clip(q0 - 64, 0, length - KB), 64)
    return q0, w0


def forward_prepare(plan, gathered, place_ref, refs, turned_ref, small_ref, scratch):
    rows_ref, low_ref, tmp_ref, sem = scratch

    def start(source, small):
        start_rows(plan, source, 0, ROW_O, rows_ref, tmp_ref, sem)
        pltpu.make_async_copy(small, low_ref, sem.at[2]).start()

    gathered.fetch(place_ref, refs, True, start)
    pltpu.make_async_copy(low_ref, low_ref, sem.at[2]).wait()
    end_rows(plan, 0, ROW_O, rows_ref, tmp_ref, sem)
    small_ref[...] = low_ref[...].astype(F32)
    turned_ref[0:D, :] = rows_ref[0:D, :].astype(F32).T.astype(BF16)
    turned_ref[T_R:T_K, :] = jnp.concatenate(
        [router_transposed(small_ref[0:8, :]), jnp.zeros((8, D), F32)], axis=0
    ).astype(BF16)
    turned_ref[T_K:T_V, :] = narrow_transposed(rows_ref[ROW_K:ROW_V, :]).astype(BF16)
    turned_ref[T_V:T_ALL, :] = narrow_transposed(rows_ref[ROW_V:ROW_O, :]).astype(BF16)


def forward_row(x_ref, code_ref, turned_ref, small_ref, outs, column_ref):
    q_ref, k_ref, v_ref, h_ref, prob_ref, lse_ref, att_ref = outs
    length = x_ref.shape[1]
    set_columns(code_ref, column_ref)
    normal, _ = norm(x_ref[0].astype(F32))
    h = (normal * small_ref[12:13, :] + small_ref[13:14, :]).astype(BF16)
    h_ref[0] = h
    turned = dot(turned_ref[0:T_K, :], h, NT)
    q_ref[0] = turned[0:D].astype(BF16)
    logits = turned[T_R : T_R + 8]
    shifted = jnp.exp(logits - jnp.max(logits, axis=0, keepdims=True))
    prob_ref[0] = shifted / jnp.sum(shifted, axis=0, keepdims=True)
    kv = dot(h, turned_ref[T_K:T_ALL, :], NT).astype(BF16)
    k_ref[0] = kv[:, 0:HEAD]
    v_ref[0] = kv[:, HEAD:]

    def block_step(block, carry):
        q0, w0 = block_places(block, length)
        bias = block_bias(code_ref, column_ref, q0, w0)
        keys = k_ref[0, pl.ds(w0, KB), :]
        values = v_ref[0, pl.ds(w0, KB), :]
        for pair in range(EXPERTS // 2):
            scores = dot(keys, two_heads(q_ref, pair, q0), NN) * (HEAD**-0.5) + bias
            peak = jnp.max(scores, axis=0, keepdims=True)
            expd = jnp.exp(scores - peak)
            summed = jnp.sum(expd, axis=0, keepdims=True)
            att = dot(values, expd.astype(BF16), TN) * (1.0 / summed)
            total = peak + jnp.log(summed)
            for half in range(2):
                head = 2 * pair + half
                att_ref[0, 64 * head : 64 * (head + 1), pl.ds(q0, QB)] = att[
                    :, QB * half : QB * (half + 1)
                ]
                lse_ref[0, head : head + 1, pl.ds(q0, QB)] = total[:, QB * half : QB * (half + 1)]
        return carry

    lax.fori_loop(0, length // QB, block_step, 0)


def forward_first(plan, gathered, count, place_ref, x_ref, code_ref, *refs):
    wins, refs = refs[:count], refs[count:]
    outs, (turned_ref, small_ref), scratch = refs[:7], refs[7:9], refs[9:]
    forward_prepare(plan, gathered, place_ref, wins, turned_ref, small_ref, scratch[1:])
    forward_row(x_ref, code_ref, turned_ref, small_ref, outs, scratch[0])


def forward_next(place_ref, x_ref, code_ref, turned_ref, small_ref, *refs):
    forward_row(x_ref, code_ref, turned_ref, small_ref, refs[7:14], refs[14])


def attention_forward(plan, gathered, place, x, code, row, before):
    rows, length = x.shape[0], x.shape[1]
    row3 = lambda a, b: pl.BlockSpec((1, a, b), lambda *_: (row, 0, 0))
    sizes = [
        (D, length, BF16),
        (length, HEAD, BF16),
        (length, HEAD, BF16),
        (length, D, BF16),
        (8, length, F32),
        (8, length, F32),
        (D, length, F32),
    ]
    out_specs = [row3(a, b) for a, b, _ in sizes]
    out_shape = [kind(c, rows, a, b) for a, b, c in sizes]
    scratch = [pltpu.VMEM((length, QB), F32)]
    in_specs = [row3(length, D), row3(1, length)]
    if before is None:
        wins = gathered.arrays(True, False)
        kernel = partial(forward_first, plan, gathered, len(wins))
        operands = [place, x, code, *wins]
        in_specs = in_specs + [ANYWHERE] * len(wins)
        out_specs = out_specs + [whole(T_ALL, D), whole(SMALL, D)]
        out_shape = out_shape + [kind(BF16, T_ALL, D), kind(F32, SMALL, D)]
        scratch = scratch + [
            pltpu.VMEM((ROW_O, D), BF16),
            pltpu.VMEM((SMALL, D), BF16),
            pltpu.VMEM((shared_rows(plan, 0, ROW_O), D), BF16),
            pltpu.SemaphoreType.DMA((3,)),
        ]
        aliases = {}
    else:
        kernel = forward_next
        operands = [place, x, code, *before[7:9], *before[:7]]
        in_specs = in_specs + [whole(T_ALL, D), whole(SMALL, D)] + [ANYWHERE] * 7
        aliases = {5 + i: i for i in range(7)}
    return pl.pallas_call(
        kernel,
        grid_spec=pltpu.PrefetchScalarGridSpec(
            num_scalar_prefetch=1,
            grid=(1,),
            in_specs=in_specs,
            out_specs=out_specs,
            scratch_shapes=scratch,
        ),
        out_shape=out_shape,
        input_output_aliases=aliases,
        cost_estimate=cost(14),
        compiler_params=params(),
    )(*operands)


TB = 512


def chosen_experts(experts_ref, length):
    ids = iota((EXPERTS, length), 0)
    chosen = (experts_ref[0, 0:1, :] == ids) | (experts_ref[0, 1:2, :] == ids)
    return chosen.astype(F32)


def valid_tokens(counts_ref, amount):
    place = pl.program_id(1) * amount + iota((amount, 1), 0)
    return (place < counts_ref[pl.program_id(0)]).astype(F32)


def by_head(values, gate):
    return jnp.concatenate(
        [values[64 * e : 64 * (e + 1)] * gate[e : e + 1] for e in range(EXPERTS)], axis=0
    )


def gelu_parts(source):
    scale = (2.0 / jnp.pi) ** 0.5
    square = source * source
    bent = jnp.tanh(source * (scale + (scale * 0.044715) * square))
    half = 0.5 * source
    value = half + half * bent
    slope = (0.5 + 0.5 * bent) + (half - half * bent * bent) * (
        scale + (3.0 * scale * 0.044715) * square
    )
    return value, slope


def first_step():
    return (pl.program_id(0) == 0) & (pl.program_id(1) == 0)


def last_step():
    return (pl.program_id(0) == pl.num_programs(0) - 1) & (
        pl.program_id(1) == pl.num_programs(1) - 1
    )


def up_kernel(plan, gathered, count, place_ref, counts_ref, *refs):
    x_ref, cot_ref, att_ref, prob_ref, experts_ref, small_ref = refs[:6]
    wins = refs[6 : 6 + count]
    hid_ref, slope_ref, mid_ref, up_ref, out_ref, gdown_ref = refs[6 + count : 12 + count]
    rows_ref, tmp_ref, wide_ref, total_ref, sem = refs[12 + count :]

    @pl.when(first_step())
    def _():
        def start(source, small):
            start_rows(plan, source, ROW_O, ROW_D, rows_ref, tmp_ref, sem)

        gathered.fetch(place_ref, wins, True, start)
        end_rows(plan, ROW_O, ROW_D, rows_ref, tmp_ref, sem)
        for c in range(4):
            lanes = slice(128 * c, 128 * (c + 1))
            wide_ref[c] = rows_ref[D:, lanes].astype(F32)
            for j in range(4):
                up_ref[:, D * j + 128 * c : D * j + 128 * (c + 1)] = wide_ref[
                    c, pl.ds(j, D, stride=4), :
                ].astype(BF16)
        out_ref[...] = rows_ref[0:D, :]
        total_ref[...] = jnp.zeros_like(total_ref)

    amount = x_ref.shape[1]
    gate = prob_ref[0] * chosen_experts(experts_ref, amount)
    mixed = by_head(att_ref[0], gate).astype(BF16)
    middle = x_ref[0].astype(F32) + dot(mixed, rows_ref[0:D, :], TN)
    mid_ref[0] = middle
    normal, _ = norm(middle)
    h = (normal * small_ref[14:15, :] + small_ref[15:16, :]).astype(BF16)
    grad_low = (valid_tokens(counts_ref, amount) * cot_ref[0].astype(F32)).astype(BF16)
    for j in range(4):
        part = slice(D * j, D * (j + 1))
        value, slope = gelu_parts(dot(h, up_ref[:, part], NN) + small_ref[8 + j : 9 + j, :])
        value = value.astype(BF16)
        hid_ref[0, :, part] = value
        slope_ref[0, :, part] = slope.astype(BF16)
        total_ref[part, :] += dot(value, grad_low, TN)

    @pl.when(last_step())
    def _():
        gdown_ref[...] = total_ref[...].astype(BF16)


def row_block(*tail):
    return pl.BlockSpec((1, TB, *tail), lambda i, j, *_: (i, j, 0))


def column_block(height):
    return pl.BlockSpec((1, height, TB), lambda i, j, *_: (i, 0, j))


def whole(*shape):
    return pl.BlockSpec(shape, lambda *_: (0,) * len(shape))


ANYWHERE = pl.BlockSpec(memory_space=pl.ANY)


def kind(dtype, *shape):
    return jax.ShapeDtypeStruct(shape, dtype)


def feed_up(plan, gathered, place, counts, x, cot, att, prob, experts, small):
    rows, length = x.shape[0], x.shape[1]
    wins = gathered.arrays(True, True)
    return pl.pallas_call(
        partial(up_kernel, plan, gathered, len(wins)),
        grid_spec=pltpu.PrefetchScalarGridSpec(
            num_scalar_prefetch=2,
            grid=(rows, length // TB),
            in_specs=[
                row_block(D),
                row_block(D),
                column_block(D),
                column_block(8),
                column_block(2),
                whole(SMALL, D),
            ]
            + [ANYWHERE] * len(wins),
            out_specs=[
                row_block(FF),
                row_block(FF),
                row_block(D),
                whole(D, FF),
                whole(D, D),
                whole(FF, D),
            ],
            scratch_shapes=[
                pltpu.VMEM((ROW_D - ROW_O, D), BF16),
                pltpu.VMEM((shared_rows(plan, ROW_O, ROW_D), D), BF16),
                pltpu.VMEM((4, FF, 128), F32),
                pltpu.VMEM((FF, D), F32),
                pltpu.SemaphoreType.DMA((2,)),
            ],
        ),
        out_shape=[
            kind(BF16, rows, length, FF),
            kind(BF16, rows, length, FF),
            kind(F32, rows, length, D),
            kind(BF16, D, FF),
            kind(BF16, D, D),
            kind(BF16, FF, D),
        ],
        cost_estimate=cost(30),
        compiler_params=params(),
    )(place, counts, x, cot, att, prob, experts, small, *wins)


def hidden_kernel(plan, gathered, count, pieces, place_ref, counts_ref, *refs):
    cot_ref, slope_ref, mid_ref, small_ref, gdown_ref = refs[:5]
    wins = refs[5 : 5 + count]
    pre_ref, down_ref, gbias_ref, gup_ref = refs[5 + count : 9 + count]
    packed = refs[9 + count : -6]
    flat_ref, tmp_ref, wide_ref, total_ref, sem, pack_sem = refs[-6:]

    @pl.when(first_step())
    def _():
        def start(source, small):
            start_rows(plan, source, ROW_D, ROW_S, down_ref, tmp_ref, sem)

        gathered.fetch(place_ref, wins, False, start)
        if pieces:
            pack_start(pieces, [1], place_ref, [flat_ref, gdown_ref], packed, pack_sem)
        end_rows(plan, ROW_D, ROW_S, down_ref, tmp_ref, sem)
        total_ref[...] = jnp.zeros_like(total_ref)
        gbias_ref[...] = jnp.zeros_like(gbias_ref)

    amount = cot_ref.shape[1]
    grad = valid_tokens(counts_ref, amount) * cot_ref[0].astype(F32)
    grad_low = grad.astype(BF16)
    normal, _ = norm(mid_ref[0])
    h = (normal * small_ref[14:15, :] + small_ref[15:16, :]).astype(BF16)
    for j in range(4):
        part = slice(D * j, D * (j + 1))
        pre = slope_ref[0, :, part].astype(F32) * dot(grad_low, down_ref[part, :], NT)
        gbias_ref[j : j + 1, :] += jnp.sum(pre, axis=0, keepdims=True)
        pre = pre.astype(BF16)
        pre_ref[0, :, part] = pre
        total_ref[:, part] += dot(h, pre, TN)
    gbias_ref[4:5, :] += jnp.sum(grad, axis=0, keepdims=True)

    @pl.when(last_step())
    def _():
        for c in range(4):
            for j in range(4):
                wide_ref[c, pl.ds(j, D, stride=4), :] = total_ref[
                    :, D * j + 128 * c : D * j + 128 * (c + 1)
                ]
            flat_ref[:, 128 * c : 128 * (c + 1)] = wide_ref[c].astype(BF16)
        gup_ref[...] = flat_ref[0 : gup_ref.shape[0], :]
        if pieces:
            pack_start(pieces, [0], place_ref, [flat_ref, gdown_ref], packed, pack_sem)
            pack_end(packed, pack_sem)


def feed_hidden(plan, gathered, place, counts, cot, slope, mid, small, gdown, pieces):
    rows, length = cot.shape[0], cot.shape[1]
    wins = gathered.arrays(False, True)
    head = LATE_ROWS if pieces else FF
    packed = [kind(BF16, LANES // 2, PLANES - 1, plan.rows, D)] * 2 if pieces else []
    return pl.pallas_call(
        partial(hidden_kernel, plan, gathered, len(wins), pieces),
        grid_spec=pltpu.PrefetchScalarGridSpec(
            num_scalar_prefetch=2,
            grid=(rows, length // TB),
            in_specs=[row_block(D), row_block(FF), row_block(D), whole(SMALL, D), whole(FF, D)]
            + [ANYWHERE] * len(wins),
            out_specs=[row_block(FF), whole(FF, D), whole(8, D), whole(head, D)]
            + [ANYWHERE] * len(packed),
            scratch_shapes=[
                pltpu.VMEM((FF, D), BF16),
                pltpu.VMEM((shared_rows(plan, ROW_D, ROW_S), D), BF16),
                pltpu.VMEM((4, FF, 128), F32),
                pltpu.VMEM((D, FF), F32),
                pltpu.SemaphoreType.DMA((2,)),
                pltpu.SemaphoreType.DMA((2,)),
            ],
        ),
        out_shape=[
            kind(BF16, rows, length, FF),
            kind(BF16, FF, D),
            kind(F32, 8, D),
            kind(BF16, head, D),
        ]
        + packed,
        cost_estimate=cost(20),
        compiler_params=params(),
    )(place, counts, cot, slope, mid, small, gdown, *wins)


def branch_kernel(
    counts_ref,
    cot_ref,
    pre_ref,
    mid_ref,
    att_ref,
    prob_ref,
    experts_ref,
    small_ref,
    up_ref,
    out_ref,
    dmid_ref,
    datt_ref,
    dlog_ref,
    gout_ref,
    gnorm_ref,
    total_ref,
):
    @pl.when(first_step())
    def _():
        total_ref[...] = jnp.zeros_like(total_ref)
        gnorm_ref[...] = jnp.zeros_like(gnorm_ref)

    amount = cot_ref.shape[1]
    grad = valid_tokens(counts_ref, amount) * cot_ref[0].astype(F32)
    normal, scaler = norm(mid_ref[0])
    back = dot(pre_ref[0], up_ref[...], NT)
    gnorm_ref[0:1, :] += jnp.sum(back * normal, axis=0, keepdims=True)
    gnorm_ref[1:2, :] += jnp.sum(back, axis=0, keepdims=True)
    dmid = grad + norm_back(back * small_ref[14:15, :], normal, scaler)
    dmid_ref[0] = dmid
    branch = dmid.astype(BF16)
    prob = prob_ref[0]
    chosen = chosen_experts(experts_ref, amount)
    gate = prob * chosen
    att = att_ref[0]
    total_ref[...] += dot(by_head(att, gate).astype(BF16), branch, NN)
    dmixed = dot(out_ref[...], branch, NT)
    dgate = jnp.concatenate(
        [
            jnp.sum(
                dmixed[64 * e : 64 * (e + 1)] * att[64 * e : 64 * (e + 1)], axis=0, keepdims=True
            )
            for e in range(EXPERTS)
        ],
        axis=0,
    )
    datt_ref[0] = by_head(dmixed, gate).astype(BF16)
    dprob = dgate * chosen
    dlog = prob * (dprob - jnp.sum(prob * dprob, axis=0, keepdims=True))
    dlog_ref[0] = jnp.concatenate([dlog, jnp.zeros_like(dlog)], axis=0).astype(BF16)

    @pl.when(last_step())
    def _():
        gout_ref[...] = total_ref[...].astype(BF16)


def feed_branch(counts, cot, pre, mid, att, prob, experts, small, up, out):
    rows, length = cot.shape[0], cot.shape[1]
    return pl.pallas_call(
        branch_kernel,
        grid_spec=pltpu.PrefetchScalarGridSpec(
            num_scalar_prefetch=1,
            grid=(rows, length // TB),
            in_specs=[
                row_block(D),
                row_block(FF),
                row_block(D),
                column_block(D),
                column_block(8),
                column_block(2),
                whole(SMALL, D),
                whole(D, FF),
                whole(D, D),
            ],
            out_specs=[
                row_block(D),
                column_block(D),
                column_block(16),
                whole(D, D),
                whole(8, D),
            ],
            scratch_shapes=[pltpu.VMEM((D, D), F32)],
        ),
        out_shape=[
            kind(F32, rows, length, D),
            kind(BF16, rows, D, length),
            kind(BF16, rows, 16, length),
            kind(BF16, D, D),
            kind(F32, 8, D),
        ],
        cost_estimate=cost(16),
        compiler_params=params(),
    )(counts, cot, pre, mid, att, prob, experts, small, up, out)


def backward_kernel(pieces, place_ref, *refs):
    x_ref, h_ref, q_ref, k_ref, v_ref, lse_ref, datt_ref, dlog_ref, code_ref = refs[:9]
    turned_ref, gbias_ref, gnorm_ref, gout_ref, gup_ref = refs[9:14]
    back_ref, ghead_ref, glow_ref = refs[14:17]
    packed = refs[17:-7]
    dk_ref, dv_ref, column_ref, total_ref, gain_ref, shift_ref, pack_sem = refs[-7:]
    length = x_ref.shape[1]

    @pl.when(pl.program_id(0) == 0)
    def _():
        total_ref[...] = jnp.zeros_like(total_ref)
        gain_ref[...] = jnp.zeros_like(gain_ref)
        shift_ref[...] = jnp.zeros_like(shift_ref)

    set_columns(code_ref, column_ref)
    dk_ref[...] = jnp.zeros_like(dk_ref)
    dv_ref[...] = jnp.zeros_like(dv_ref)

    def block_step(block, carry):
        q0, w0 = block_places(block, length)
        bias = block_bias(code_ref, column_ref, q0, w0)
        keys = k_ref[0, pl.ds(w0, KB), :]
        values = v_ref[0, pl.ds(w0, KB), :]
        dk = jnp.zeros((KB, HEAD), F32)
        dv = jnp.zeros((KB, HEAD), F32)
        for pair in range(EXPERTS // 2):
            queries = two_heads(q_ref, pair, q0)
            datt = two_heads(datt_ref, pair, q0)
            total = jnp.concatenate(
                [lse_ref[0, 2 * pair + half : 2 * pair + half + 1, pl.ds(q0, QB)] for half in (0, 1)],
                axis=1,
            )
            scores = dot(keys, queries, NN) * (HEAD**-0.5) + bias
            soft = jnp.exp(scores - total)
            dsoft = dot(values, datt, NN)
            dv = dv + dot(soft.astype(BF16), datt, NT)
            inner = jnp.sum(soft * dsoft, axis=0, keepdims=True)
            dscores = (soft * (dsoft - inner)).astype(BF16)
            dk = dk + dot(dscores, queries, NT)
            dq = (dot(keys, dscores, TN) * (HEAD**-0.5)).astype(BF16)
            for half in range(2):
                head = 2 * pair + half
                back_ref[0, 64 * head : 64 * (head + 1), pl.ds(q0, QB)] = dq[
                    :, QB * half : QB * (half + 1)
                ]
        dk_ref[pl.ds(w0, KB), :] += dk * (HEAD**-0.5)
        dv_ref[pl.ds(w0, KB), :] += dv
        return carry

    lax.fori_loop(0, length // QB, block_step, 0)
    back_ref[0, T_R:T_K, :] = dlog_ref[0]
    back_ref[0, T_K:T_V, :] = dk_ref[...].T.astype(BF16)
    back_ref[0, T_V:T_ALL, :] = dv_ref[...].T.astype(BF16)
    normal, _ = norm(x_ref[0].astype(F32))
    back = back_ref[0]
    total_ref[...] += dot(back, h_ref[0], NN)
    gain_ref[...] += dot(back, normal.astype(BF16), NN)
    shift_ref[...] += jnp.sum(back.astype(F32), axis=1, keepdims=True)

    @pl.when(pl.program_id(0) == pl.num_programs(0) - 1)
    def _():
        ghead_ref[0:D, :] = total_ref[0:D, :].T.astype(BF16)
        low = total_ref[T_K:T_ALL, :].astype(BF16)
        ghead_ref[D : D + 64, :] = narrow_flat(low[0:64]).astype(BF16)
        ghead_ref[D + 64 : D + 128, :] = narrow_flat(low[64:128]).astype(BF16)
        turned = turned_ref[...].astype(F32)
        glow_ref[...] = jnp.concatenate(
            [
                router_flat(total_ref[T_R : T_R + 8, :]),
                gbias_ref[0:4, :],
                jnp.sum(turned * gain_ref[...], axis=0, keepdims=True),
                jnp.sum(turned * shift_ref[...], axis=0, keepdims=True),
                gnorm_ref[0:2, :],
                gbias_ref[4:5, :],
                jnp.zeros((SMALL - 17, D), F32),
            ],
            axis=0,
        ).astype(BF16)
        if pieces:
            ins = [ghead_ref, gout_ref, gup_ref, glow_ref]
            pack_start(pieces, range(4), place_ref, ins, packed, pack_sem)
            pack_end(packed, pack_sem)


def attention_backward(
    plan, place, x, h, q, k, v, lse, datt, dlog, code, turned, gbias, gnorm, gout, gup, pieces
):
    rows, length = x.shape[0], x.shape[1]
    row3 = lambda a, b: pl.BlockSpec((1, a, b), lambda i, *_: (i, 0, 0))
    packed = [kind(BF16, LANES // 2, 1, plan.rows + SMALL, D)] * 2 if pieces else []
    head = min(LATE_ROWS, gup.shape[0])
    return pl.pallas_call(
        partial(backward_kernel, pieces),
        grid_spec=pltpu.PrefetchScalarGridSpec(
            num_scalar_prefetch=1,
            grid=(rows,),
            in_specs=[
                row3(length, D),
                row3(length, D),
                row3(D, length),
                row3(length, HEAD),
                row3(length, HEAD),
                row3(8, length),
                row3(D, length),
                row3(16, length),
                row3(1, length),
                whole(T_ALL, D),
                whole(8, D),
                whole(8, D),
                whole(D, D),
                whole(head, D),
            ],
            out_specs=[row3(T_ALL, length), whole(ROW_O, D), whole(SMALL, D)]
            + [ANYWHERE] * len(packed),
            scratch_shapes=[
                pltpu.VMEM((length, HEAD), F32),
                pltpu.VMEM((length, HEAD), F32),
                pltpu.VMEM((length, QB), F32),
                pltpu.VMEM((T_ALL, D), F32),
                pltpu.VMEM((T_ALL, D), F32),
                pltpu.VMEM((T_ALL, 1), F32),
                pltpu.SemaphoreType.DMA((2,)),
            ],
        ),
        out_shape=[
            kind(BF16, rows, T_ALL, length),
            kind(BF16, ROW_O, D),
            kind(BF16, SMALL, D),
        ]
        + packed,
        cost_estimate=cost(33),
        compiler_params=params(),
    )(place, x, h, q, k, v, lse, datt, dlog, code, turned, gbias, gnorm, gout, gup)


def input_kernel(x_ref, dmid_ref, back_ref, turned_ref, small_ref, gx_ref):
    normal, scaler = norm(x_ref[0].astype(F32))
    back = dot(back_ref[0], turned_ref[...], TN) * small_ref[12:13, :]
    gx_ref[0] = (dmid_ref[0] + norm_back(back, normal, scaler)).astype(BF16)


def input_grad(x, dmid, back, turned, small):
    rows, length = x.shape[0], x.shape[1]
    return pl.pallas_call(
        input_kernel,
        grid=(rows, length // TB),
        in_specs=[
            row_block(D),
            row_block(D),
            column_block(T_ALL),
            whole(T_ALL, D),
            whole(SMALL, D),
        ],
        out_specs=row_block(D),
        out_shape=kind(BF16, rows, length, D),
        cost_estimate=cost(8),
        compiler_params=params(),
    )(x, dmid, back, turned, small)


def output_kernel(counts_ref, mid_ref, hid_ref, small_ref, down_ref, out_ref):
    result = dot(hid_ref[0], down_ref[...], NN) + small_ref[16:17, :]
    valid = valid_tokens(counts_ref, mid_ref.shape[1])
    out_ref[0] = (valid * (mid_ref[0] + result)).astype(BF16)


def layer_output(counts, mid, hid, small, down):
    rows, length = mid.shape[0], mid.shape[1]
    return pl.pallas_call(
        output_kernel,
        grid_spec=pltpu.PrefetchScalarGridSpec(
            num_scalar_prefetch=1,
            grid=(rows, length // TB),
            in_specs=[row_block(D), row_block(FF), whole(SMALL, D), whole(FF, D)],
            out_specs=row_block(D),
        ),
        out_shape=kind(BF16, rows, length, D),
        cost_estimate=cost(9),
        compiler_params=params(),
    )(counts, mid, hid, small, down)


PLANES = 4
LANES = 8
ALL = PLANES * LANES
LATE_ROWS = 192


def move(value, pairs):
    return lax.ppermute(value, AXES, pairs)


def across(value, bits):
    return move(value, [(d, d ^ bits) for d in range(ALL)])


def by_plane(values, plane):
    out = values[-1]
    for z in range(len(values) - 1):
        out = jnp.where(plane == z, values[z], out)
    return out


def plane_spread(own):
    return [own] + [across(own, bits) for bits in (2, 4, 6)]


def core_spread(got):
    swapped = [across(part, 1) for part in got]
    return [part for both in zip(got, swapped) for part in both]


def plane_gather(plan, window, my_plane):
    got = [window]
    for s in range(1, PLANES):
        got.append(
            move(window, [(z * LANES + f, (z ^ s) * LANES + f) for z in range(PLANES) for f in range(LANES)])
        )
    of = lambda z: by_plane([got[z ^ mine] for mine in range(PLANES)], my_plane)
    low = ROW_S - 16 * plan.first(ALL - 1)
    planes = [of(z) for z in range(PLANES)]
    head = jnp.concatenate([planes[0], planes[-1][low : low + SMALL]], axis=0)
    return head, jnp.stack(planes[1:])


def pack_start(pieces, sources, place_ref, ins, packed, sem):
    keep_ref, send_ref = packed
    for place in range(LANES):

        def start(place=place):
            for source, at, amount, plane, lane, to in pieces:
                if source not in sources:
                    continue
                out = send_ref if (lane ^ place) & 1 else keep_ref
                pltpu.make_async_copy(
                    ins[source].at[pl.ds(at, amount), :],
                    out.at[(lane ^ place) >> 1, plane, pl.ds(to, amount), :],
                    sem.at[(lane ^ place) & 1],
                ).start()

        pl.when(place_ref[0] == place)(start)


def pack_end(packed, sem):
    for i in range(2):
        pltpu.make_async_copy(packed[i], packed[i], sem.at[i]).wait()


def window_pieces(plan, windows, spans, extra):
    pieces = []
    for d in windows:
        plane, lane = divmod(d, LANES)
        plane = plane - windows[0] // LANES
        begin = 16 * plan.first(d)
        for source, (low, high) in enumerate(spans):
            a, b = max(begin, low), min(begin + plan.rows, high)
            if a < b:
                pieces.append((source, a - low, b - a, plane, lane, a - begin))
        end = spans[-1][1]
        if begin + plan.rows > end:
            left = begin + plan.rows - end
            pieces.append((len(spans) - 1, 0, left, plane, lane, plan.rows - left))
        if extra:
            pieces.append((len(spans), 0, SMALL, plane, lane, plan.rows))
    return pieces


def core_sum(keep, send):
    got = across(send, 1)
    return [(keep[p].astype(F32) + got[p].astype(F32)).astype(BF16) for p in range(LANES // 2)]


def plane_sum(parts):
    total = parts[0].astype(F32)
    for p in range(1, LANES // 2):
        total = total + across(parts[p], 2 * p).astype(F32)
    return total.astype(BF16)


def main_parts(total, my_plane):
    owned = [total[0]] + [total[z] for z in range(PLANES - 1)]
    pick = lambda s: by_plane([owned[mine ^ s] for mine in range(PLANES)], my_plane)
    out = [pick(0)]
    for s in range(1, PLANES):
        pairs = [
            (z * LANES + f, (z ^ s) * LANES + f)
            for z in range(PLANES)
            if z ^ s
            for f in range(LANES)
        ]
        out.append(move(pick(s), pairs))
    return out


def head_parts(total):
    out = [total]
    last = PLANES - 1
    for s in range(1, PLANES):
        pairs = [(s * LANES + f, f) for f in range(LANES)]
        pairs.append(((s - 1) * LANES + LANES - 1, last * LANES + LANES - 1))
        out.append(move(total, pairs))
    return out


def owned_kernel(plan, at_ref, me_ref, *refs):
    main, head = refs[:PLANES], refs[PLANES : 2 * PLANES]
    out_ref, sum_ref, pad_ref = refs[2 * PLANES :]

    def add(parts, low, high):
        total = parts[0][low:high].astype(F32)
        for part in parts[1:]:
            total = total + part[low:high].astype(F32)
        return total

    @pl.when(me_ref[0] < LANES)
    def _():
        sum_ref[...] = add(head, 0, plan.rows)

    @pl.when(me_ref[0] >= LANES)
    def _():
        sum_ref[...] = add(main, 0, plan.rows)

    @pl.when(me_ref[0] == ALL - 1)
    def _():
        low = ROW_S - 16 * plan.first(ALL - 1)
        sum_ref[low : low + SMALL, :] = add(head, plan.rows, plan.rows + SMALL)

    for j in range(4):
        pad_ref[pl.ds(j, plan.rows, stride=4), :] = sum_ref[:, 128 * j : 128 * (j + 1)]
    out_ref[...] = pad_ref[pl.ds(at_ref[0], plan.lanes), :]


def take_owned(plan, at, me, main, head):
    out = pl.pallas_call(
        partial(owned_kernel, plan),
        grid_spec=pltpu.PrefetchScalarGridSpec(
            num_scalar_prefetch=2,
            grid=(1,),
            in_specs=[whole(plan.rows, D)] * PLANES + [whole(plan.rows + SMALL, D)] * PLANES,
            out_specs=whole(plan.lanes, 128),
            scratch_shapes=[
                pltpu.VMEM((plan.rows, D), F32),
                pltpu.VMEM((plan.rows * 4, 128), F32),
            ],
        ),
        out_shape=kind(F32, plan.lanes, 128),
        compiler_params=params(),
    )(at, me, *main, *head)
    return out.reshape(-1)


def plain_sum(plan, planes, lanes, me, at, ghead, gout, gup, gdown, glow):
    grads = jnp.concatenate([ghead, gout, gup, gdown, glow], axis=0)
    grads = jnp.pad(grads, ((0, plan.rows), (0, 0)))
    parts = jnp.stack([grads[16 * plan.first(d) :][: plan.rows] for d in range(plan.devices)])
    parts = parts.reshape(planes, lanes, plan.rows, D)
    parts = lax.psum_scatter(parts, "fsdp", scatter_dimension=1, tiled=True)
    parts = lax.psum_scatter(parts, "dp", scatter_dimension=0, tiled=True)
    flat = parts.reshape(-1).astype(F32)
    return lax.dynamic_slice(flat, (at[0] * 128,), (plan.lanes * 128,))


def local(planes, lanes, x, shard, segments, experts, counts, cot):
    plan = Plan(planes * lanes, shard.shape[0])
    my_plane, my_lane = lax.axis_index("dp"), lax.axis_index("fsdp")
    me = my_plane * lanes + my_lane
    place = my_lane.astype(jnp.int32).reshape(1)
    at = ((plan.lanes * me) % 64).astype(jnp.int32).reshape(1)
    window = make_window(plan, at, shard)
    staged = (planes, lanes, plan.lanes) == (PLANES, LANES, 659)
    main_pieces, head_pieces = [], []
    ready = [place, place]
    if staged:
        head, rest = plane_gather(plan, window, my_plane)
        ready[0] = after(place, rest)
        head = core_spread(plane_spread(head))
        rest = plane_spread(rest)
        ready[1] = after(place, *rest)
        gathered = Gathered(plan, lanes, head, core_spread(rest), None)
        main_pieces = window_pieces(
            plan, range(LANES, ALL), [(ROW_U, ROW_D), (ROW_D, ROW_S)], False
        )
        head_pieces = window_pieces(
            plan, range(LANES), [(0, ROW_O), (ROW_O, ROW_U), (ROW_U, ROW_U + LATE_ROWS)], True
        )
    else:
        gathered = Gathered(plan, lanes, None, None, lax.all_gather(window, AXES, axis=0))
    rows, length = x.shape[0], x.shape[1]
    places = jnp.arange(length, dtype=jnp.int32)[None, :]
    code = jnp.where(places < counts[:, None], segments, -1 - places)
    code = code.astype(F32).reshape(-1, 1, length)
    pairs = jnp.swapaxes(experts, 1, 2)
    state = attention_forward(plan, gathered, ready[0], x, code, 0, None)
    turned, small = state[7:9]
    for row in range(1, rows):
        before = [*state[:7], turned, small]
        state = attention_forward(plan, gathered, ready[1], x, code, row, before)
    q, k, v, h, prob, lse, att = state[:7]
    hid, slope, mid, up, out, gdown = feed_up(
        plan, gathered, place, counts, x, cot, att, prob, pairs, small
    )
    pre, down, gbias, gup, *packed = feed_hidden(
        plan, gathered, place, counts, cot, slope, mid, small, gdown, main_pieces
    )
    dmid, datt, dlog, gout, gnorm = feed_branch(
        counts, cot, pre, mid, att, prob, pairs, small, up, out
    )
    third = place
    if staged:
        parts = core_sum(*packed)
        third = after(place, *parts)
        main = plane_sum(parts)
    back, ghead, glow, *packed = attention_backward(
        plan, third, x, h, q, k, v, lse, datt, dlog, code, turned, gbias, gnorm, gout, gup, head_pieces
    )
    if not staged:
        grads = plain_sum(plan, planes, lanes, me, at, ghead, gout, gup, gdown, glow)
        output = layer_output(counts, mid, hid, small, down)
        return output, input_grad(x, dmid, back, turned, small), grads
    main = main_parts(main, my_plane)
    parts = core_sum(packed[0][:, 0], packed[1][:, 0])
    grad_tokens = input_grad(x, dmid, after(back, *parts), turned, small)
    total = plane_sum(parts)
    output = layer_output(counts, after(mid, total), hid, small, down)
    me = me.astype(jnp.int32).reshape(1)
    return output, grad_tokens, take_owned(plan, at, me, main, head_parts(total))


def solution(mesh):
    spec = P(AXES)
    return jax.shard_map(
        partial(local, mesh.shape["dp"], mesh.shape["fsdp"]),
        mesh=mesh,
        in_specs=(spec,) * 6,
        out_specs=(spec,) * 3,
        check_vma=False,
    )
```

time: 925 us -> 258 us (0.28); the launches traced: 909 us -> 256 us
  matrix products: 247 us -> 0 us
  waiting for transfers between devices: 283 us -> 48.5 us
  other arithmetic: 183 us -> 7.75 us
  local copies, waits for them, and re-layouts: 178 us -> 3.74 us
  Pallas kernels: 0 us -> 157 us
  starting transfers between devices: 0.08 us -> 38.2 us
  between operations: 15.3 us -> 1.11 us
    dot_general x49 -> x0, matrix products: 247 us -> none  [the longest x4 40.7 us: attend_back(): jnp.einsum('qeh,kh->eqk', query_block, key_rows, preferred_element_type=j...]
    unnamed x3 -> x0, waiting for transfers between devices: 198 us -> none
    pallas_call x0 -> x10, Pallas kernels: none -> 157 us  [the longest x1 34.3 us: attention_backward(): pl.pallas_call(partial(backward_kernel, pieces), grid_spec=pltpu.Prefetch...]
    all_gather x1 -> x0, other arithmetic: 99.3 us -> none  [local(): gathered = lax.all_gather(low_params, ('dp', 'fsdp'), axis=0, tiled=True)]
    all_gather x1 -> x0, waiting for transfers between devices: 85.4 us -> none  [local(): gathered = lax.all_gather(low_params, ('dp', 'fsdp'), axis=0, tiled=True)]
    dynamic_update_slice x4 -> x0, local copies, waits for them, and re-layouts: 77 us -> none  [local(): lax.map(attend_row, (query_rows, key_by_row, value_by_row, segments, vali...]
    ppermute x0 -> x31, waiting for transfers between devices: none -> 48.5 us  [move(): return lax.ppermute(value, AXES, pairs)]
    unnamed x167 -> x50, local copies, waits for them, and re-layouts: 50.9 us -> 3.14 us
  transfers between devices with their start and end apart: 2 -> 31, of which waited for: 2 -> 11; matrix products, arithmetic and copies ran while one was open for 2% -> 1% of each run, Pallas kernels for 0% -> 25%
where the time goes in v1:
time: 258 us; the launch traced here: 256 us
  Pallas kernels  157 us (61%)
  waiting for transfers between devices  48.5 us (19%)
  starting transfers between devices  38.2 us (15%)
  other arithmetic  7.75 us (3%)
  local copies, waits for them, and re-layouts  3.74 us (1%)
    ppermute x31, waiting for transfers between devices, move(): return lax.ppermute(value, AXES, pairs)  48.5 us
    ppermute x31, starting transfers between devices, move(): return lax.ppermute(value, AXES, pairs)  38.2 us
    pallas_call x1, Pallas kernels, attention_backward(): pl.pallas_call(partial(backward_kernel, pieces), grid_spec=pltpu.Prefetch...  34.3 us
    pallas_call x1, Pallas kernels, feed_up(): pl.pallas_call(partial(up_kernel, plan, gathered, len(wins)), grid_spec=p...  31 us
    pallas_call x2, Pallas kernels, attention_forward(): pl.pallas_call(kernel, grid_spec=pltpu.PrefetchScalarGridSpec(num_scalar_...  29.9 us
    pallas_call x1, Pallas kernels, feed_hidden(): pl.pallas_call(partial(hidden_kernel, plan, gathered, len(wins), pieces),...  23 us
    pallas_call x1, Pallas kernels, feed_branch(): pl.pallas_call(branch_kernel, grid_spec=pltpu.PrefetchScalarGridSpec(num_...  16.8 us
    pallas_call x1, Pallas kernels, layer_output(): pl.pallas_call(output_kernel, grid_spec=pltpu.PrefetchScalarGridSpec(num_...  10.2 us
  transfers between devices with their start and end apart: 31, of which 11 were waited for; matrix products, arithmetic and copies ran while one was open for 1% of the time, Pallas kernels for 25%

profile of v1, /device:TPU:0, one launch (start us, length us, event | category | flops | bytes accessed | tf_op | source)
XLA Modules:
  0.0 256.3 jit_solution(12883903024026036615)
XLA Ops:
  0.7 1.7 shard_map.85
  2.4 4.0 %collective-permute-start.2 = (bf16[192,512]{1,0:T(8,128)(2,1)}, bf16[192,512]{1,0:T(8,128)(2,1)S(1)}, u32[]{:S(2)}, u32[]{:S(2)}) collective-permute-start(bf16[192,512]{1,0:T(8,128)(2,1)} %shard_map.85), channel_id=1, source_target_pairs={{0,16},{1,17},{2,18},{3,19},{4,20},{5,21},{6,22},{7,23},{8,24},{9,... | collective-permute-start | bytes 589832 | tf_op jit(solution)/shard_map/ppermute | solution.py:894
  8.0 9.5 %collective-permute-done.2 = bf16[192,512]{1,0:T(8,128)(2,1)S(1)} collective-permute-done((bf16[192,512]{1,0:T(8,128)(2,1)}, bf16[192,512]{1,0:T(8,128)(2,1)S(1)}, u32[]{:S(2)}, u32[]{:S(2)}) %collective-permute-start.2) | collective-permute-done | bytes 196640 | tf_op jit(solution)/shard_map/ppermute | solution.py:894
  17.5 3.7 %collective-permute-done = bf16[192,512]{1,0:T(8,128)(2,1)S(1)} collective-permute-done((bf16[192,512]{1,0:T(8,128)(2,1)}, bf16[192,512]{1,0:T(8,128)(2,1)S(1)}, u32[]{:S(2)}, u32[]{:S(2)}) %collective-permute-start) | collective-permute-done | bytes 196640 | tf_op jit(solution)/shard_map/ppermute | solution.py:894
  22.3 2.5 collective-permute-start.11
  25.8 6.0 %collective-permute-done.11.refs_6_.refs_12_ = bf16[224,512]{1,0:T(8,128)(2,1)S(1)} collective-permute-done((bf16[224,512]{1,0:T(8,128)(2,1)S(1)}, bf16[224,512]{1,0:T(8,128)(2,1)S(1)}, u32[]{:S(2)}, u32[]{:S(2)}) %collective-permute-start.11) | collective-permute-done | bytes 229408 | tf_op jit(solution)/shard_map/ppermute | solution.py:894
  31.8 2.8 %collective-permute-done.9.refs_4_.refs_10_ = bf16[224,512]{1,0:T(8,128)(2,1)S(1)} collective-permute-done((bf16[224,512]{1,0:T(8,128)(2,1)S(1)}, bf16[224,512]{1,0:T(8,128)(2,1)S(1)}, u32[]{:S(2)}, u32[]{:S(2)}) %collective-permute-start.9) | collective-permute-done | bytes 229408 | tf_op jit(solution)/shard_map/ppermute | solution.py:894
  36.0 1.8 collective-permute-start.5
  40.4 15.9 %shard_map.86 = (bf16[2,512,1024]{2,1,0:T(8,128)(2,1)}, bf16[2,1024,64]{2,1,0:T(8,128)(2,1)}, bf16[2,1024,64]{2,1,0:T(8,128)(2,1)}, bf16[2,1024,512]{2,1,0:T(8,1...) custom-call(s32[1]{0:T(128)} %bitcast.place_ref, ...), custom_call_target="tpu_custom_call" | custom-call | flops 15399999488 | bytes 1400000 | tf_op jit(solution)/shard_map/pallas_call | solution.py:360
  56.4 8.9 %collective-permute-done.4.refs_18_.refs_9_ = bf16[3,192,512]{2,1,0:T(8,128)(2,1)S(1)} collective-permute-done((bf16[3,192,512]{2,1,0:T(8,128)(2,1)S(1)}, bf16[3,192,512]{2,1,0:T(8,128)(2,1)S(1)}, u32[]{:S(2)}, u32[]{:S(2)}) %collective-permute-start.4) | collective-permute-done | bytes 589856 | tf_op jit(solution)/shard_map/ppermute | solution.py:894
  65.9 14.0 %shard_map.87 = (bf16[2,512,1024]{2,1,0:T(8,128)(2,1)}, bf16[2,1024,64]{2,1,0:T(8,128)(2,1)}, bf16[2,1024,64]{2,1,0:T(8,128)(2,1)}, bf16[2,1024,512]{2,1,0:T(8,1...) custom-call(s32[1]{0:T(128)} %bitcast.place_ref, ...), custom_call_target="tpu_custom_call", output_to_operand_aliasing={{0}: (5, {}), {1}: (6, {}), {2}: (7, {}), {3}: (8, {}), {4}... | custom-call | flops 15399999488 | bytes 1400000 | tf_op jit(solution)/shard_map/pallas_call | solution.py:360
  81.4 31.0 %shard_map.88 = (bf16[2,1024,2048]{2,1,0:T(8,128)(2,1)}, bf16[2,1024,2048]{2,1,0:T(8,128)(2,1)}, f32[2,1024,512]{2,1,0:T(8,128)}, bf16[512,2048]{1,0:T(8,128)(2,...) custom-call(s32[1]{0:T(128)} %bitcast.place_ref, s32[2]{0:T(128)} %counts_ref.7, bf16[2,1024,512]{2,1,0:T(8,128)(2,1)} %x_ref.5, ...), custom_call_target="tpu_custom_call" | custom-call | flops 32999999488 | bytes 3000000 | tf_op jit(solution)/shard_map/pallas_call | solution.py:484
  112.4 23.0 %shard_map.89 = (bf16[2,1024,2048]{2,1,0:T(8,128)(2,1)}, bf16[2048,512]{1,0:T(8,128)(2,1)}, f32[8,512]{1,0:T(8,128)}, bf16[192,512]{1,0:T(8,128)(2,1)}, bf16[4,3...) custom-call(s32[1]{0:T(128)} %bitcast.place_ref, s32[2]{0:T(128)} %counts_ref.7, ...), custom_call_target="tpu_custom_call" | custom-call | flops 22000001024 | bytes 2000000 | tf_op jit(solution)/shard_map/pallas_call | solution.py:579
  136.0 4.4 %collective-permute-done.17 = bf16[4,3,192,512]{3,2,1,0:T(8,128)(2,1)S(1)} collective-permute-done((bf16[4,3,192,512]{3,2,1,0:T(8,128)(2,1)}, bf16[4,3,192,512]{3,2,1,0:T(8,128)(2,1)S(1)}, u32[]{:S(2)}, u32[]{:S(2)}) %collective-permute-start.17) | collective-permute-done | bytes 2359328 | tf_op jit(solution)/shard_map/ppermute | solution.py:894
  140.3 1.9 fusion.1
  145.8 16.8 %shard_map.90 = (f32[2,1024,512]{2,1,0:T(8,128)}, bf16[2,512,1024]{2,1,0:T(8,128)(2,1)}, bf16[2,16,1024]{2,1,0:T(8,128)(2,1)}, bf16[512,512]{1,0:T(8,128)(2,1)}, f32[8,512]{1,0:T(8,128)}) custom-call(s32[2]{0:T(128)} %counts_ref.7, bf16[2,1024,512]{2,1,0:T(8,128)(2,1)} %cot_ref.1, bf16[2,1024,2048]{2,1,0:T(8,128)(2,1)} %get-tuple-element.68.pre_ref, ...), custom_call_target="tpu_custom_call" | custom-call | flops 17600000000 | bytes 1600000 | tf_op jit(solution)/shard_map/pallas_call | solution.py:668
  162.6 9.0 %collective-permute-done.24 = bf16[3,192,512]{2,1,0:T(8,128)(2,1)S(1)} collective-permute-done((bf16[3,192,512]{2,1,0:T(8,128)(2,1)S(1)}, bf16[3,192,512]{2,1,0:T(8,128)(2,1)S(1)}, u32[]{:S(2)}, u32[]{:S(2)}) %collective-permute-start.24) | collective-permute-done | bytes 589856 | tf_op jit(solution)/shard_map/ppermute | solution.py:894
  174.4 34.3 %shard_map.91 = (bf16[2,656,1024]{2,1,0:T(8,128)(2,1)}, bf16[640,512]{1,0:T(8,128)(2,1)}, bf16[32,512]{1,0:T(8,128)(2,1)}, bf16[4,1,224,512]{3,2,1,0:T(8,128)(2,1)}, bf16[4,1,224,512]{3,2,1,0:T(8,128)(2,1)}) custom-call(s32[1]{0:T(128)} %bitcast.place_ref, bf16[2,1024,512]{2,1,0:T(8,128)(2,1)} %x_ref.5, bf16[2,1024,512]{2,1,0:T(8,128)(2,1)} %get-tuple-element.63.refs_1_, ...), custom_call_target="tpu_custom_call" | custom-call | flops 36300001280 | bytes 3300000 | tf_op jit(solution)/shard_map/pallas_call | solution.py:796
  208.8 2.7 %collective-permute-done.18 = bf16[4,224,512]{2,1,0:T(8,128)(2,1)S(1)} collective-permute-done((bf16[4,224,512]{2,1,0:T(8,128)(2,1)}, bf16[4,224,512]{2,1,0:T(8,128)(2,1)S(1)}, u32[]{:S(2)}, u32[]{:S(2)}) %collective-permute-start.18) | collective-permute-done | bytes 917536 | tf_op jit(solution)/shard_map/ppermute | solution.py:894
  217.1 4.3 %collective-permute-start.27 = (bf16[192,512]{1,0:T(8,128)(2,1)S(1)}, bf16[192,512]{1,0:T(8,128)(2,1)S(1)}, u32[]{:S(2)}, u32[]{:S(2)}) collective-permute-start(bf16[192,512]{1,0:T(8,128)(2,1)S(1)} %get-tuple-element.99), channel_id=1, source_target_pairs={{0,24},{1,25},{2,26},{3,27},{4,28},{5,29},{6,30},{7,31},{8,16},{9,... | collective-permute-start | bytes 589832 | tf_op jit(solution)/shard_map/ppermute | solution.py:894
  221.5 6.8 %collective-permute-start.25 = (bf16[192,512]{1,0:T(8,128)(2,1)S(1)}, bf16[192,512]{1,0:T(8,128)(2,1)S(1)}, u32[]{:S(2)}, u32[]{:S(2)}) collective-permute-start(bf16[192,512]{1,0:T(8,128)(2,1)S(1)} %get-tuple-element.101), channel_id=1, source_target_pairs={{0,8},{1,9},{2,10},{3,11},{4,12},{5,13},{6,14},{7,15},{16,24},{17,... | collective-permute-start | bytes 589832 | tf_op jit(solution)/shard_map/ppermute | solution.py:894
  233.7 10.2 %shard_map.92 = bf16[2,1024,512]{2,1,0:T(8,128)(2,1)} custom-call(s32[2]{0:T(128)} %counts_ref.7, f32[2,1024,512]{2,1,0:T(8,128)} %get-tuple-element.79.refs_2_.mid_ref, bf16[2,1024,2048]{2,1,0:T(8,128)(2,1)} %get-tuple-element.80.hid_ref, f32[32,512]{1,0:T(8,128)} %get-tuple-element.47.small_ref.refs_5_.refs_3_, bf16[2048,512]{1,0:T(8,128)(2,1)} %get-tuple-element.81.down_ref), custom_call_target="tpu_custom_call" | custom-call | flops 9900000256 | bytes 900000 | tf_op jit(solution)/shard_map/pallas_call | solution.py:873
  245.2 7.8 %shard_map.93 = bf16[2,1024,512]{2,1,0:T(8,128)(2,1)} custom-call(bf16[2,1024,512]{2,1,0:T(8,128)(2,1)} %x_ref.5, f32[2,1024,512]{2,1,0:T(8,128)} %get-tuple-element.82.dmid_ref, bf16[2,656,1024]{2,1,0:T(8,128)(2,1)} %get-tuple-element.84.back_ref, bf16[656,512]{1,0:T(8,128)(2,1)} %get-tuple-element.46.turned_ref.refs_9_, ...), custom_call_target="tpu_custom_call" | custom-call | flops 8800000000 | bytes 800000 | tf_op jit(solution)/shard_map/pallas_call | solution.py:848
  253.9 2.4 shard_map.94
  (110 shorter events, 29.9 us)
Async XLA Ops:
  2.4 15.1 %collective-permute-start.2 = (bf16[192,512]{1,0:T(8,128)(2,1)}, bf16[192,512]{1,0:T(8,128)(2,1)S(1)}, u32[]{:S(2)}, u32[]{:S(2)}) collective-permute-start(bf16[192,512]{1,0:T(8,128)(2,1)} %shard_map.85), channel_id=1, source_target_pairs={{0,16},{1,17},{2,18},{3,19},{4,20},{5,21},{6,22},{7,23},{8,24},{9,... | collective-permute-start | bytes 589832 | tf_op jit(solution)/shard_map/ppermute | solution.py:894
  6.4 11.1 %collective-permute-start.1 = (bf16[192,512]{1,0:T(8,128)(2,1)}, bf16[192,512]{1,0:T(8,128)(2,1)S(1)}, u32[]{:S(2)}, u32[]{:S(2)}) collective-permute-start(bf16[192,512]{1,0:T(8,128)(2,1)} %shard_map.85), channel_id=1, source_target_pairs={{0,8},{1,9},{2,10},{3,11},{4,12},{5,13},{6,14},{7,15},{8,0},{9,1},... | collective-permute-start | bytes 589832 | tf_op jit(solution)/shard_map/ppermute | solution.py:894
  8.0 13.2 %collective-permute-start = (bf16[192,512]{1,0:T(8,128)(2,1)}, bf16[192,512]{1,0:T(8,128)(2,1)S(1)}, u32[]{:S(2)}, u32[]{:S(2)}) collective-permute-start(bf16[192,512]{1,0:T(8,128)(2,1)} %shard_map.85), channel_id=1, source_target_pairs={{0,24},{1,25},{2,26},{3,27},{4,28},{5,29},{6,30},{7,31},{8,16},{9,... | collective-permute-start | bytes 589832 | tf_op jit(solution)/shard_map/ppermute | solution.py:894
  22.3 9.5 %collective-permute-start.11 = (bf16[224,512]{1,0:T(8,128)(2,1)S(1)}, bf16[224,512]{1,0:T(8,128)(2,1)S(1)}, u32[]{:S(2)}, u32[]{:S(2)}) collective-permute-start(bf16[224,512]{1,0:T(8,128)(2,1)S(1)} %pad_maximum_fusion.1.refs_0_.refs_6_), channel_id=1, source_target_pairs={{0,6},{1,7},{2,4},{3,5},{4,2},{5,3},{6,0},{7,1},{8,14},{9,15},{10,... | collective-permute-start | bytes 688136 | tf_op jit(solution)/shard_map/ppermute | solution.py:894
  24.8 9.8 %collective-permute-start.9 = (bf16[224,512]{1,0:T(8,128)(2,1)S(1)}, bf16[224,512]{1,0:T(8,128)(2,1)S(1)}, u32[]{:S(2)}, u32[]{:S(2)}) collective-permute-start(bf16[224,512]{1,0:T(8,128)(2,1)S(1)} %pad_maximum_fusion.1.refs_0_.refs_6_), channel_id=1, source_target_pairs={{0,4},{1,5},{2,6},{3,7},{4,0},{5,1},{6,2},{7,3},{8,12},{9,13},{10,... | collective-permute-start | bytes 688136 | tf_op jit(solution)/shard_map/ppermute | solution.py:894
  25.8 10.2 %collective-permute-start.6 = (bf16[224,512]{1,0:T(8,128)(2,1)S(1)}, bf16[224,512]{1,0:T(8,128)(2,1)S(1)}, u32[]{:S(2)}, u32[]{:S(2)}) collective-permute-start(bf16[224,512]{1,0:T(8,128)(2,1)S(1)} %pad_maximum_fusion.1.refs_0_.refs_6_), channel_id=1, source_target_pairs={{0,1},{1,0},{2,3},{3,2},{4,5},{5,4},{6,7},{7,6},{8,9},{9,8},{10,11... | collective-permute-start | bytes 688136 | tf_op jit(solution)/shard_map/ppermute | solution.py:894
  35.9 44.0 %collective-permute-start.13 = (bf16[3,192,512]{2,1,0:T(8,128)(2,1)S(1)}, bf16[3,192,512]{2,1,0:T(8,128)(2,1)S(1)}, u32[]{:S(2)}, u32[]{:S(2)}) collective-permute-start(bf16[3,192,512]{2,1,0:T(8,128)(2,1)S(1)} %pad_maximum_fusion.refs_14_.refs_5_), channel_id=1, source_target_pairs={{0,1},{1,0},{2,3},{3,2},{4,5},{5,4},{6,7},{7,6},{8,9},{9,8},{10,11... | collective-permute-start | bytes 1769480 | tf_op jit(solution)/shard_map/ppermute | solution.py:894
  36.0 20.3 %collective-permute-start.5 = (bf16[3,192,512]{2,1,0:T(8,128)(2,1)S(1)}, bf16[3,192,512]{2,1,0:T(8,128)(2,1)S(1)}, u32[]{:S(2)}, u32[]{:S(2)}) collective-permute-start(bf16[3,192,512]{2,1,0:T(8,128)(2,1)S(1)} %pad_maximum_fusion.refs_14_.refs_5_), channel_id=1, source_target_pairs={{0,6},{1,7},{2,4},{3,5},{4,2},{5,3},{6,0},{7,1},{8,14},{9,15},{10,... | collective-permute-start | bytes 1769480 | tf_op jit(solution)/shard_map/ppermute | solution.py:894
  37.8 27.5 %collective-permute-start.4 = (bf16[3,192,512]{2,1,0:T(8,128)(2,1)S(1)}, bf16[3,192,512]{2,1,0:T(8,128)(2,1)S(1)}, u32[]{:S(2)}, u32[]{:S(2)}) collective-permute-start(bf16[3,192,512]{2,1,0:T(8,128)(2,1)S(1)} %pad_maximum_fusion.refs_14_.refs_5_), channel_id=1, source_target_pairs={{0,4},{1,5},{2,6},{3,7},{4,0},{5,1},{6,2},{7,3},{8,12},{9,13},{10,... | collective-permute-start | bytes 1769480 | tf_op jit(solution)/shard_map/ppermute | solution.py:894
  39.0 26.3 %collective-permute-start.3 = (bf16[3,192,512]{2,1,0:T(8,128)(2,1)S(1)}, bf16[3,192,512]{2,1,0:T(8,128)(2,1)S(1)}, u32[]{:S(2)}, u32[]{:S(2)}) collective-permute-start(bf16[3,192,512]{2,1,0:T(8,128)(2,1)S(1)} %pad_maximum_fusion.refs_14_.refs_5_), channel_id=1, source_target_pairs={{0,2},{1,3},{2,0},{3,1},{4,6},{5,7},{6,4},{7,5},{8,10},{9,11},{10,... | collective-permute-start | bytes 1769480 | tf_op jit(solution)/shard_map/ppermute | solution.py:894
  65.4 14.6 %collective-permute-start.16 = (bf16[3,192,512]{2,1,0:T(8,128)(2,1)S(1)}, bf16[3,192,512]{2,1,0:T(8,128)(2,1)S(1)}, u32[]{:S(2)}, u32[]{:S(2)}) collective-permute-start(bf16[3,192,512]{2,1,0:T(8,128)(2,1)S(1)} %collective-permute-done.5.refs_20_.refs_11_), channel_id=1, source_target_pairs={{0,1},{1,0},{2,3},{3,2},{4,5},{5,4},{6,7},{7,6},{8,9},{9,8},{10,11... | collective-permute-start | bytes 1769480 | tf_op jit(solution)/shard_map/ppermute | solution.py:894
  65.4 14.6 %collective-permute-start.15 = (bf16[3,192,512]{2,1,0:T(8,128)(2,1)S(1)}, bf16[3,192,512]{2,1,0:T(8,128)(2,1)S(1)}, u32[]{:S(2)}, u32[]{:S(2)}) collective-permute-start(bf16[3,192,512]{2,1,0:T(8,128)(2,1)S(1)} %collective-permute-done.4.refs_18_.refs_9_), channel_id=1, source_target_pairs={{0,1},{1,0},{2,3},{3,2},{4,5},{5,4},{6,7},{7,6},{8,9},{9,8},{10,11... | collective-permute-start | bytes 1769480 | tf_op jit(solution)/shard_map/ppermute | solution.py:894
  65.9 14.1 %collective-permute-start.14 = (bf16[3,192,512]{2,1,0:T(8,128)(2,1)S(1)}, bf16[3,192,512]{2,1,0:T(8,128)(2,1)S(1)}, u32[]{:S(2)}, u32[]{:S(2)}) collective-permute-start(bf16[3,192,512]{2,1,0:T(8,128)(2,1)S(1)} %collective-permute-done.3.refs_16_.refs_7_), channel_id=1, source_target_pairs={{0,1},{1,0},{2,3},{3,2},{4,5},{5,4},{6,7},{7,6},{8,9},{9,8},{10,11... | collective-permute-start | bytes 1769480 | tf_op jit(solution)/shard_map/ppermute | solution.py:894
  142.3 20.3 %collective-permute-start.22 = (bf16[3,192,512]{2,1,0:T(8,128)(2,1)S(1)}, bf16[3,192,512]{2,1,0:T(8,128)(2,1)S(1)}, u32[]{:S(2)}, u32[]{:S(2)}) collective-permute-start(bf16[3,192,512]{2,1,0:T(8,128)(2,1)S(1)} %get-tuple-element.89), channel_id=1, source_target_pairs={{0,2},{1,3},{2,0},{3,1},{4,6},{5,7},{6,4},{7,5},{8,10},{9,11},{10,... | collective-permute-start | bytes 1769480 | tf_op jit(solution)/shard_map/ppermute | solution.py:894
  143.8 27.8 %collective-permute-start.24 = (bf16[3,192,512]{2,1,0:T(8,128)(2,1)S(1)}, bf16[3,192,512]{2,1,0:T(8,128)(2,1)S(1)}, u32[]{:S(2)}, u32[]{:S(2)}) collective-permute-start(bf16[3,192,512]{2,1,0:T(8,128)(2,1)S(1)} %get-tuple-element.90), channel_id=1, source_target_pairs={{0,6},{1,7},{2,4},{3,5},{4,2},{5,3},{6,0},{7,1},{8,14},{9,15},{10,... | collective-permute-start | bytes 1769480 | tf_op jit(solution)/shard_map/ppermute | solution.py:894
  145.3 27.7 %collective-permute-start.23 = (bf16[3,192,512]{2,1,0:T(8,128)(2,1)S(1)}, bf16[3,192,512]{2,1,0:T(8,128)(2,1)S(1)}, u32[]{:S(2)}, u32[]{:S(2)}) collective-permute-start(bf16[3,192,512]{2,1,0:T(8,128)(2,1)S(1)} %get-tuple-element.91), channel_id=1, source_target_pairs={{0,4},{1,5},{2,6},{3,7},{4,0},{5,1},{6,2},{7,3},{8,12},{9,13},{10,... | collective-permute-start | bytes 1769480 | tf_op jit(solution)/shard_map/ppermute | solution.py:894
  212.8 15.4 %collective-permute-start.19 = (bf16[224,512]{1,0:T(8,128)(2,1)S(1)}, bf16[224,512]{1,0:T(8,128)(2,1)S(1)}, u32[]{:S(2)}, u32[]{:S(2)}) collective-permute-start(bf16[224,512]{1,0:T(8,128)(2,1)S(1)} %get-tuple-element.92), channel_id=1, source_target_pairs={{0,2},{1,3},{2,0},{3,1},{4,6},{5,7},{6,4},{7,5},{8,10},{9,11},{10,... | collective-permute-start | bytes 688136 | tf_op jit(solution)/shard_map/ppermute | solution.py:894
  213.7 16.2 %collective-permute-start.21 = (bf16[224,512]{1,0:T(8,128)(2,1)S(1)}, bf16[224,512]{1,0:T(8,128)(2,1)S(1)}, u32[]{:S(2)}, u32[]{:S(2)}) collective-permute-start(bf16[224,512]{1,0:T(8,128)(2,1)S(1)} %get-tuple-element.93), channel_id=1, source_target_pairs={{0,6},{1,7},{2,4},{3,5},{4,2},{5,3},{6,0},{7,1},{8,14},{9,15},{10,... | collective-permute-start | bytes 688136 | tf_op jit(solution)/shard_map/ppermute | solution.py:894
  214.9 15.0 %collective-permute-start.20 = (bf16[224,512]{1,0:T(8,128)(2,1)S(1)}, bf16[224,512]{1,0:T(8,128)(2,1)S(1)}, u32[]{:S(2)}, u32[]{:S(2)}) collective-permute-start(bf16[224,512]{1,0:T(8,128)(2,1)S(1)} %get-tuple-element.94), channel_id=1, source_target_pairs={{0,4},{1,5},{2,6},{3,7},{4,0},{5,1},{6,2},{7,3},{8,12},{9,13},{10,... | collective-permute-start | bytes 688136 | tf_op jit(solution)/shard_map/ppermute | solution.py:894
  217.1 26.7 %collective-permute-start.27 = (bf16[192,512]{1,0:T(8,128)(2,1)S(1)}, bf16[192,512]{1,0:T(8,128)(2,1)S(1)}, u32[]{:S(2)}, u32[]{:S(2)}) collective-permute-start(bf16[192,512]{1,0:T(8,128)(2,1)S(1)} %get-tuple-element.99), channel_id=1, source_target_pairs={{0,24},{1,25},{2,26},{3,27},{4,28},{5,29},{6,30},{7,31},{8,16},{9,... | collective-permute-start | bytes 589832 | tf_op jit(solution)/shard_map/ppermute | solution.py:894
  221.5 31.4 %collective-permute-start.25 = (bf16[192,512]{1,0:T(8,128)(2,1)S(1)}, bf16[192,512]{1,0:T(8,128)(2,1)S(1)}, u32[]{:S(2)}, u32[]{:S(2)}) collective-permute-start(bf16[192,512]{1,0:T(8,128)(2,1)S(1)} %get-tuple-element.101), channel_id=1, source_target_pairs={{0,8},{1,9},{2,10},{3,11},{4,12},{5,13},{6,14},{7,15},{16,24},{17,... | collective-permute-start | bytes 589832 | tf_op jit(solution)/shard_map/ppermute | solution.py:894
  228.3 24.7 %collective-permute-start.26 = (bf16[192,512]{1,0:T(8,128)(2,1)S(1)}, bf16[192,512]{1,0:T(8,128)(2,1)S(1)}, u32[]{:S(2)}, u32[]{:S(2)}) collective-permute-start(bf16[192,512]{1,0:T(8,128)(2,1)S(1)} %get-tuple-element.102), channel_id=1, source_target_pairs={{0,16},{1,17},{2,18},{3,19},{4,20},{5,21},{6,22},{7,23},{8,24},{9,... | collective-permute-start | bytes 589832 | tf_op jit(solution)/shard_map/ppermute | solution.py:894
  231.1 21.9 %collective-permute-start.30 = (bf16[224,512]{1,0:T(8,128)(2,1)S(1)}, bf16[224,512]{1,0:T(8,128)(2,1)S(1)}, u32[]{:S(2)}, u32[]{:S(2)}) collective-permute-start(bf16[224,512]{1,0:T(8,128)(2,1)S(1)} %add_convert_fusion.5), channel_id=1, source_target_pairs={{24,0},{25,1},{26,2},{27,3},{28,4},{29,5},{30,6},{31,7},{23,31}} | collective-permute-start | bytes 688136 | tf_op jit(solution)/shard_map/ppermute | solution.py:894
  232.4 20.6 %collective-permute-start.29 = (bf16[224,512]{1,0:T(8,128)(2,1)S(1)}, bf16[224,512]{1,0:T(8,128)(2,1)S(1)}, u32[]{:S(2)}, u32[]{:S(2)}) collective-permute-start(bf16[224,512]{1,0:T(8,128)(2,1)S(1)} %add_convert_fusion.5), channel_id=1, source_target_pairs={{16,0},{17,1},{18,2},{19,3},{20,4},{21,5},{22,6},{23,7},{15,31}} | collective-permute-start | bytes 688136 | tf_op jit(solution)/shard_map/ppermute | solution.py:894
  (32 other events, 255.5 us)

commit v2 on v1

--- a/solution.py
+++ b/solution.py
@@ -50,6 +50,10 @@
 
 def after(value, *others):
     return lax.optimization_barrier((value, *others))[0]
+
+
+def all_after(values, *others):
+    return lax.optimization_barrier((*values, *others))[: len(values)]
 
 
 def params(mib=VMEM_MIB):
@@ -144,72 +148,90 @@
 
 
 class Gathered:
-    def __init__(self, plan, lanes, head, rest, whole):
-        self.plan, self.lanes = plan, lanes
-        self.head, self.rest, self.whole = head, rest, whole
+    def __init__(self, plan, whole=None, own=(), head=(), rest=(), diag=()):
+        self.plan, self.whole = plan, whole
+        self.parts = [list(own), list(head), list(rest), list(diag)]
         self.small_at = ROW_S - 16 * plan.first(plan.devices - 1)
 
-    def arrays(self, need_head, need_rest):
+    def arrays(self, kinds):
         if self.whole is not None:
             return [self.whole]
-        return (self.head if need_head else []) + (self.rest if need_rest else [])
-
-    def fetch(self, place_ref, refs, need_head, start):
+        return [array for i in range(kinds) for array in self.parts[i]]
+
+    def fetch(self, place_ref, refs, kinds, start):
         if self.whole is not None:
             last = self.plan.devices - 1
             start(lambda d: refs[0].at[d], refs[0].at[last, pl.ds(self.small_at, SMALL), :])
             return
-        head = refs[: self.lanes] if need_head else None
-        rest = refs[self.lanes :] if need_head else refs
-        for place in range(self.lanes):
-
-            def source(d, place=place):
-                plane, lane = divmod(d, self.lanes)
-                if plane == 0:
-                    return head[lane ^ place]
-                return rest[lane ^ place].at[plane - 1]
-
-            small = None
-            if need_head:
-                small = head[(self.lanes - 1) ^ place].at[pl.ds(self.plan.rows, SMALL), :]
-            pl.when(place_ref[0] == place)(partial(start, source, small))
-
-
-def spread(j):
-    return (iota((64, D), 1) == 8 * iota((64, D), 0) + j).astype(BF16)
+        sets, at = [], 0
+        for part in self.parts[:kinds]:
+            sets.append(refs[at : at + len(part)])
+            at += len(part)
+        for mine in range(PLANES):
+            for place in range(LANES):
+
+                def source(d, mine=mine, place=place):
+                    plane, lane = divmod(d, LANES)
+                    lane = lane ^ place
+                    if plane == mine:
+                        return sets[0][lane]
+                    if plane == early_plane(mine):
+                        return sets[1][lane].at[pl.ds(0, self.plan.rows), :]
+                    if lane < 6:
+                        return sets[2][lane].at[late_planes(mine).index(plane)]
+                    return sets[3][2 * ((plane ^ mine) - 1) + (lane & 1)]
+
+                small = sets[1][(LANES - 1) ^ place].at[pl.ds(self.plan.rows, SMALL), :]
+                here = (place_ref[0] == place) & (place_ref[1] == mine)
+                pl.when(here)(partial(start, source, small))
+
+
+def narrow_places():
+    row, column = iota((D, D), 0), iota((D, D), 1)
+    return (column == 8 * (row % 64) + row // 64).astype(BF16)
 
 
 def narrow_transposed(flat):
-    out = jnp.zeros((64, D), F32)
-    for j in range(8):
-        out = out + dot(flat[:, 64 * j : 64 * (j + 1)], spread(j), TN)
-    return out
+    stacked = [
+        jnp.concatenate([flat[64 * i : 64 * (i + 1), 64 * j : 64 * (j + 1)] for i in (0, 1)], axis=1)
+        for j in range(8)
+    ]
+    return dot(jnp.concatenate(stacked, axis=0), narrow_places(), TN)
 
 
 def narrow_flat(turned):
-    return jnp.concatenate([dot(spread(j), turned, NT) for j in range(8)], axis=1)
+    stacked = dot(narrow_places(), turned, NT)
+    return jnp.concatenate(
+        [
+            jnp.concatenate(
+                [stacked[64 * j : 64 * (j + 1), 64 * i : 64 * (i + 1)] for j in range(8)], axis=1
+            )
+            for i in (0, 1)
+        ],
+        axis=0,
+    )
+
+
+def router_mask():
+    return iota((64, D), 1) % 8 == iota((64, D), 0) % 8
+
+
+def router_places():
+    return (iota((D, 64), 0) // 8 == iota((D, 64), 1)).astype(BF16)
 
 
 def router_transposed(flat):
-    lane = iota((8, D), 1) % 8
-    at = iota((8, D), 0)
-    pick = (iota((D, 64), 0) // 8 == iota((D, 64), 1)).astype(BF16)
-    pieces = []
-    for r in range(8):
-        row = jnp.broadcast_to(flat[r : r + 1, :], (8, D))
-        pieces.append(dot(jnp.where(lane == at, row, 0.0).astype(BF16), pick, NN))
-    return jnp.concatenate(pieces, axis=1)
+    rows = jnp.concatenate([jnp.broadcast_to(flat[r : r + 1, :], (8, D)) for r in range(8)], axis=0)
+    picked = dot(jnp.where(router_mask(), rows, 0.0).astype(BF16), router_places(), NN)
+    return jnp.concatenate([picked[8 * r : 8 * (r + 1), :] for r in range(8)], axis=1)
 
 
 def router_flat(turned):
-    lane = iota((8, D), 1) % 8
-    at = iota((8, D), 0)
-    pick = (iota((64, D), 1) // 8 == iota((64, D), 0)).astype(BF16)
-    rows = []
-    for r in range(8):
-        full = dot(turned[:, 64 * r : 64 * (r + 1)].astype(BF16), pick, NN)
-        rows.append(jnp.sum(jnp.where(lane == at, full, 0.0), axis=0, keepdims=True))
-    return jnp.concatenate(rows, axis=0)
+    stacked = jnp.concatenate([turned[:, 64 * r : 64 * (r + 1)] for r in range(8)], axis=0)
+    full = jnp.where(router_mask(), dot(stacked.astype(BF16), router_places(), NT), 0.0)
+    return jnp.concatenate(
+        [jnp.sum(full[8 * r : 8 * (r + 1)], axis=0, keepdims=True) for r in range(8)], axis=0
+    )
 
 
 def norm(source):
@@ -236,6 +258,12 @@
     )
 
 
+def two_rows(ref, pair, q0):
+    return jnp.concatenate(
+        [ref[0, 2 * pair + half : 2 * pair + half + 1, pl.ds(q0, QB)] for half in (0, 1)], axis=1
+    )
+
+
 def block_bias(code_ref, column_ref, q0, w0):
     row = code_ref[0, :, pl.ds(q0, QB)]
     bias = jnp.where(column_ref[pl.ds(w0, KB), :] == row, 0.0, NEG)
@@ -260,7 +288,7 @@
         start_rows(plan, source, 0, ROW_O, rows_ref, tmp_ref, sem)
         pltpu.make_async_copy(small, low_ref, sem.at[2]).start()
 
-    gathered.fetch(place_ref, refs, True, start)
+    gathered.fetch(place_ref, refs, 2, start)
     pltpu.make_async_copy(low_ref, low_ref, sem.at[2]).wait()
     end_rows(plan, 0, ROW_O, rows_ref, tmp_ref, sem)
     small_ref[...] = low_ref[...].astype(F32)
@@ -268,8 +296,7 @@
     turned_ref[T_R:T_K, :] = jnp.concatenate(
         [router_transposed(small_ref[0:8, :]), jnp.zeros((8, D), F32)], axis=0
     ).astype(BF16)
-    turned_ref[T_K:T_V, :] = narrow_transposed(rows_ref[ROW_K:ROW_V, :]).astype(BF16)
-    turned_ref[T_V:T_ALL, :] = narrow_transposed(rows_ref[ROW_V:ROW_O, :]).astype(BF16)
+    turned_ref[T_K:T_ALL, :] = narrow_transposed(rows_ref[ROW_K:ROW_O, :]).astype(BF16)
 
 
 def forward_row(x_ref, code_ref, turned_ref, small_ref, outs, column_ref):
@@ -293,22 +320,22 @@
         bias = block_bias(code_ref, column_ref, q0, w0)
         keys = k_ref[0, pl.ds(w0, KB), :]
         values = v_ref[0, pl.ds(w0, KB), :]
-        for pair in range(EXPERTS // 2):
-            scores = dot(keys, two_heads(q_ref, pair, q0), NN) * (HEAD**-0.5) + bias
-            peak = jnp.max(scores, axis=0, keepdims=True)
-            expd = jnp.exp(scores - peak)
-            summed = jnp.sum(expd, axis=0, keepdims=True)
-            att = dot(values, expd.astype(BF16), TN) * (1.0 / summed)
-            total = peak + jnp.log(summed)
+        pairs = range(EXPERTS // 2)
+        scores = [dot(keys, two_heads(q_ref, pair, q0), NN) * (HEAD**-0.5) + bias for pair in pairs]
+        peak = [jnp.max(part, axis=0, keepdims=True) for part in scores]
+        expd = [jnp.exp(part - top) for part, top in zip(scores, peak)]
+        summed = [jnp.sum(part, axis=0, keepdims=True) for part in expd]
+        atts = [dot(values, part.astype(BF16), TN) for part in expd]
+        for pair in pairs:
+            att = atts[pair] * (1.0 / summed[pair])
+            total = peak[pair] + jnp.log(summed[pair])
             for half in range(2):
-                head = 2 * pair + half
-                att_ref[0, 64 * head : 64 * (head + 1), pl.ds(q0, QB)] = att[
-                    :, QB * half : QB * (half + 1)
-                ]
-                lse_ref[0, head : head + 1, pl.ds(q0, QB)] = total[:, QB * half : QB * (half + 1)]
+                head, part = 2 * pair + half, slice(QB * half, QB * (half + 1))
+                att_ref[0, 64 * head : 64 * (head + 1), pl.ds(q0, QB)] = att[:, part]
+                lse_ref[0, head : head + 1, pl.ds(q0, QB)] = total[:, part]
         return carry
 
-    lax.fori_loop(0, length // QB, block_step, 0)
+    lax.fori_loop(0, length // QB, block_step, 0, unroll=2)
 
 
 def forward_first(plan, gathered, count, place_ref, x_ref, code_ref, *refs):
@@ -339,7 +366,7 @@
     scratch = [pltpu.VMEM((length, QB), F32)]
     in_specs = [row3(length, D), row3(1, length)]
     if before is None:
-        wins = gathered.arrays(True, False)
+        wins = gathered.arrays(2)
         kernel = partial(forward_first, plan, gathered, len(wins))
         operands = [place, x, code, *wins]
         in_specs = in_specs + [ANYWHERE] * len(wins)
@@ -396,12 +423,9 @@
 def gelu_parts(source):
     scale = (2.0 / jnp.pi) ** 0.5
     square = source * source
-    bent = jnp.tanh(source * (scale + (scale * 0.044715) * square))
-    half = 0.5 * source
-    value = half + half * bent
-    slope = (0.5 + 0.5 * bent) + (half - half * bent * bent) * (
-        scale + (3.0 * scale * 0.044715) * square
-    )
+    share = 0.5 + 0.5 * jnp.tanh(source * (scale + (scale * 0.044715) * square))
+    value = source * share
+    slope = share + (value - value * share) * (2.0 * scale + (6.0 * scale * 0.044715) * square)
     return value, slope
 
 
@@ -415,48 +439,101 @@
     )
 
 
-def up_kernel(plan, gathered, count, place_ref, counts_ref, *refs):
+def feed_kernel(plan, gathered, count, pieces, place_ref, counts_ref, *refs):
     x_ref, cot_ref, att_ref, prob_ref, experts_ref, small_ref = refs[:6]
     wins = refs[6 : 6 + count]
-    hid_ref, slope_ref, mid_ref, up_ref, out_ref, gdown_ref = refs[6 + count : 12 + count]
-    rows_ref, tmp_ref, wide_ref, total_ref, sem = refs[12 + count :]
+    hid_ref, mid_ref, dmid_ref, datt_ref, dlog_ref, inner_ref = refs[6 + count : 12 + count]
+    down_ref, gout_ref, gsmall_ref, gup_ref, gdown_ref = refs[12 + count : 17 + count]
+    packed = refs[17 + count : -12]
+    rows_ref, up_ref, flat_ref, tmp_ref, tmp2_ref, wide_ref = refs[-12:-6]
+    tdown_ref, tup_ref, tout_ref, sem, sem2, pack_sem = refs[-6:]
 
     @pl.when(first_step())
     def _():
         def start(source, small):
             start_rows(plan, source, ROW_O, ROW_D, rows_ref, tmp_ref, sem)
-
-        gathered.fetch(place_ref, wins, True, start)
+            start_rows(plan, source, ROW_D, ROW_S, down_ref, tmp2_ref, sem2)
+
+        gathered.fetch(place_ref, wins, 4, start)
+        for ref in (tdown_ref, tup_ref, tout_ref, gsmall_ref):
+            ref[...] = jnp.zeros_like(ref)
         end_rows(plan, ROW_O, ROW_D, rows_ref, tmp_ref, sem)
         for c in range(4):
-            lanes = slice(128 * c, 128 * (c + 1))
-            wide_ref[c] = rows_ref[D:, lanes].astype(F32)
+            wide_ref[c] = rows_ref[D:, 128 * c : 128 * (c + 1)].astype(F32)
             for j in range(4):
                 up_ref[:, D * j + 128 * c : D * j + 128 * (c + 1)] = wide_ref[
                     c, pl.ds(j, D, stride=4), :
                 ].astype(BF16)
-        out_ref[...] = rows_ref[0:D, :]
-        total_ref[...] = jnp.zeros_like(total_ref)
+        end_rows(plan, ROW_D, ROW_S, down_ref, tmp2_ref, sem2)
 
     amount = x_ref.shape[1]
-    gate = prob_ref[0] * chosen_experts(experts_ref, amount)
-    mixed = by_head(att_ref[0], gate).astype(BF16)
+    prob = prob_ref[0]
+    chosen = chosen_experts(experts_ref, amount)
+    gate = prob * chosen
+    att = att_ref[0]
+    mixed = by_head(att, gate).astype(BF16)
     middle = x_ref[0].astype(F32) + dot(mixed, rows_ref[0:D, :], TN)
     mid_ref[0] = middle
-    normal, _ = norm(middle)
-    h = (normal * small_ref[14:15, :] + small_ref[15:16, :]).astype(BF16)
-    grad_low = (valid_tokens(counts_ref, amount) * cot_ref[0].astype(F32)).astype(BF16)
-    for j in range(4):
-        part = slice(D * j, D * (j + 1))
-        value, slope = gelu_parts(dot(h, up_ref[:, part], NN) + small_ref[8 + j : 9 + j, :])
+    normal, scaler = norm(middle)
+    gain = small_ref[14:15, :]
+    h = (normal * gain + small_ref[15:16, :]).astype(BF16)
+    grad = valid_tokens(counts_ref, amount) * cot_ref[0].astype(F32)
+    grad_low = grad.astype(BF16)
+    parts = [slice(2 * D * j, 2 * D * (j + 1)) for j in range(2)]
+    dhid = [dot(grad_low, down_ref[part, :], NT) for part in parts]
+    back = jnp.zeros((amount, D), F32)
+    for j, part in enumerate(parts):
+        bias = jnp.concatenate([small_ref[8 + i : 9 + i, :] for i in (2 * j, 2 * j + 1)], axis=1)
+        value, slope = gelu_parts(dot(h, up_ref[:, part], NN) + bias)
         value = value.astype(BF16)
         hid_ref[0, :, part] = value
-        slope_ref[0, :, part] = slope.astype(BF16)
-        total_ref[part, :] += dot(value, grad_low, TN)
+        pre = slope * dhid[j]
+        sums = jnp.sum(pre, axis=0, keepdims=True)
+        for i in range(2):
+            gsmall_ref[2 * j + i : 2 * j + i + 1, :] += sums[:, D * i : D * (i + 1)]
+        pre = pre.astype(BF16)
+        tdown_ref[part, :] += dot(value, grad_low, TN)
+        tup_ref[:, part] += dot(h, pre, TN)
+        back = back + dot(pre, up_ref[:, part], NT)
+    gsmall_ref[4:5, :] += jnp.sum(back * normal, axis=0, keepdims=True)
+    gsmall_ref[5:6, :] += jnp.sum(back, axis=0, keepdims=True)
+    gsmall_ref[6:7, :] += jnp.sum(grad, axis=0, keepdims=True)
+    dmid = grad + norm_back(back * gain, normal, scaler)
+    dmid_ref[0] = dmid
+    branch = dmid.astype(BF16)
+    tout_ref[...] += dot(mixed, branch, NN)
+    dmixed = dot(rows_ref[0:D, :], branch, NT)
+    dgate = jnp.concatenate(
+        [
+            jnp.sum(
+                dmixed[64 * e : 64 * (e + 1)] * att[64 * e : 64 * (e + 1)], axis=0, keepdims=True
+            )
+            for e in range(EXPERTS)
+        ],
+        axis=0,
+    )
+    datt_ref[0] = by_head(dmixed, gate).astype(BF16)
+    inner_ref[0] = gate * dgate
+    dprob = dgate * chosen
+    dlog = prob * (dprob - jnp.sum(prob * dprob, axis=0, keepdims=True))
+    dlog_ref[0] = jnp.concatenate([dlog, jnp.zeros_like(dlog)], axis=0).astype(BF16)
 
     @pl.when(last_step())
     def _():
-        gdown_ref[...] = total_ref[...].astype(BF16)
+        gdown_ref[...] = tdown_ref[...].astype(BF16)
+        if pieces:
+            pack_start(pieces, [1], place_ref, [flat_ref, gdown_ref], packed, pack_sem)
+        gout_ref[...] = tout_ref[...].astype(BF16)
+        for c in range(4):
+            for j in range(4):
+                wide_ref[c, pl.ds(j, D, stride=4), :] = tup_ref[
+                    :, D * j + 128 * c : D * j + 128 * (c + 1)
+                ]
+            flat_ref[:, 128 * c : 128 * (c + 1)] = wide_ref[c].astype(BF16)
+        gup_ref[...] = flat_ref[0 : gup_ref.shape[0], :]
+        if pieces:
+            pack_start(pieces, [0], place_ref, [flat_ref, gdown_ref], packed, pack_sem)
+            pack_end(packed, pack_sem)
 
 
 def row_block(*tail):
@@ -478,11 +555,13 @@
     return jax.ShapeDtypeStruct(shape, dtype)
 
 
-def feed_up(plan, gathered, place, counts, x, cot, att, prob, experts, small):
+def feed_forward(plan, gathered, place, counts, x, cot, att, prob, experts, small, pieces):
     rows, length = x.shape[0], x.shape[1]
-    wins = gathered.arrays(True, True)
+    wins = gathered.arrays(4)
+    head = LATE_ROWS if pieces else FF
+    packed = [kind(BF16, LANES // 2, PLANES - 1, plan.rows, D)] * 2 if pieces else []
     return pl.pallas_call(
-        partial(up_kernel, plan, gathered, len(wins)),
+        partial(feed_kernel, plan, gathered, len(wins), pieces),
         grid_spec=pltpu.PrefetchScalarGridSpec(
             num_scalar_prefetch=2,
             grid=(rows, length // TB),
@@ -497,214 +576,55 @@
             + [ANYWHERE] * len(wins),
             out_specs=[
                 row_block(FF),
-                row_block(FF),
                 row_block(D),
-                whole(D, FF),
+                row_block(D),
+                column_block(D),
+                column_block(16),
+                column_block(8),
+                whole(FF, D),
                 whole(D, D),
+                whole(8, D),
+                whole(head, D),
                 whole(FF, D),
-            ],
+            ]
+            + [ANYWHERE] * len(packed),
             scratch_shapes=[
                 pltpu.VMEM((ROW_D - ROW_O, D), BF16),
+                pltpu.VMEM((D, FF), BF16),
+                pltpu.VMEM((FF, D), BF16),
                 pltpu.VMEM((shared_rows(plan, ROW_O, ROW_D), D), BF16),
+                pltpu.VMEM((shared_rows(plan, ROW_D, ROW_S), D), BF16),
                 pltpu.VMEM((4, FF, 128), F32),
                 pltpu.VMEM((FF, D), F32),
+                pltpu.VMEM((D, FF), F32),
+                pltpu.VMEM((D, D), F32),
                 pltpu.SemaphoreType.DMA((2,)),
-            ],
-        ),
-        out_shape=[
-            kind(BF16, rows, length, FF),
-            kind(BF16, rows, length, FF),
-            kind(F32, rows, length, D),
-            kind(BF16, D, FF),
-            kind(BF16, D, D),
-            kind(BF16, FF, D),
-        ],
-        cost_estimate=cost(30),
-        compiler_params=params(),
-    )(place, counts, x, cot, att, prob, experts, small, *wins)
-
-
-def hidden_kernel(plan, gathered, count, pieces, place_ref, counts_ref, *refs):
-    cot_ref, slope_ref, mid_ref, small_ref, gdown_ref = refs[:5]
-    wins = refs[5 : 5 + count]
-    pre_ref, down_ref, gbias_ref, gup_ref = refs[5 + count : 9 + count]
-    packed = refs[9 + count : -6]
-    flat_ref, tmp_ref, wide_ref, total_ref, sem, pack_sem = refs[-6:]
-
-    @pl.when(first_step())
-    def _():
-        def start(source, small):
-            start_rows(plan, source, ROW_D, ROW_S, down_ref, tmp_ref, sem)
-
-        gathered.fetch(place_ref, wins, False, start)
-        if pieces:
-            pack_start(pieces, [1], place_ref, [flat_ref, gdown_ref], packed, pack_sem)
-        end_rows(plan, ROW_D, ROW_S, down_ref, tmp_ref, sem)
-        total_ref[...] = jnp.zeros_like(total_ref)
-        gbias_ref[...] = jnp.zeros_like(gbias_ref)
-
-    amount = cot_ref.shape[1]
-    grad = valid_tokens(counts_ref, amount) * cot_ref[0].astype(F32)
-    grad_low = grad.astype(BF16)
-    normal, _ = norm(mid_ref[0])
-    h = (normal * small_ref[14:15, :] + small_ref[15:16, :]).astype(BF16)
-    for j in range(4):
-        part = slice(D * j, D * (j + 1))
-        pre = slope_ref[0, :, part].astype(F32) * dot(grad_low, down_ref[part, :], NT)
-        gbias_ref[j : j + 1, :] += jnp.sum(pre, axis=0, keepdims=True)
-        pre = pre.astype(BF16)
-        pre_ref[0, :, part] = pre
-        total_ref[:, part] += dot(h, pre, TN)
-    gbias_ref[4:5, :] += jnp.sum(grad, axis=0, keepdims=True)
-
-    @pl.when(last_step())
-    def _():
-        for c in range(4):
-            for j in range(4):
-                wide_ref[c, pl.ds(j, D, stride=4), :] = total_ref[
-                    :, D * j + 128 * c : D * j + 128 * (c + 1)
-                ]
-            flat_ref[:, 128 * c : 128 * (c + 1)] = wide_ref[c].astype(BF16)
-        gup_ref[...] = flat_ref[0 : gup_ref.shape[0], :]
-        if pieces:
-            pack_start(pieces, [0], place_ref, [flat_ref, gdown_ref], packed, pack_sem)
-            pack_end(packed, pack_sem)
-
-
-def feed_hidden(plan, gathered, place, counts, cot, slope, mid, small, gdown, pieces):
-    rows, length = cot.shape[0], cot.shape[1]
-    wins = gathered.arrays(False, True)
-    head = LATE_ROWS if pieces else FF
-    packed = [kind(BF16, LANES // 2, PLANES - 1, plan.rows, D)] * 2 if pieces else []
-    return pl.pallas_call(
-        partial(hidden_kernel, plan, gathered, len(wins), pieces),
-        grid_spec=pltpu.PrefetchScalarGridSpec(
-            num_scalar_prefetch=2,
-            grid=(rows, length // TB),
-            in_specs=[row_block(D), row_block(FF), row_block(D), whole(SMALL, D), whole(FF, D)]
-            + [ANYWHERE] * len(wins),
-            out_specs=[row_block(FF), whole(FF, D), whole(8, D), whole(head, D)]
-            + [ANYWHERE] * len(packed),
-            scratch_shapes=[
-                pltpu.VMEM((FF, D), BF16),
-                pltpu.VMEM((shared_rows(plan, ROW_D, ROW_S), D), BF16),
-                pltpu.VMEM((4, FF, 128), F32),
-                pltpu.VMEM((D, FF), F32),
                 pltpu.SemaphoreType.DMA((2,)),
                 pltpu.SemaphoreType.DMA((2,)),
             ],
         ),
         out_shape=[
             kind(BF16, rows, length, FF),
-            kind(BF16, FF, D),
-            kind(F32, 8, D),
-            kind(BF16, head, D),
-        ]
-        + packed,
-        cost_estimate=cost(20),
-        compiler_params=params(),
-    )(place, counts, cot, slope, mid, small, gdown, *wins)
-
-
-def branch_kernel(
-    counts_ref,
-    cot_ref,
-    pre_ref,
-    mid_ref,
-    att_ref,
-    prob_ref,
-    experts_ref,
-    small_ref,
-    up_ref,
-    out_ref,
-    dmid_ref,
-    datt_ref,
-    dlog_ref,
-    gout_ref,
-    gnorm_ref,
-    total_ref,
-):
-    @pl.when(first_step())
-    def _():
-        total_ref[...] = jnp.zeros_like(total_ref)
-        gnorm_ref[...] = jnp.zeros_like(gnorm_ref)
-
-    amount = cot_ref.shape[1]
-    grad = valid_tokens(counts_ref, amount) * cot_ref[0].astype(F32)
-    normal, scaler = norm(mid_ref[0])
-    back = dot(pre_ref[0], up_ref[...], NT)
-    gnorm_ref[0:1, :] += jnp.sum(back * normal, axis=0, keepdims=True)
-    gnorm_ref[1:2, :] += jnp.sum(back, axis=0, keepdims=True)
-    dmid = grad + norm_back(back * small_ref[14:15, :], normal, scaler)
-    dmid_ref[0] = dmid
-    branch = dmid.astype(BF16)
-    prob = prob_ref[0]
-    chosen = chosen_experts(experts_ref, amount)
-    gate = prob * chosen
-    att = att_ref[0]
-    total_ref[...] += dot(by_head(att, gate).astype(BF16), branch, NN)
-    dmixed = dot(out_ref[...], branch, NT)
-    dgate = jnp.concatenate(
-        [
-            jnp.sum(
-                dmixed[64 * e : 64 * (e + 1)] * att[64 * e : 64 * (e + 1)], axis=0, keepdims=True
-            )
-            for e in range(EXPERTS)
-        ],
-        axis=0,
-    )
-    datt_ref[0] = by_head(dmixed, gate).astype(BF16)
-    dprob = dgate * chosen
-    dlog = prob * (dprob - jnp.sum(prob * dprob, axis=0, keepdims=True))
-    dlog_ref[0] = jnp.concatenate([dlog, jnp.zeros_like(dlog)], axis=0).astype(BF16)
-
-    @pl.when(last_step())
-    def _():
-        gout_ref[...] = total_ref[...].astype(BF16)
-
-
-def feed_branch(counts, cot, pre, mid, att, prob, experts, small, up, out):
-    rows, length = cot.shape[0], cot.shape[1]
-    return pl.pallas_call(
-        branch_kernel,
-        grid_spec=pltpu.PrefetchScalarGridSpec(
-            num_scalar_prefetch=1,
-            grid=(rows, length // TB),
-            in_specs=[
-                row_block(D),
-                row_block(FF),
-                row_block(D),
-                column_block(D),
-                column_block(8),
-                column_block(2),
-                whole(SMALL, D),
-                whole(D, FF),
-                whole(D, D),
-            ],
-            out_specs=[
-                row_block(D),
-                column_block(D),
-                column_block(16),
-                whole(D, D),
-                whole(8, D),
-            ],
-            scratch_shapes=[pltpu.VMEM((D, D), F32)],
-        ),
-        out_shape=[
+            kind(F32, rows, length, D),
             kind(F32, rows, length, D),
             kind(BF16, rows, D, length),
             kind(BF16, rows, 16, length),
+            kind(F32, rows, 8, length),
+            kind(BF16, FF, D),
             kind(BF16, D, D),
             kind(F32, 8, D),
-        ],
-        cost_estimate=cost(16),
-        compiler_params=params(),
-    )(counts, cot, pre, mid, att, prob, experts, small, up, out)
+            kind(BF16, head, D),
+            kind(BF16, FF, D),
+        ]
+        + packed,
+        cost_estimate=cost(50),
+        compiler_params=params(60),
+    )(place, counts, x, cot, att, prob, experts, small, *wins)
 
 
 def backward_kernel(pieces, place_ref, *refs):
-    x_ref, h_ref, q_ref, k_ref, v_ref, lse_ref, datt_ref, dlog_ref, code_ref = refs[:9]
-    turned_ref, gbias_ref, gnorm_ref, gout_ref, gup_ref = refs[9:14]
+    x_ref, h_ref, q_ref, k_ref, v_ref, lse_ref, inner_ref, datt_ref, dlog_ref, code_ref = refs[:10]
+    turned_ref, gsmall_ref, gout_ref, gup_ref = refs[10:14]
     back_ref, ghead_ref, glow_ref = refs[14:17]
     packed = refs[17:-7]
     dk_ref, dv_ref, column_ref, total_ref, gain_ref, shift_ref, pack_sem = refs[-7:]
@@ -725,33 +645,30 @@
         bias = block_bias(code_ref, column_ref, q0, w0)
         keys = k_ref[0, pl.ds(w0, KB), :]
         values = v_ref[0, pl.ds(w0, KB), :]
-        dk = jnp.zeros((KB, HEAD), F32)
-        dv = jnp.zeros((KB, HEAD), F32)
-        for pair in range(EXPERTS // 2):
-            queries = two_heads(q_ref, pair, q0)
-            datt = two_heads(datt_ref, pair, q0)
-            total = jnp.concatenate(
-                [lse_ref[0, 2 * pair + half : 2 * pair + half + 1, pl.ds(q0, QB)] for half in (0, 1)],
-                axis=1,
-            )
-            scores = dot(keys, queries, NN) * (HEAD**-0.5) + bias
-            soft = jnp.exp(scores - total)
-            dsoft = dot(values, datt, NN)
-            dv = dv + dot(soft.astype(BF16), datt, NT)
-            inner = jnp.sum(soft * dsoft, axis=0, keepdims=True)
-            dscores = (soft * (dsoft - inner)).astype(BF16)
-            dk = dk + dot(dscores, queries, NT)
-            dq = (dot(keys, dscores, TN) * (HEAD**-0.5)).astype(BF16)
+        pairs = range(EXPERTS // 2)
+        queries = [two_heads(q_ref, pair, q0) for pair in pairs]
+        datt = [two_heads(datt_ref, pair, q0) for pair in pairs]
+        soft = [
+            jnp.exp(dot(keys, part, NN) * (HEAD**-0.5) + bias - two_rows(lse_ref, pair, q0))
+            for pair, part in enumerate(queries)
+        ]
+        dscores = [
+            (soft[pair] * (dot(values, part, NN) - two_rows(inner_ref, pair, q0))).astype(BF16)
+            for pair, part in enumerate(datt)
+        ]
+        soft = jnp.concatenate([part.astype(BF16) for part in soft], axis=1)
+        dv = dot(soft, jnp.concatenate(datt, axis=1), NT)
+        dk = dot(jnp.concatenate(dscores, axis=1), jnp.concatenate(queries, axis=1), NT)
+        for pair in pairs:
+            dq = (dot(keys, dscores[pair], TN) * (HEAD**-0.5)).astype(BF16)
             for half in range(2):
-                head = 2 * pair + half
-                back_ref[0, 64 * head : 64 * (head + 1), pl.ds(q0, QB)] = dq[
-                    :, QB * half : QB * (half + 1)
-                ]
+                head, part = 2 * pair + half, slice(QB * half, QB * (half + 1))
+                back_ref[0, 64 * head : 64 * (head + 1), pl.ds(q0, QB)] = dq[:, part]
         dk_ref[pl.ds(w0, KB), :] += dk * (HEAD**-0.5)
         dv_ref[pl.ds(w0, KB), :] += dv
         return carry
 
-    lax.fori_loop(0, length // QB, block_step, 0)
+    lax.fori_loop(0, length // QB, block_step, 0, unroll=2)
     back_ref[0, T_R:T_K, :] = dlog_ref[0]
     back_ref[0, T_K:T_V, :] = dk_ref[...].T.astype(BF16)
     back_ref[0, T_V:T_ALL, :] = dv_ref[...].T.astype(BF16)
@@ -764,18 +681,15 @@
     @pl.when(pl.program_id(0) == pl.num_programs(0) - 1)
     def _():
         ghead_ref[0:D, :] = total_ref[0:D, :].T.astype(BF16)
-        low = total_ref[T_K:T_ALL, :].astype(BF16)
-        ghead_ref[D : D + 64, :] = narrow_flat(low[0:64]).astype(BF16)
-        ghead_ref[D + 64 : D + 128, :] = narrow_flat(low[64:128]).astype(BF16)
+        ghead_ref[D:ROW_O, :] = narrow_flat(total_ref[T_K:T_ALL, :].astype(BF16)).astype(BF16)
         turned = turned_ref[...].astype(F32)
         glow_ref[...] = jnp.concatenate(
             [
                 router_flat(total_ref[T_R : T_R + 8, :]),
-                gbias_ref[0:4, :],
+                gsmall_ref[0:4, :],
                 jnp.sum(turned * gain_ref[...], axis=0, keepdims=True),
                 jnp.sum(turned * shift_ref[...], axis=0, keepdims=True),
-                gnorm_ref[0:2, :],
-                gbias_ref[4:5, :],
+                gsmall_ref[4:7, :],
                 jnp.zeros((SMALL - 17, D), F32),
             ],
             axis=0,
@@ -787,7 +701,7 @@
 
 
 def attention_backward(
-    plan, place, x, h, q, k, v, lse, datt, dlog, code, turned, gbias, gnorm, gout, gup, pieces
+    plan, place, x, h, q, k, v, lse, inner, datt, dlog, code, turned, gsmall, gout, gup, pieces
 ):
     rows, length = x.shape[0], x.shape[1]
     row3 = lambda a, b: pl.BlockSpec((1, a, b), lambda i, *_: (i, 0, 0))
@@ -805,11 +719,11 @@
                 row3(length, HEAD),
                 row3(length, HEAD),
                 row3(8, length),
+                row3(8, length),
                 row3(D, length),
                 row3(16, length),
                 row3(1, length),
                 whole(T_ALL, D),
-                whole(8, D),
                 whole(8, D),
                 whole(D, D),
                 whole(head, D),
@@ -834,7 +748,7 @@
         + packed,
         cost_estimate=cost(33),
         compiler_params=params(),
-    )(place, x, h, q, k, v, lse, datt, dlog, code, turned, gbias, gnorm, gout, gup)
+    )(place, x, h, q, k, v, lse, inner, datt, dlog, code, turned, gsmall, gout, gup)
 
 
 def input_kernel(x_ref, dmid_ref, back_ref, turned_ref, small_ref, gx_ref):
@@ -905,8 +819,12 @@
     return out
 
 
-def plane_spread(own):
-    return [own] + [across(own, bits) for bits in (2, 4, 6)]
+def early_plane(mine):
+    return 0 if mine else PLANES - 1
+
+
+def late_planes(mine):
+    return [z for z in range(PLANES) if z not in (mine, early_plane(mine))]
 
 
 def core_spread(got):
@@ -914,17 +832,31 @@
     return [part for both in zip(got, swapped) for part in both]
 
 
-def plane_gather(plan, window, my_plane):
+def gather_staged(plan, window, my_plane):
     got = [window]
     for s in range(1, PLANES):
-        got.append(
-            move(window, [(z * LANES + f, (z ^ s) * LANES + f) for z in range(PLANES) for f in range(LANES)])
-        )
-    of = lambda z: by_plane([got[z ^ mine] for mine in range(PLANES)], my_plane)
+        pairs = [(z * LANES + f, (z ^ s) * LANES + f) for z in range(PLANES) for f in range(LANES)]
+        got.append(move(window, pairs))
+    own = [window] + [across(window, bits) for bits in (2, 4, 6)]
+    of = lambda f: by_plane([got[f(mine) ^ mine] for mine in range(PLANES)], my_plane)
     low = ROW_S - 16 * plan.first(ALL - 1)
-    planes = [of(z) for z in range(PLANES)]
-    head = jnp.concatenate([planes[0], planes[-1][low : low + SMALL]], axis=0)
-    return head, jnp.stack(planes[1:])
+    last = of(lambda mine: PLANES - 1)
+    head = jnp.concatenate([of(early_plane), last[low : low + SMALL]], axis=0)
+    rest = jnp.stack([of(lambda mine: late_planes(mine)[0]), of(lambda mine: late_planes(mine)[1])])
+    head = [head] + [across(head, bits) for bits in (2, 4, 6)]
+    ready = [rest, *own]
+    rest = [rest] + [across(rest, bits) for bits in (2, 4)]
+    diag = []
+    for s in range(1, PLANES):
+        pairs = [
+            ((z ^ s) * LANES + f, z * LANES + f)
+            for z in range(PLANES)
+            if z ^ s in late_planes(z)
+            for f in range(LANES)
+        ]
+        diag.append(move(own[3], pairs))
+    spread = [core_spread(part) for part in (own, head, rest, diag)]
+    return Gathered(plan, None, *spread), ready
 
 
 def pack_start(pieces, sources, place_ref, ins, packed, sem):
@@ -974,17 +906,26 @@
     return [(keep[p].astype(F32) + got[p].astype(F32)).astype(BF16) for p in range(LANES // 2)]
 
 
-def plane_sum(parts):
+def plane_swap(parts):
+    return [parts[0]] + [across(parts[p], 2 * p) for p in range(1, LANES // 2)]
+
+
+def summed(parts):
     total = parts[0].astype(F32)
-    for p in range(1, LANES // 2):
-        total = total + across(parts[p], 2 * p).astype(F32)
+    for part in parts[1:]:
+        total = total + part.astype(F32)
     return total.astype(BF16)
 
 
-def main_parts(total, my_plane):
+def main_picks(total, my_plane):
     owned = [total[0]] + [total[z] for z in range(PLANES - 1)]
-    pick = lambda s: by_plane([owned[mine ^ s] for mine in range(PLANES)], my_plane)
-    out = [pick(0)]
+    return [
+        by_plane([owned[mine ^ s] for mine in range(PLANES)], my_plane) for s in range(PLANES)
+    ]
+
+
+def main_parts(picks):
+    out = [picks[0]]
     for s in range(1, PLANES):
         pairs = [
             (z * LANES + f, (z ^ s) * LANES + f)
@@ -992,7 +933,7 @@
             if z ^ s
             for f in range(LANES)
         ]
-        out.append(move(pick(s), pairs))
+        out.append(move(picks[s], pairs))
     return out
 
 
@@ -1068,19 +1009,15 @@
     plan = Plan(planes * lanes, shard.shape[0])
     my_plane, my_lane = lax.axis_index("dp"), lax.axis_index("fsdp")
     me = my_plane * lanes + my_lane
-    place = my_lane.astype(jnp.int32).reshape(1)
+    place = jnp.stack([my_lane, my_plane]).astype(jnp.int32)
     at = ((plan.lanes * me) % 64).astype(jnp.int32).reshape(1)
     window = make_window(plan, at, shard)
     staged = (planes, lanes, plan.lanes) == (PLANES, LANES, 659)
     main_pieces, head_pieces = [], []
-    ready = [place, place]
+    first = place
     if staged:
-        head, rest = plane_gather(plan, window, my_plane)
-        ready[0] = after(place, rest)
-        head = core_spread(plane_spread(head))
-        rest = plane_spread(rest)
-        ready[1] = after(place, *rest)
-        gathered = Gathered(plan, lanes, head, core_spread(rest), None)
+        gathered, ready = gather_staged(plan, window, my_plane)
+        first = after(place, *ready)
         main_pieces = window_pieces(
             plan, range(LANES, ALL), [(ROW_U, ROW_D), (ROW_D, ROW_S)], False
         )
@@ -1088,46 +1025,43 @@
             plan, range(LANES), [(0, ROW_O), (ROW_O, ROW_U), (ROW_U, ROW_U + LATE_ROWS)], True
         )
     else:
-        gathered = Gathered(plan, lanes, None, None, lax.all_gather(window, AXES, axis=0))
+        gathered = Gathered(plan, lax.all_gather(window, AXES, axis=0))
     rows, length = x.shape[0], x.shape[1]
     places = jnp.arange(length, dtype=jnp.int32)[None, :]
     code = jnp.where(places < counts[:, None], segments, -1 - places)
     code = code.astype(F32).reshape(-1, 1, length)
     pairs = jnp.swapaxes(experts, 1, 2)
-    state = attention_forward(plan, gathered, ready[0], x, code, 0, None)
+    state = attention_forward(plan, gathered, first, x, code, 0, None)
     turned, small = state[7:9]
     for row in range(1, rows):
         before = [*state[:7], turned, small]
-        state = attention_forward(plan, gathered, ready[1], x, code, row, before)
+        state = attention_forward(plan, gathered, place, x, code, row, before)
     q, k, v, h, prob, lse, att = state[:7]
-    hid, slope, mid, up, out, gdown = feed_up(
-        plan, gathered, place, counts, x, cot, att, prob, pairs, small
-    )
-    pre, down, gbias, gup, *packed = feed_hidden(
-        plan, gathered, place, counts, cot, slope, mid, small, gdown, main_pieces
-    )
-    dmid, datt, dlog, gout, gnorm = feed_branch(
-        counts, cot, pre, mid, att, prob, pairs, small, up, out
+    hid, mid, dmid, datt, dlog, inner, down, gout, gsmall, gup, gdown, *packed = feed_forward(
+        plan, gathered, place, counts, x, cot, att, prob, pairs, small, main_pieces
     )
     third = place
     if staged:
         parts = core_sum(*packed)
         third = after(place, *parts)
-        main = plane_sum(parts)
+        main = plane_swap(parts)
     back, ghead, glow, *packed = attention_backward(
-        plan, third, x, h, q, k, v, lse, datt, dlog, code, turned, gbias, gnorm, gout, gup, head_pieces
+        plan, third, x, h, q, k, v, lse, inner, datt, dlog, code, turned, gsmall, gout, gup, head_pieces
     )
     if not staged:
         grads = plain_sum(plan, planes, lanes, me, at, ghead, gout, gup, gdown, glow)
         output = layer_output(counts, mid, hid, small, down)
         return output, input_grad(x, dmid, back, turned, small), grads
-    main = main_parts(main, my_plane)
-    parts = core_sum(packed[0][:, 0], packed[1][:, 0])
-    grad_tokens = input_grad(x, dmid, after(back, *parts), turned, small)
-    total = plane_sum(parts)
+    keep, send = (part[:, 0] for part in packed)
+    main = summed(all_after(main, keep))
+    picks = main_picks(main, my_plane)
+    parts = core_sum(keep, send)
+    grad_tokens = input_grad(x, dmid, after(back, *parts, *picks), turned, small)
+    total = summed(all_after(plane_swap(parts), grad_tokens))
     output = layer_output(counts, after(mid, total), hid, small, down)
     me = me.astype(jnp.int32).reshape(1)
-    return output, grad_tokens, take_owned(plan, at, me, main, head_parts(total))
+    owned = all_after([*main_parts(picks), *head_parts(total)], output)
+    return output, grad_tokens, take_owned(plan, at, me, owned[:PLANES], owned[PLANES:])
 
 
 def solution(mesh):

time: 258 us -> 203 us (0.79)
  Pallas kernels: 157 us -> 112 us
  waiting for transfers between devices: 48.5 us -> 31 us
  starting transfers between devices: 38.2 us -> 49.7 us
    pallas_call x3 -> x1, Pallas kernels: 70.8 us -> 45.8 us  [feed_forward(): pl.pallas_call(partial(feed_kernel, plan, gathered, len(wins), pieces), g...]
    ppermute x31 -> x42, waiting for transfers between devices: 48.5 us -> 31 us  [move(): return lax.ppermute(value, AXES, pairs)]
    ppermute x31 -> x42, starting transfers between devices: 38.2 us -> 49.7 us  [move(): return lax.ppermute(value, AXES, pairs)]
    pallas_call x1, Pallas kernels: 34.3 us -> 23.9 us  [attention_backward(): pl.pallas_call(partial(backward_kernel, pieces), grid_spec=pltpu.Prefetch...]
    pallas_call x2, Pallas kernels: 29.9 us -> 20.8 us  [attention_forward(): pl.pallas_call(kernel, grid_spec=pltpu.PrefetchScalarGridSpec(num_scalar_...]
  transfers between devices with their start and end apart: 31 -> 42, of which waited for: 11 -> 14; matrix products, arithmetic and copies ran while one was open for 1% -> 2% of each run, Pallas kernels for 25% -> 31%
where the time goes in v2:
time: 203 us
  Pallas kernels  112 us (55%)
  starting transfers between devices  49.7 us (24%)
  waiting for transfers between devices  31 us (15%)
  other arithmetic  5.42 us (3%)
  local copies, waits for them, and re-layouts  2.97 us (1%)
    ppermute x42, starting transfers between devices, move(): return lax.ppermute(value, AXES, pairs)  49.7 us
    pallas_call x1, Pallas kernels, feed_forward(): pl.pallas_call(partial(feed_kernel, plan, gathered, len(wins), pieces), g...  45.8 us
    ppermute x42, waiting for transfers between devices, move(): return lax.ppermute(value, AXES, pairs)  31 us
    pallas_call x1, Pallas kernels, attention_backward(): pl.pallas_call(partial(backward_kernel, pieces), grid_spec=pltpu.Prefetch...  23.9 us
    pallas_call x2, Pallas kernels, attention_forward(): pl.pallas_call(kernel, grid_spec=pltpu.PrefetchScalarGridSpec(num_scalar_...  20.8 us
    pallas_call x1, Pallas kernels, layer_output(): pl.pallas_call(output_kernel, grid_spec=pltpu.PrefetchScalarGridSpec(num_...  10.2 us
    pallas_call x1, Pallas kernels, input_grad(): pl.pallas_call(input_kernel, grid=(rows, length // TB), in_specs=[row_blo...  7.73 us
  transfers between devices with their start and end apart: 42, of which 14 were waited for; matrix products, arithmetic and copies ran while one was open for 2% of the time, Pallas kernels for 31%

profile of v2, /device:TPU:0, one launch (start us, length us, event | category | flops | bytes accessed | tf_op | source)
XLA Modules:
  0.0 202.8 jit_solution(8946385367016213483)
XLA Ops:
  0.7 1.7 shard_map.85.refs_0_.refs_6_
  2.4 4.0 %collective-permute-start.2 = (bf16[192,512]{1,0:T(8,128)(2,1)}, bf16[192,512]{1,0:T(8,128)(2,1)S(1)}, u32[]{:S(2)}, u32[]{:S(2)}) collective-permute-start(bf16[192,512]{1,0:T(8,128)(2,1)} %shard_map.85.refs_0_.refs_6_), channel_id=1, source_target_pairs={{0,16},{1,17},{2,18},{3,19},{4,20},{5,21},{6,22},{7,23},{8,24},{9,... | collective-permute-start | bytes 589832 | tf_op jit(solution)/shard_map/ppermute | solution.py:808
  8.0 2.7 %collective-permute-start.5 = (bf16[192,512]{1,0:T(8,128)(2,1)}, bf16[192,512]{1,0:T(8,128)(2,1)S(1)}, u32[]{:S(2)}, u32[]{:S(2)}) collective-permute-start(bf16[192,512]{1,0:T(8,128)(2,1)} %shard_map.85.refs_0_.refs_6_), channel_id=1, source_target_pairs={{0,6},{1,7},{2,4},{3,5},{4,2},{5,3},{6,0},{7,1},{8,14},{9,15},{10,... | collective-permute-start | bytes 589832 | tf_op jit(solution)/shard_map/ppermute | solution.py:808
  10.7 6.8 %collective-permute-done.2 = bf16[192,512]{1,0:T(8,128)(2,1)S(1)} collective-permute-done((bf16[192,512]{1,0:T(8,128)(2,1)}, bf16[192,512]{1,0:T(8,128)(2,1)S(1)}, u32[]{:S(2)}, u32[]{:S(2)}) %collective-permute-start.2) | collective-permute-done | bytes 196640 | tf_op jit(solution)/shard_map/ppermute | solution.py:808
  17.5 2.1 %collective-permute-start.4 = (bf16[192,512]{1,0:T(8,128)(2,1)}, bf16[192,512]{1,0:T(8,128)(2,1)S(1)}, u32[]{:S(2)}, u32[]{:S(2)}) collective-permute-start(bf16[192,512]{1,0:T(8,128)(2,1)} %shard_map.85.refs_0_.refs_6_), channel_id=1, source_target_pairs={{0,4},{1,5},{2,6},{3,7},{4,0},{5,1},{6,2},{7,3},{8,12},{9,13},{10,... | collective-permute-start | bytes 589832 | tf_op jit(solution)/shard_map/ppermute | solution.py:808
  22.8 2.5 %collective-permute-start.15 = (bf16[224,512]{1,0:T(8,128)(2,1)S(1)}, bf16[224,512]{1,0:T(8,128)(2,1)S(1)}, u32[]{:S(2)}, u32[]{:S(2)}) collective-permute-start(bf16[224,512]{1,0:T(8,128)(2,1)S(1)} %pad_maximum_fusion.1.refs_8_.refs_14_), channel_id=1, source_target_pairs={{0,6},{1,7},{2,4},{3,5},{4,2},{5,3},{6,0},{7,1},{8,14},{9,15},{10,... | collective-permute-start | bytes 688136 | tf_op jit(solution)/shard_map/ppermute | solution.py:808
  28.4 3.9 %collective-permute-done.15.refs_14_.refs_20_ = bf16[224,512]{1,0:T(8,128)(2,1)S(1)} collective-permute-done((bf16[224,512]{1,0:T(8,128)(2,1)S(1)}, bf16[224,512]{1,0:T(8,128)(2,1)S(1)}, u32[]{:S(2)}, u32[]{:S(2)}) %collective-permute-start.15) | collective-permute-done | bytes 229408 | tf_op jit(solution)/shard_map/ppermute | solution.py:808
  32.3 2.8 %collective-permute-done.13.refs_12_.refs_18_ = bf16[224,512]{1,0:T(8,128)(2,1)S(1)} collective-permute-done((bf16[224,512]{1,0:T(8,128)(2,1)S(1)}, bf16[224,512]{1,0:T(8,128)(2,1)S(1)}, u32[]{:S(2)}, u32[]{:S(2)}) %collective-permute-start.13) | collective-permute-done | bytes 229408 | tf_op jit(solution)/shard_map/ppermute | solution.py:808
  36.4 1.7 collective-permute-start.20
  42.1 11.2 %shard_map.86 = (bf16[2,512,1024]{2,1,0:T(8,128)(2,1)}, bf16[2,1024,64]{2,1,0:T(8,128)(2,1)}, bf16[2,1024,64]{2,1,0:T(8,128)(2,1)}, bf16[2,1024,512]{2,1,0:T(8,1...) custom-call(s32[2]{0:T(128)} %pad_add_fusion.place_ref, ...), custom_call_target="tpu_custom_call" | custom-call | flops 15399999488 | bytes 1400000 | tf_op jit(solution)/shard_map/pallas_call | solution.py:387
  53.3 3.2 %collective-permute-done.24.refs_30_ = bf16[192,512]{1,0:T(8,128)(2,1)S(1)} collective-permute-done((bf16[192,512]{1,0:T(8,128)(2,1)S(1)}, bf16[192,512]{1,0:T(8,128)(2,1)S(1)}, u32[]{:S(2)}, u32[]{:S(2)}) %collective-permute-start.24) | collective-permute-done | bytes 196640 | tf_op jit(solution)/shard_map/ppermute | solution.py:808
  57.8 9.6 %shard_map.87 = (bf16[2,512,1024]{2,1,0:T(8,128)(2,1)}, bf16[2,1024,64]{2,1,0:T(8,128)(2,1)}, bf16[2,1024,64]{2,1,0:T(8,128)(2,1)}, bf16[2,1024,512]{2,1,0:T(8,1...) custom-call(s32[2]{0:T(128)} %pad_add_fusion.place_ref, ...), custom_call_target="tpu_custom_call", output_to_operand_aliasing={{0}: (5, {}), {1}: (6, {}), {2}: (7, {}), {3}: (8, {}), {4}... | custom-call | flops 15399999488 | bytes 1400000 | tf_op jit(solution)/shard_map/pallas_call | solution.py:387
  68.6 45.8 %shard_map.88 = (bf16[2,1024,2048]{2,1,0:T(8,128)(2,1)}, f32[2,1024,512]{2,1,0:T(8,128)}, f32[2,1024,512]{2,1,0:T(8,128)}, bf16[2,512,1024]{2,1,0:T(8,128)(2,1)}...) custom-call(s32[2]{0:T(128)} %pad_add_fusion.place_ref, ...), custom_call_target="tpu_custom_call" | custom-call | flops 54999998464 | bytes 5000000 | tf_op jit(solution)/shard_map/pallas_call | solution.py:563
  114.7 4.5 %collective-permute-done.28 = bf16[4,3,192,512]{3,2,1,0:T(8,128)(2,1)S(1)} collective-permute-done((bf16[4,3,192,512]{3,2,1,0:T(8,128)(2,1)}, bf16[4,3,192,512]{3,2,1,0:T(8,128)(2,1)S(1)}, u32[]{:S(2)}, u32[]{:S(2)}) %collective-permute-start.28) | collective-permute-done | bytes 2359328 | tf_op jit(solution)/shard_map/ppermute | solution.py:808
  119.2 2.3 %fusion.3 = (bf16[3,192,512]{2,1,0:T(8,128)(2,1)S(1)}, bf16[3,192,512]{2,1,0:T(8,128)(2,1)S(1)}, bf16[3,192,512]{2,1,0:T(8,128)(2,1)S(1)}, bf16[3,192,512]{2,1,0:T(8,128)(2,1)S(1)}) fusion(bf16[4,3,192,512]{3,2,1,0:T(8,128)(2,1)S(1)} %collective-permute-done.28, bf16[4,3,192,512]{3,2,1,0:T(8,128)(2,1)} %get-tuple-element.67), kind=kLoop, calls=%fused_computation.8 | loop fusion | flops 4718592 | bytes 7077888 | tf_op jit(solution)/shard_map/convert_element_type | solution.py:906
  125.1 23.9 %shard_map.89 = (bf16[2,656,1024]{2,1,0:T(8,128)(2,1)}, bf16[640,512]{1,0:T(8,128)(2,1)}, bf16[32,512]{1,0:T(8,128)(2,1)}, bf16[4,1,224,512]{3,2,1,0:T(8,128)(2,1)}, bf16[4,1,224,512]{3,2,1,0:T(8,128)(2,1)}) custom-call(s32[2]{0:T(128)} %pad_add_fusion.place_ref, bf16[2,1024,512]{2,1,0:T(8,128)(2,1)} %x_ref.5, ...), custom_call_target="tpu_custom_call" | custom-call | flops 36300001280 | bytes 3300000 | tf_op jit(solution)/shard_map/pallas_call | solution.py:710
  149.1 1.6 collective-permute-done.34
  151.7 10.6 %collective-permute-start.38 = (bf16[192,512]{1,0:T(8,128)(2,1)S(1)}, bf16[192,512]{1,0:T(8,128)(2,1)S(1)}, u32[]{:S(2)}, u32[]{:S(2)}) collective-permute-start(bf16[192,512]{1,0:T(8,128)(2,1)S(1)} %get-tuple-element.113), channel_id=1, source_target_pairs={{0,24},{1,25},{2,26},{3,27},{4,28},{5,29},{6,30},{7,31},{8,16},{9,... | collective-permute-start | bytes 589832 | tf_op jit(solution)/shard_map/ppermute | solution.py:808
  162.4 3.0 %collective-permute-start.36 = (bf16[192,512]{1,0:T(8,128)(2,1)S(1)}, bf16[192,512]{1,0:T(8,128)(2,1)S(1)}, u32[]{:S(2)}, u32[]{:S(2)}) collective-permute-start(bf16[192,512]{1,0:T(8,128)(2,1)S(1)} %get-tuple-element.115), channel_id=1, source_target_pairs={{0,8},{1,9},{2,10},{3,11},{4,12},{5,13},{6,14},{7,15},{16,24},{17,... | collective-permute-start | bytes 589832 | tf_op jit(solution)/shard_map/ppermute | solution.py:808
  169.3 7.7 %shard_map.90 = bf16[2,1024,512]{2,1,0:T(8,128)(2,1)} custom-call(bf16[2,1024,512]{2,1,0:T(8,128)(2,1)} %x_ref.5, f32[2,1024,512]{2,1,0:T(8,128)} %get-tuple-element.83.dmid_ref, bf16[2,656,1024]{2,1,0:T(8,128)(2,1)} %get-tuple-element.89.back_ref, bf16[656,512]{1,0:T(8,128)(2,1)} %get-tuple-element.55.turned_ref.refs_10_, ...), custom_call_target="tpu_custom_call" | custom-call | flops 8800000000 | bytes 800000 | tf_op jit(solution)/shard_map/pallas_call | solution.py:762
  182.6 10.2 %shard_map.91 = bf16[2,1024,512]{2,1,0:T(8,128)(2,1)} custom-call(s32[2]{0:T(128)} %counts_ref.3, f32[2,1024,512]{2,1,0:T(8,128)} %get-tuple-element.94.mid_ref, bf16[2,1024,2048]{2,1,0:T(8,128)(2,1)} %get-tuple-element.95.hid_ref, f32[32,512]{1,0:T(8,128)} %get-tuple-element.56.small_ref.refs_5_, bf16[2048,512]{1,0:T(8,128)(2,1)} %get-tuple-element.96.down_ref), custom_call_target="tpu_custom_call" | custom-call | flops 9900000256 | bytes 900000 | tf_op jit(solution)/shard_map/pallas_call | solution.py:787
  192.8 2.1 %collective-permute-done.40.refs_6_ = bf16[224,512]{1,0:T(8,128)(2,1)S(1)} collective-permute-done((bf16[224,512]{1,0:T(8,128)(2,1)S(1)}, bf16[224,512]{1,0:T(8,128)(2,1)S(1)}, u32[]{:S(2)}, u32[]{:S(2)}) %collective-permute-start.40) | collective-permute-done | bytes 229408 | tf_op jit(solution)/shard_map/ppermute | solution.py:808
  194.9 4.8 %collective-permute-done.39.refs_5_ = bf16[224,512]{1,0:T(8,128)(2,1)S(1)} collective-permute-done((bf16[224,512]{1,0:T(8,128)(2,1)S(1)}, bf16[224,512]{1,0:T(8,128)(2,1)S(1)}, u32[]{:S(2)}, u32[]{:S(2)}) %collective-permute-start.39) | collective-permute-done | bytes 229408 | tf_op jit(solution)/shard_map/ppermute | solution.py:808
  200.5 2.4 %shard_map.92 = f32[659,128]{1,0:T(8,128)} custom-call(s32[1]{0:T(128)} %bitcast.2.at_ref, s32[1]{0:T(128)} %bitcast.23.me_ref, bf16[192,512]{1,0:T(8,128)(2,1)} %get-tuple-element.97.refs_0_, bf16[192,512]{1,0:T(8,128)(2,1)} %copy-done.8, bf16[192,512]{1,0:T(8,128)(2,1)} %copy-done.9, bf16[192,512]{1,0:T(8,128)(2,1)} %copy-done.7, ...), custom_call_target="tpu_custom_call" | custom-call | tf_op jit(solution)/shard_map/pallas_call | solution.py:979
  (155 shorter events, 30.4 us)
Async XLA Ops:
  2.4 15.1 %collective-permute-start.2 = (bf16[192,512]{1,0:T(8,128)(2,1)}, bf16[192,512]{1,0:T(8,128)(2,1)S(1)}, u32[]{:S(2)}, u32[]{:S(2)}) collective-permute-start(bf16[192,512]{1,0:T(8,128)(2,1)} %shard_map.85.refs_0_.refs_6_), channel_id=1, source_target_pairs={{0,16},{1,17},{2,18},{3,19},{4,20},{5,21},{6,22},{7,23},{8,24},{9,... | collective-permute-start | bytes 589832 | tf_op jit(solution)/shard_map/ppermute | solution.py:808
  6.4 13.1 %collective-permute-start.1 = (bf16[192,512]{1,0:T(8,128)(2,1)}, bf16[192,512]{1,0:T(8,128)(2,1)S(1)}, u32[]{:S(2)}, u32[]{:S(2)}) collective-permute-start(bf16[192,512]{1,0:T(8,128)(2,1)} %shard_map.85.refs_0_.refs_6_), channel_id=1, source_target_pairs={{0,8},{1,9},{2,10},{3,11},{4,12},{5,13},{6,14},{7,15},{8,0},{9,1},... | collective-permute-start | bytes 589832 | tf_op jit(solution)/shard_map/ppermute | solution.py:808
  8.0 13.2 %collective-permute-start = (bf16[192,512]{1,0:T(8,128)(2,1)}, bf16[192,512]{1,0:T(8,128)(2,1)S(1)}, u32[]{:S(2)}, u32[]{:S(2)}) collective-permute-start(bf16[192,512]{1,0:T(8,128)(2,1)} %shard_map.85.refs_0_.refs_6_), channel_id=1, source_target_pairs={{0,24},{1,25},{2,26},{3,27},{4,28},{5,29},{6,30},{7,31},{8,16},{9,... | collective-permute-start | bytes 589832 | tf_op jit(solution)/shard_map/ppermute | solution.py:808
  8.0 17.3 %collective-permute-start.6 = (bf16[192,512]{1,0:T(8,128)(2,1)}, bf16[192,512]{1,0:T(8,128)(2,1)S(1)}, u32[]{:S(2)}, u32[]{:S(2)}) collective-permute-start(bf16[192,512]{1,0:T(8,128)(2,1)} %shard_map.85.refs_0_.refs_6_), channel_id=1, source_target_pairs={{0,1},{1,0},{2,3},{3,2},{4,5},{5,4},{6,7},{7,6},{8,9},{9,8},{10,11... | collective-permute-start | bytes 589832 | tf_op jit(solution)/shard_map/ppermute | solution.py:808
  8.0 14.0 %collective-permute-start.5 = (bf16[192,512]{1,0:T(8,128)(2,1)}, bf16[192,512]{1,0:T(8,128)(2,1)S(1)}, u32[]{:S(2)}, u32[]{:S(2)}) collective-permute-start(bf16[192,512]{1,0:T(8,128)(2,1)} %shard_map.85.refs_0_.refs_6_), channel_id=1, source_target_pairs={{0,6},{1,7},{2,4},{3,5},{4,2},{5,3},{6,0},{7,1},{8,14},{9,15},{10,... | collective-permute-start | bytes 589832 | tf_op jit(solution)/shard_map/ppermute | solution.py:808
  36.4 20.9 %collective-permute-start.20 = (bf16[2,192,512]{2,1,0:T(8,128)(2,1)S(1)}, bf16[2,192,512]{2,1,0:T(8,128)(2,1)S(1)}, u32[]{:S(2)}, u32[]{:S(2)}) collective-permute-start(bf16[2,192,512]{2,1,0:T(8,128)(2,1)S(1)} %pad_maximum_fusion.refs_22_), channel_id=1, source_target_pairs={{0,4},{1,5},{2,6},{3,7},{4,0},{5,1},{6,2},{7,3},{8,12},{9,13},{10,... | collective-permute-start | bytes 1179656 | tf_op jit(solution)/shard_map/ppermute | solution.py:808
  38.1 19.5 %collective-permute-start.18 = (bf16[2,192,512]{2,1,0:T(8,128)(2,1)S(1)}, bf16[2,192,512]{2,1,0:T(8,128)(2,1)S(1)}, u32[]{:S(2)}, u32[]{:S(2)}) collective-permute-start(bf16[2,192,512]{2,1,0:T(8,128)(2,1)S(1)} %pad_maximum_fusion.refs_22_), channel_id=1, source_target_pairs={{0,2},{1,3},{2,0},{3,1},{4,6},{5,7},{6,4},{7,5},{8,10},{9,11},{10,... | collective-permute-start | bytes 1179656 | tf_op jit(solution)/shard_map/ppermute | solution.py:808
  38.7 17.7 %collective-permute-start.24 = (bf16[192,512]{1,0:T(8,128)(2,1)S(1)}, bf16[192,512]{1,0:T(8,128)(2,1)S(1)}, u32[]{:S(2)}, u32[]{:S(2)}) collective-permute-start(bf16[192,512]{1,0:T(8,128)(2,1)S(1)} %collective-permute-done.5.refs_6_.refs_12_), channel_id=1, source_target_pairs={{16,0},{17,1},{18,2},{19,3},{20,4},{21,5},{22,6},{23,7},{24,8},{25... | collective-permute-start | bytes 589832 | tf_op jit(solution)/shard_map/ppermute | solution.py:808
  40.1 16.7 %collective-permute-start.22 = (bf16[192,512]{1,0:T(8,128)(2,1)S(1)}, bf16[192,512]{1,0:T(8,128)(2,1)S(1)}, u32[]{:S(2)}, u32[]{:S(2)}) collective-permute-start(bf16[192,512]{1,0:T(8,128)(2,1)S(1)} %collective-permute-done.5.refs_6_.refs_12_), channel_id=1, source_target_pairs={{8,0},{9,1},{10,2},{11,3},{12,4},{13,5},{14,6},{15,7},{24,16},{25,... | collective-permute-start | bytes 589832 | tf_op jit(solution)/shard_map/ppermute | solution.py:808
  41.4 15.6 %collective-permute-start.27 = (bf16[192,512]{1,0:T(8,128)(2,1)S(1)}, bf16[192,512]{1,0:T(8,128)(2,1)S(1)}, u32[]{:S(2)}, u32[]{:S(2)}) collective-permute-start(bf16[192,512]{1,0:T(8,128)(2,1)S(1)} %collective-permute-done.26.refs_32_), channel_id=1, source_target_pairs={{0,1},{1,0},{2,3},{3,2},{4,5},{5,4},{6,7},{7,6},{8,9},{9,8},{10,11... | collective-permute-start | bytes 589832 | tf_op jit(solution)/shard_map/ppermute | solution.py:808
  56.5 11.0 %collective-permute-start.17 = (bf16[2,192,512]{2,1,0:T(8,128)(2,1)S(1)}, bf16[2,192,512]{2,1,0:T(8,128)(2,1)S(1)}, u32[]{:S(2)}, u32[]{:S(2)}) collective-permute-start(bf16[2,192,512]{2,1,0:T(8,128)(2,1)S(1)} %pad_maximum_fusion.refs_22_), channel_id=1, source_target_pairs={{0,1},{1,0},{2,3},{3,2},{4,5},{5,4},{6,7},{7,6},{8,9},{9,8},{10,11... | collective-permute-start | bytes 1179656 | tf_op jit(solution)/shard_map/ppermute | solution.py:808
  56.8 10.7 %collective-permute-start.25 = (bf16[192,512]{1,0:T(8,128)(2,1)S(1)}, bf16[192,512]{1,0:T(8,128)(2,1)S(1)}, u32[]{:S(2)}, u32[]{:S(2)}) collective-permute-start(bf16[192,512]{1,0:T(8,128)(2,1)S(1)} %collective-permute-done.24.refs_30_), channel_id=1, source_target_pairs={{0,1},{1,0},{2,3},{3,2},{4,5},{5,4},{6,7},{7,6},{8,9},{9,8},{10,11... | collective-permute-start | bytes 589832 | tf_op jit(solution)/shard_map/ppermute | solution.py:808
  121.5 27.5 %collective-permute-start.35 = (bf16[3,192,512]{2,1,0:T(8,128)(2,1)S(1)}, bf16[3,192,512]{2,1,0:T(8,128)(2,1)S(1)}, u32[]{:S(2)}, u32[]{:S(2)}) collective-permute-start(bf16[3,192,512]{2,1,0:T(8,128)(2,1)S(1)} %get-tuple-element.105), channel_id=1, source_target_pairs={{0,6},{1,7},{2,4},{3,5},{4,2},{5,3},{6,0},{7,1},{8,14},{9,15},{10,... | collective-permute-start | bytes 1769480 | tf_op jit(solution)/shard_map/ppermute | solution.py:808
  122.8 27.9 %collective-permute-start.34 = (bf16[3,192,512]{2,1,0:T(8,128)(2,1)S(1)}, bf16[3,192,512]{2,1,0:T(8,128)(2,1)S(1)}, u32[]{:S(2)}, u32[]{:S(2)}) collective-permute-start(bf16[3,192,512]{2,1,0:T(8,128)(2,1)S(1)} %get-tuple-element.106), channel_id=1, source_target_pairs={{0,4},{1,5},{2,6},{3,7},{4,0},{5,1},{6,2},{7,3},{8,12},{9,13},{10,... | collective-permute-start | bytes 1769480 | tf_op jit(solution)/shard_map/ppermute | solution.py:808
  124.3 26.3 %collective-permute-start.33 = (bf16[3,192,512]{2,1,0:T(8,128)(2,1)S(1)}, bf16[3,192,512]{2,1,0:T(8,128)(2,1)S(1)}, u32[]{:S(2)}, u32[]{:S(2)}) collective-permute-start(bf16[3,192,512]{2,1,0:T(8,128)(2,1)S(1)} %get-tuple-element.107), channel_id=1, source_target_pairs={{0,2},{1,3},{2,0},{3,1},{4,6},{5,7},{6,4},{7,5},{8,10},{9,11},{10,... | collective-permute-start | bytes 1769480 | tf_op jit(solution)/shard_map/ppermute | solution.py:808
  149.0 16.4 %collective-permute-start.29 = (bf16[4,224,512]{2,1,0:T(8,128)(2,1)}, bf16[4,224,512]{2,1,0:T(8,128)(2,1)S(1)}, u32[]{:S(2)}, u32[]{:S(2)}) collective-permute-start(bf16[4,224,512]{2,1,0:T(8,128)(2,1)} %bitcast.84), channel_id=1, source_target_pairs={{0,1},{1,0},{2,3},{3,2},{4,5},{5,4},{6,7},{7,6},{8,9},{9,8},{10,11... | collective-permute-start | bytes 2752520 | tf_op jit(solution)/shard_map/ppermute | solution.py:808
  151.7 29.6 %collective-permute-start.38 = (bf16[192,512]{1,0:T(8,128)(2,1)S(1)}, bf16[192,512]{1,0:T(8,128)(2,1)S(1)}, u32[]{:S(2)}, u32[]{:S(2)}) collective-permute-start(bf16[192,512]{1,0:T(8,128)(2,1)S(1)} %get-tuple-element.113), channel_id=1, source_target_pairs={{0,24},{1,25},{2,26},{3,27},{4,28},{5,29},{6,30},{7,31},{8,16},{9,... | collective-permute-start | bytes 589832 | tf_op jit(solution)/shard_map/ppermute | solution.py:808
  162.4 30.4 %collective-permute-start.36 = (bf16[192,512]{1,0:T(8,128)(2,1)S(1)}, bf16[192,512]{1,0:T(8,128)(2,1)S(1)}, u32[]{:S(2)}, u32[]{:S(2)}) collective-permute-start(bf16[192,512]{1,0:T(8,128)(2,1)S(1)} %get-tuple-element.115), channel_id=1, source_target_pairs={{0,8},{1,9},{2,10},{3,11},{4,12},{5,13},{6,14},{7,15},{16,24},{17,... | collective-permute-start | bytes 589832 | tf_op jit(solution)/shard_map/ppermute | solution.py:808
  165.7 11.3 %collective-permute-start.32 = (bf16[224,512]{1,0:T(8,128)(2,1)S(1)}, bf16[224,512]{1,0:T(8,128)(2,1)S(1)}, u32[]{:S(2)}, u32[]{:S(2)}) collective-permute-start(bf16[224,512]{1,0:T(8,128)(2,1)S(1)} %get-tuple-element.109), channel_id=1, source_target_pairs={{0,6},{1,7},{2,4},{3,5},{4,2},{5,3},{6,0},{7,1},{8,14},{9,15},{10,... | collective-permute-start | bytes 688136 | tf_op jit(solution)/shard_map/ppermute | solution.py:808
  167.1 11.5 %collective-permute-start.31 = (bf16[224,512]{1,0:T(8,128)(2,1)S(1)}, bf16[224,512]{1,0:T(8,128)(2,1)S(1)}, u32[]{:S(2)}, u32[]{:S(2)}) collective-permute-start(bf16[224,512]{1,0:T(8,128)(2,1)S(1)} %get-tuple-element.110), channel_id=1, source_target_pairs={{0,4},{1,5},{2,6},{3,7},{4,0},{5,1},{6,2},{7,3},{8,12},{9,13},{10,... | collective-permute-start | bytes 688136 | tf_op jit(solution)/shard_map/ppermute | solution.py:808
  177.0 15.8 %collective-permute-start.37 = (bf16[192,512]{1,0:T(8,128)(2,1)S(1)}, bf16[192,512]{1,0:T(8,128)(2,1)S(1)}, u32[]{:S(2)}, u32[]{:S(2)}) collective-permute-start(bf16[192,512]{1,0:T(8,128)(2,1)S(1)} %get-tuple-element.116), channel_id=1, source_target_pairs={{0,16},{1,17},{2,18},{3,19},{4,20},{5,21},{6,22},{7,23},{8,24},{9,... | collective-permute-start | bytes 589832 | tf_op jit(solution)/shard_map/ppermute | solution.py:808
  178.7 14.1 %collective-permute-start.41 = (bf16[224,512]{1,0:T(8,128)(2,1)S(1)}, bf16[224,512]{1,0:T(8,128)(2,1)S(1)}, u32[]{:S(2)}, u32[]{:S(2)}) collective-permute-start(bf16[224,512]{1,0:T(8,128)(2,1)S(1)} %add_convert_fusion.5.refs_4_), channel_id=1, source_target_pairs={{24,0},{25,1},{26,2},{27,3},{28,4},{29,5},{30,6},{31,7},{23,31}} | collective-permute-start | bytes 688136 | tf_op jit(solution)/shard_map/ppermute | solution.py:808
  180.0 14.9 %collective-permute-start.40 = (bf16[224,512]{1,0:T(8,128)(2,1)S(1)}, bf16[224,512]{1,0:T(8,128)(2,1)S(1)}, u32[]{:S(2)}, u32[]{:S(2)}) collective-permute-start(bf16[224,512]{1,0:T(8,128)(2,1)S(1)} %add_convert_fusion.5.refs_4_), channel_id=1, source_target_pairs={{16,0},{17,1},{18,2},{19,3},{20,4},{21,5},{22,6},{23,7},{15,31}} | collective-permute-start | bytes 688136 | tf_op jit(solution)/shard_map/ppermute | solution.py:808
  181.3 18.4 %collective-permute-start.39 = (bf16[224,512]{1,0:T(8,128)(2,1)S(1)}, bf16[224,512]{1,0:T(8,128)(2,1)S(1)}, u32[]{:S(2)}, u32[]{:S(2)}) collective-permute-start(bf16[224,512]{1,0:T(8,128)(2,1)S(1)} %add_convert_fusion.5.refs_4_), channel_id=1, source_target_pairs={{8,0},{9,1},{10,2},{11,3},{12,4},{13,5},{14,6},{15,7},{7,31}} | collective-permute-start | bytes 688136 | tf_op jit(solution)/shard_map/ppermute | solution.py:808
  (55 other events, 504.9 us)

commit v3 on v2

--- a/solution.py
+++ b/solution.py
@@ -444,7 +444,7 @@
     wins = refs[6 : 6 + count]
     hid_ref, mid_ref, dmid_ref, datt_ref, dlog_ref, inner_ref = refs[6 + count : 12 + count]
     down_ref, gout_ref, gsmall_ref, gup_ref, gdown_ref = refs[12 + count : 17 + count]
-    packed = refs[17 + count : -12]
+    packed, bias_ref = refs[17 + count : -13], refs[-13]
     rows_ref, up_ref, flat_ref, tmp_ref, tmp2_ref, wide_ref = refs[-12:-6]
     tdown_ref, tup_ref, tout_ref, sem, sem2, pack_sem = refs[-6:]
 
@@ -521,8 +521,10 @@
     @pl.when(last_step())
     def _():
         gdown_ref[...] = tdown_ref[...].astype(BF16)
+        bias_ref[...] = jnp.concatenate([gsmall_ref[6:7, :], jnp.zeros((15, D), F32)]).astype(BF16)
+        ins = [flat_ref, gdown_ref, bias_ref]
         if pieces:
-            pack_start(pieces, [1], place_ref, [flat_ref, gdown_ref], packed, pack_sem)
+            pack_start(pieces, [1, 2], place_ref, ins, packed, pack_sem)
         gout_ref[...] = tout_ref[...].astype(BF16)
         for c in range(4):
             for j in range(4):
@@ -532,7 +534,7 @@
             flat_ref[:, 128 * c : 128 * (c + 1)] = wide_ref[c].astype(BF16)
         gup_ref[...] = flat_ref[0 : gup_ref.shape[0], :]
         if pieces:
-            pack_start(pieces, [0], place_ref, [flat_ref, gdown_ref], packed, pack_sem)
+            pack_start(pieces, [0], place_ref, ins, packed, pack_sem)
             pack_end(packed, pack_sem)
 
 
@@ -589,6 +591,7 @@
             ]
             + [ANYWHERE] * len(packed),
             scratch_shapes=[
+                pltpu.VMEM((16, D), BF16),
                 pltpu.VMEM((ROW_D - ROW_O, D), BF16),
                 pltpu.VMEM((D, FF), BF16),
                 pltpu.VMEM((FF, D), BF16),
@@ -705,7 +708,7 @@
 ):
     rows, length = x.shape[0], x.shape[1]
     row3 = lambda a, b: pl.BlockSpec((1, a, b), lambda i, *_: (i, 0, 0))
-    packed = [kind(BF16, LANES // 2, 1, plan.rows + SMALL, D)] * 2 if pieces else []
+    packed = [kind(BF16, LANES // 2, 1, plan.rows, D)] * 2 if pieces else []
     head = min(LATE_ROWS, gup.shape[0])
     return pl.pallas_call(
         partial(backward_kernel, pieces),
@@ -838,13 +841,14 @@
         pairs = [(z * LANES + f, (z ^ s) * LANES + f) for z in range(PLANES) for f in range(LANES)]
         got.append(move(window, pairs))
     own = [window] + [across(window, bits) for bits in (2, 4, 6)]
+    got[1:], corner = all_after(got[1:], own[3]), own[3]
     of = lambda f: by_plane([got[f(mine) ^ mine] for mine in range(PLANES)], my_plane)
     low = ROW_S - 16 * plan.first(ALL - 1)
     last = of(lambda mine: PLANES - 1)
     head = jnp.concatenate([of(early_plane), last[low : low + SMALL]], axis=0)
     rest = jnp.stack([of(lambda mine: late_planes(mine)[0]), of(lambda mine: late_planes(mine)[1])])
     head = [head] + [across(head, bits) for bits in (2, 4, 6)]
-    ready = [rest, *own]
+    ready = [rest]
     rest = [rest] + [across(rest, bits) for bits in (2, 4)]
     diag = []
     for s in range(1, PLANES):
@@ -854,7 +858,8 @@
             if z ^ s in late_planes(z)
             for f in range(LANES)
         ]
-        diag.append(move(own[3], pairs))
+        diag.append(move(corner, pairs))
+    ready += diag[:1]
     spread = [core_spread(part) for part in (own, head, rest, diag)]
     return Gathered(plan, None, *spread), ready
 
@@ -882,22 +887,32 @@
         pltpu.make_async_copy(packed[i], packed[i], sem.at[i]).wait()
 
 
-def window_pieces(plan, windows, spans, extra):
+SMALL_AT = 176
+
+
+def window_pieces(plan, windows, spans, small):
     pieces = []
     for d in windows:
         plane, lane = divmod(d, LANES)
         plane = plane - windows[0] // LANES
-        begin = 16 * plan.first(d)
-        for source, (low, high) in enumerate(spans):
-            a, b = max(begin, low), min(begin + plan.rows, high)
+        begin, size = 16 * plan.first(d), plan.rows
+        if small and lane == LANES - 1:
+            size = SMALL_AT
+            pieces.append((len(spans), 0, 16, plane, lane, SMALL_AT))
+        done = begin
+        for source, (low, high) in enumerate(spans + [(begin + size, begin + size)]):
+            a, b = max(begin, low), min(begin + size, high)
+            if a > done and a >= high or a < b and a > done:
+                pieces.append((0, 0, a - done, plane, lane, done - begin))
             if a < b:
                 pieces.append((source, a - low, b - a, plane, lane, a - begin))
-        end = spans[-1][1]
-        if begin + plan.rows > end:
-            left = begin + plan.rows - end
-            pieces.append((len(spans) - 1, 0, left, plane, lane, plan.rows - left))
-        if extra:
-            pieces.append((len(spans), 0, SMALL, plane, lane, plan.rows))
+            done = max(done, min(max(a, b), begin + size))
+    for d in windows:
+        plane, lane = divmod(d, LANES)
+        plane = plane - windows[0] // LANES
+        rows = sorted((p[5], p[5] + p[2]) for p in pieces if p[3:5] == (plane, lane))
+        assert rows[0][0] == 0 and rows[-1][1] == plan.rows
+        assert all(x[1] == y[0] for x, y in zip(rows, rows[1:]))
     return pieces
 
 
@@ -924,7 +939,7 @@
     ]
 
 
-def main_parts(picks):
+def to_planes(picks):
     out = [picks[0]]
     for s in range(1, PLANES):
         pairs = [
@@ -968,7 +983,7 @@
     @pl.when(me_ref[0] == ALL - 1)
     def _():
         low = ROW_S - 16 * plan.first(ALL - 1)
-        sum_ref[low : low + SMALL, :] = add(head, plan.rows, plan.rows + SMALL)
+        sum_ref[low : low + 16, :] = add(head, SMALL_AT, SMALL_AT + 16)
 
     for j in range(4):
         pad_ref[pl.ds(j, plan.rows, stride=4), :] = sum_ref[:, 128 * j : 128 * (j + 1)]
@@ -981,7 +996,7 @@
         grid_spec=pltpu.PrefetchScalarGridSpec(
             num_scalar_prefetch=2,
             grid=(1,),
-            in_specs=[whole(plan.rows, D)] * PLANES + [whole(plan.rows + SMALL, D)] * PLANES,
+            in_specs=[whole(plan.rows, D)] * (2 * PLANES),
             out_specs=whole(plan.lanes, 128),
             scratch_shapes=[
                 pltpu.VMEM((plan.rows, D), F32),
@@ -1019,7 +1034,7 @@
         gathered, ready = gather_staged(plan, window, my_plane)
         first = after(place, *ready)
         main_pieces = window_pieces(
-            plan, range(LANES, ALL), [(ROW_U, ROW_D), (ROW_D, ROW_S)], False
+            plan, range(LANES, ALL), [(ROW_U, ROW_D), (ROW_D, ROW_S), (ROW_S + 16, ROWS_ALL)], False
         )
         head_pieces = window_pieces(
             plan, range(LANES), [(0, ROW_O), (ROW_O, ROW_U), (ROW_U, ROW_U + LATE_ROWS)], True
@@ -1060,7 +1075,7 @@
     total = summed(all_after(plane_swap(parts), grad_tokens))
     output = layer_output(counts, after(mid, total), hid, small, down)
     me = me.astype(jnp.int32).reshape(1)
-    owned = all_after([*main_parts(picks), *head_parts(total)], output)
+    owned = all_after([*to_planes(picks), *head_parts(total)], output)
     return output, grad_tokens, take_owned(plan, at, me, owned[:PLANES], owned[PLANES:])
 
 

time: 203 us -> 196 us (0.966)
  starting transfers between devices: 49.7 us -> 43.5 us
    ppermute x42, starting transfers between devices: 49.7 us -> 43.5 us  [move(): return lax.ppermute(value, AXES, pairs)]
  transfers between devices with their start and end apart: 42 -> 42, of which waited for: 14 -> 9; matrix products, arithmetic and copies ran while one was open for 2% -> 2% of each run, Pallas kernels for 31% -> 32%
where the time goes in v3:
time: 196 us; the launch traced here: 195 us
  Pallas kernels  112 us (57%)
  starting transfers between devices  43.5 us (22%)
  waiting for transfers between devices  30.3 us (15%)
  other arithmetic  5.36 us (3%)
  local copies, waits for them, and re-layouts  2.51 us (1%)
    pallas_call x1, Pallas kernels, feed_forward(): pl.pallas_call(partial(feed_kernel, plan, gathered, len(wins), pieces), g...  45.8 us
    ppermute x42, starting transfers between devices, move(): return lax.ppermute(value, AXES, pairs)  43.5 us
    ppermute x42, waiting for transfers between devices, move(): return lax.ppermute(value, AXES, pairs)  30.3 us
    pallas_call x1, Pallas kernels, attention_backward(): pl.pallas_call(partial(backward_kernel, pieces), grid_spec=pltpu.Prefetch...  23.8 us
    pallas_call x2, Pallas kernels, attention_forward(): pl.pallas_call(kernel, grid_spec=pltpu.PrefetchScalarGridSpec(num_scalar_...  20.8 us
    pallas_call x1, Pallas kernels, layer_output(): pl.pallas_call(output_kernel, grid_spec=pltpu.PrefetchScalarGridSpec(num_...  10.2 us
    pallas_call x1, Pallas kernels, input_grad(): pl.pallas_call(input_kernel, grid=(rows, length // TB), in_specs=[row_blo...  7.72 us
  transfers between devices with their start and end apart: 42, of which 9 were waited for; matrix products, arithmetic and copies ran while one was open for 2% of the time, Pallas kernels for 32%

profile of v3, /device:TPU:0, one launch (start us, length us, event | category | flops | bytes accessed | tf_op | source)
XLA Modules:
  0.0 195.4 jit_solution(15155444044449558592)
XLA Ops:
  0.7 1.7 shard_map.85.refs_0_.refs_6_
  2.4 3.9 %collective-permute-start.3 = (bf16[192,512]{1,0:T(8,128)(2,1)}, bf16[192,512]{1,0:T(8,128)(2,1)S(1)}, u32[]{:S(2)}, u32[]{:S(2)}) collective-permute-start(bf16[192,512]{1,0:T(8,128)(2,1)} %shard_map.85.refs_0_.refs_6_), channel_id=1, source_target_pairs={{0,6},{1,7},{2,4},{3,5},{4,2},{5,3},{6,0},{7,1},{8,14},{9,15},{10,... | collective-permute-start | bytes 589832 | tf_op jit(solution)/shard_map/ppermute | solution.py:811
  6.3 3.6 %collective-permute-start.2 = (bf16[192,512]{1,0:T(8,128)(2,1)}, bf16[192,512]{1,0:T(8,128)(2,1)S(1)}, u32[]{:S(2)}, u32[]{:S(2)}) collective-permute-start(bf16[192,512]{1,0:T(8,128)(2,1)} %shard_map.85.refs_0_.refs_6_), channel_id=1, source_target_pairs={{0,24},{1,25},{2,26},{3,27},{4,28},{5,29},{6,30},{7,31},{8,16},{9,... | collective-permute-start | bytes 589832 | tf_op jit(solution)/shard_map/ppermute | solution.py:811
  11.4 1.7 collective-permute-start.6
  13.1 3.1 %collective-permute-done.2 = bf16[192,512]{1,0:T(8,128)(2,1)S(1)} collective-permute-done((bf16[192,512]{1,0:T(8,128)(2,1)}, bf16[192,512]{1,0:T(8,128)(2,1)S(1)}, u32[]{:S(2)}, u32[]{:S(2)}) %collective-permute-start.2) | collective-permute-done | bytes 196640 | tf_op jit(solution)/shard_map/ppermute | solution.py:811
  16.2 10.3 %collective-permute-done.1 = bf16[192,512]{1,0:T(8,128)(2,1)S(1)} collective-permute-done((bf16[192,512]{1,0:T(8,128)(2,1)}, bf16[192,512]{1,0:T(8,128)(2,1)S(1)}, u32[]{:S(2)}, u32[]{:S(2)}) %collective-permute-start.1) | collective-permute-done | bytes 196640 | tf_op jit(solution)/shard_map/ppermute | solution.py:811
  28.5 1.5 collective-permute-start.14
  34.3 5.9 %collective-permute-done.4.refs_28_ = bf16[192,512]{1,0:T(8,128)(2,1)S(1)} collective-permute-done((bf16[192,512]{1,0:T(8,128)(2,1)S(1)}, bf16[192,512]{1,0:T(8,128)(2,1)S(1)}, u32[]{:S(2)}, u32[]{:S(2)}) %collective-permute-start.4) | collective-permute-done | bytes 196640 | tf_op jit(solution)/shard_map/ppermute | solution.py:811
  45.9 11.2 %shard_map.86 = (bf16[2,512,1024]{2,1,0:T(8,128)(2,1)}, bf16[2,1024,64]{2,1,0:T(8,128)(2,1)}, bf16[2,1024,64]{2,1,0:T(8,128)(2,1)}, bf16[2,1024,512]{2,1,0:T(8,1...) custom-call(s32[2]{0:T(128)} %pad_add_fusion.place_ref, ...), custom_call_target="tpu_custom_call" | custom-call | flops 15399999488 | bytes 1400000 | tf_op jit(solution)/shard_map/pallas_call | solution.py:387
  59.1 9.6 %shard_map.87 = (bf16[2,512,1024]{2,1,0:T(8,128)(2,1)}, bf16[2,1024,64]{2,1,0:T(8,128)(2,1)}, bf16[2,1024,64]{2,1,0:T(8,128)(2,1)}, bf16[2,1024,512]{2,1,0:T(8,1...) custom-call(s32[2]{0:T(128)} %pad_add_fusion.place_ref, ...), custom_call_target="tpu_custom_call", output_to_operand_aliasing={{0}: (5, {}), {1}: (6, {}), {2}: (7, {}), {3}: (8, {}), {4}... | custom-call | flops 15399999488 | bytes 1400000 | tf_op jit(solution)/shard_map/pallas_call | solution.py:387
  69.9 45.8 %shard_map.88 = (bf16[2,1024,2048]{2,1,0:T(8,128)(2,1)}, f32[2,1024,512]{2,1,0:T(8,128)}, f32[2,1024,512]{2,1,0:T(8,128)}, bf16[2,512,1024]{2,1,0:T(8,128)(2,1)}...) custom-call(s32[2]{0:T(128)} %pad_add_fusion.place_ref, ...), custom_call_target="tpu_custom_call" | custom-call | flops 54999998464 | bytes 5000000 | tf_op jit(solution)/shard_map/pallas_call | solution.py:565
  115.8 4.7 %collective-permute-done.28 = bf16[4,3,192,512]{3,2,1,0:T(8,128)(2,1)S(1)} collective-permute-done((bf16[4,3,192,512]{3,2,1,0:T(8,128)(2,1)}, bf16[4,3,192,512]{3,2,1,0:T(8,128)(2,1)S(1)}, u32[]{:S(2)}, u32[]{:S(2)}) %collective-permute-start.28) | collective-permute-done | bytes 2359328 | tf_op jit(solution)/shard_map/ppermute | solution.py:811
  120.5 2.3 %fusion.3 = (bf16[3,192,512]{2,1,0:T(8,128)(2,1)S(1)}, bf16[3,192,512]{2,1,0:T(8,128)(2,1)S(1)}, bf16[3,192,512]{2,1,0:T(8,128)(2,1)S(1)}, bf16[3,192,512]{2,1,0:T(8,128)(2,1)S(1)}) fusion(bf16[4,3,192,512]{3,2,1,0:T(8,128)(2,1)S(1)} %collective-permute-done.28, bf16[4,3,192,512]{3,2,1,0:T(8,128)(2,1)} %get-tuple-element.73), kind=kLoop, calls=%fused_computation.8 | loop fusion | flops 4718592 | bytes 7077888 | tf_op jit(solution)/shard_map/convert_element_type | solution.py:921
  122.8 1.8 collective-permute-start.35
  126.4 23.8 %shard_map.89 = (bf16[2,656,1024]{2,1,0:T(8,128)(2,1)}, bf16[640,512]{1,0:T(8,128)(2,1)}, bf16[32,512]{1,0:T(8,128)(2,1)}, bf16[4,1,192,512]{3,2,1,0:T(8,128)(2,1)}, bf16[4,1,192,512]{3,2,1,0:T(8,128)(2,1)}) custom-call(s32[2]{0:T(128)} %pad_add_fusion.place_ref, bf16[2,1024,512]{2,1,0:T(8,128)(2,1)} %x_ref.5, ...), custom_call_target="tpu_custom_call" | custom-call | flops 36300001280 | bytes 3300000 | tf_op jit(solution)/shard_map/pallas_call | solution.py:713
  150.3 1.5 collective-permute-done.34
  153.0 4.6 %collective-permute-start.38 = (bf16[192,512]{1,0:T(8,128)(2,1)S(1)}, bf16[192,512]{1,0:T(8,128)(2,1)S(1)}, u32[]{:S(2)}, u32[]{:S(2)}) collective-permute-start(bf16[192,512]{1,0:T(8,128)(2,1)S(1)} %get-tuple-element.119), channel_id=1, source_target_pairs={{0,24},{1,25},{2,26},{3,27},{4,28},{5,29},{6,30},{7,31},{8,16},{9,... | collective-permute-start | bytes 589832 | tf_op jit(solution)/shard_map/ppermute | solution.py:811
  157.6 2.6 %collective-permute-start.36 = (bf16[192,512]{1,0:T(8,128)(2,1)S(1)}, bf16[192,512]{1,0:T(8,128)(2,1)S(1)}, u32[]{:S(2)}, u32[]{:S(2)}) collective-permute-start(bf16[192,512]{1,0:T(8,128)(2,1)S(1)} %get-tuple-element.121), channel_id=1, source_target_pairs={{0,8},{1,9},{2,10},{3,11},{4,12},{5,13},{6,14},{7,15},{16,24},{17,... | collective-permute-start | bytes 589832 | tf_op jit(solution)/shard_map/ppermute | solution.py:811
  160.4 1.7 collective-permute-start.32
  164.0 7.7 %shard_map.90 = bf16[2,1024,512]{2,1,0:T(8,128)(2,1)} custom-call(bf16[2,1024,512]{2,1,0:T(8,128)(2,1)} %x_ref.5, f32[2,1024,512]{2,1,0:T(8,128)} %get-tuple-element.89.dmid_ref, bf16[2,656,1024]{2,1,0:T(8,128)(2,1)} %get-tuple-element.95.back_ref, bf16[656,512]{1,0:T(8,128)(2,1)} %get-tuple-element.61.turned_ref.refs_10_, ...), custom_call_target="tpu_custom_call" | custom-call | flops 8800000000 | bytes 800000 | tf_op jit(solution)/shard_map/pallas_call | solution.py:765
  171.7 2.9 %collective-permute-start.37 = (bf16[192,512]{1,0:T(8,128)(2,1)S(1)}, bf16[192,512]{1,0:T(8,128)(2,1)S(1)}, u32[]{:S(2)}, u32[]{:S(2)}) collective-permute-start(bf16[192,512]{1,0:T(8,128)(2,1)S(1)} %get-tuple-element.122), channel_id=1, source_target_pairs={{0,16},{1,17},{2,18},{3,19},{4,20},{5,21},{6,22},{7,23},{8,24},{9,... | collective-permute-start | bytes 589832 | tf_op jit(solution)/shard_map/ppermute | solution.py:811
  178.7 10.2 %shard_map.91 = bf16[2,1024,512]{2,1,0:T(8,128)(2,1)} custom-call(s32[2]{0:T(128)} %counts_ref.3, f32[2,1024,512]{2,1,0:T(8,128)} %get-tuple-element.100.mid_ref, bf16[2,1024,2048]{2,1,0:T(8,128)(2,1)} %get-tuple-element.101.hid_ref, f32[32,512]{1,0:T(8,128)} %get-tuple-element.62.small_ref.refs_5_, bf16[2048,512]{1,0:T(8,128)(2,1)} %get-tuple-element.102.down_ref), custom_call_target="tpu_custom_call" | custom-call | flops 9900000256 | bytes 900000 | tf_op jit(solution)/shard_map/pallas_call | solution.py:790
  188.9 3.4 %collective-permute-done.39.refs_5_ = bf16[192,512]{1,0:T(8,128)(2,1)S(1)} collective-permute-done((bf16[192,512]{1,0:T(8,128)(2,1)S(1)}, bf16[192,512]{1,0:T(8,128)(2,1)S(1)}, u32[]{:S(2)}, u32[]{:S(2)}) %collective-permute-start.39) | collective-permute-done | bytes 196640 | tf_op jit(solution)/shard_map/ppermute | solution.py:811
  193.0 2.3 %shard_map.92 = f32[659,128]{1,0:T(8,128)} custom-call(s32[1]{0:T(128)} %bitcast.2.at_ref, s32[1]{0:T(128)} %bitcast.23.me_ref, bf16[192,512]{1,0:T(8,128)(2,1)} %get-tuple-element.103.refs_0_, bf16[192,512]{1,0:T(8,128)(2,1)} %copy-done.5, bf16[192,512]{1,0:T(8,128)(2,1)} %copy-done.6, bf16[192,512]{1,0:T(8,128)(2,1)} %copy-done.4, ...), custom_call_target="tpu_custom_call" | custom-call | tf_op jit(solution)/shard_map/pallas_call | solution.py:994
  (155 shorter events, 26.1 us)
Async XLA Ops:
  9.9 16.6 %collective-permute-start.1 = (bf16[192,512]{1,0:T(8,128)(2,1)}, bf16[192,512]{1,0:T(8,128)(2,1)S(1)}, u32[]{:S(2)}, u32[]{:S(2)}) collective-permute-start(bf16[192,512]{1,0:T(8,128)(2,1)} %shard_map.85.refs_0_.refs_6_), channel_id=1, source_target_pairs={{0,16},{1,17},{2,18},{3,19},{4,20},{5,21},{6,22},{7,23},{8,24},{9,... | collective-permute-start | bytes 589832 | tf_op jit(solution)/shard_map/ppermute | solution.py:811
  9.9 16.6 %collective-permute-start = (bf16[192,512]{1,0:T(8,128)(2,1)}, bf16[192,512]{1,0:T(8,128)(2,1)S(1)}, u32[]{:S(2)}, u32[]{:S(2)}) collective-permute-start(bf16[192,512]{1,0:T(8,128)(2,1)} %shard_map.85.refs_0_.refs_6_), channel_id=1, source_target_pairs={{0,8},{1,9},{2,10},{3,11},{4,12},{5,13},{6,14},{7,15},{8,0},{9,1},... | collective-permute-start | bytes 589832 | tf_op jit(solution)/shard_map/ppermute | solution.py:811
  10.7 16.7 %collective-permute-start.8 = (bf16[192,512]{1,0:T(8,128)(2,1)}, bf16[192,512]{1,0:T(8,128)(2,1)S(1)}, u32[]{:S(2)}, u32[]{:S(2)}) collective-permute-start(bf16[192,512]{1,0:T(8,128)(2,1)} %shard_map.85.refs_0_.refs_6_), channel_id=1, source_target_pairs={{0,4},{1,5},{2,6},{3,7},{4,0},{5,1},{6,2},{7,3},{8,12},{9,13},{10,... | collective-permute-start | bytes 589832 | tf_op jit(solution)/shard_map/ppermute | solution.py:811
  11.4 16.1 %collective-permute-start.6 = (bf16[192,512]{1,0:T(8,128)(2,1)}, bf16[192,512]{1,0:T(8,128)(2,1)S(1)}, u32[]{:S(2)}, u32[]{:S(2)}) collective-permute-start(bf16[192,512]{1,0:T(8,128)(2,1)} %shard_map.85.refs_0_.refs_6_), channel_id=1, source_target_pairs={{0,2},{1,3},{2,0},{3,1},{4,6},{5,7},{6,4},{7,5},{8,10},{9,11},{10,... | collective-permute-start | bytes 589832 | tf_op jit(solution)/shard_map/ppermute | solution.py:811
  16.2 13.9 %collective-permute-start.5 = (bf16[192,512]{1,0:T(8,128)(2,1)}, bf16[192,512]{1,0:T(8,128)(2,1)S(1)}, u32[]{:S(2)}, u32[]{:S(2)}) collective-permute-start(bf16[192,512]{1,0:T(8,128)(2,1)} %shard_map.85.refs_0_.refs_6_), channel_id=1, source_target_pairs={{0,1},{1,0},{2,3},{3,2},{4,5},{5,4},{6,7},{7,6},{8,9},{9,8},{10,11... | collective-permute-start | bytes 589832 | tf_op jit(solution)/shard_map/ppermute | solution.py:811
  28.0 12.2 %collective-permute-start.16 = (bf16[224,512]{1,0:T(8,128)(2,1)S(1)}, bf16[224,512]{1,0:T(8,128)(2,1)S(1)}, u32[]{:S(2)}, u32[]{:S(2)}) collective-permute-start(bf16[224,512]{1,0:T(8,128)(2,1)S(1)} %pad_maximum_fusion.1.refs_8_.refs_14_), channel_id=1, source_target_pairs={{0,6},{1,7},{2,4},{3,5},{4,2},{5,3},{6,0},{7,1},{8,14},{9,15},{10,... | collective-permute-start | bytes 688136 | tf_op jit(solution)/shard_map/ppermute | solution.py:811
  28.5 12.2 %collective-permute-start.14 = (bf16[224,512]{1,0:T(8,128)(2,1)S(1)}, bf16[224,512]{1,0:T(8,128)(2,1)S(1)}, u32[]{:S(2)}, u32[]{:S(2)}) collective-permute-start(bf16[224,512]{1,0:T(8,128)(2,1)S(1)} %pad_maximum_fusion.1.refs_8_.refs_14_), channel_id=1, source_target_pairs={{0,4},{1,5},{2,6},{3,7},{4,0},{5,1},{6,2},{7,3},{8,12},{9,13},{10,... | collective-permute-start | bytes 688136 | tf_op jit(solution)/shard_map/ppermute | solution.py:811
  42.0 16.5 %collective-permute-start.21 = (bf16[2,192,512]{2,1,0:T(8,128)(2,1)S(1)}, bf16[2,192,512]{2,1,0:T(8,128)(2,1)S(1)}, u32[]{:S(2)}, u32[]{:S(2)}) collective-permute-start(bf16[2,192,512]{2,1,0:T(8,128)(2,1)S(1)} %pad_maximum_fusion.refs_22_), channel_id=1, source_target_pairs={{0,4},{1,5},{2,6},{3,7},{4,0},{5,1},{6,2},{7,3},{8,12},{9,13},{10,... | collective-permute-start | bytes 1179656 | tf_op jit(solution)/shard_map/ppermute | solution.py:811
  43.3 15.3 %collective-permute-start.19 = (bf16[2,192,512]{2,1,0:T(8,128)(2,1)S(1)}, bf16[2,192,512]{2,1,0:T(8,128)(2,1)S(1)}, u32[]{:S(2)}, u32[]{:S(2)}) collective-permute-start(bf16[2,192,512]{2,1,0:T(8,128)(2,1)S(1)} %pad_maximum_fusion.refs_22_), channel_id=1, source_target_pairs={{0,2},{1,3},{2,0},{3,1},{4,6},{5,7},{6,4},{7,5},{8,10},{9,11},{10,... | collective-permute-start | bytes 1179656 | tf_op jit(solution)/shard_map/ppermute | solution.py:811
  43.8 24.9 %collective-permute-start.18 = (bf16[2,192,512]{2,1,0:T(8,128)(2,1)S(1)}, bf16[2,192,512]{2,1,0:T(8,128)(2,1)S(1)}, u32[]{:S(2)}, u32[]{:S(2)}) collective-permute-start(bf16[2,192,512]{2,1,0:T(8,128)(2,1)S(1)} %pad_maximum_fusion.refs_22_), channel_id=1, source_target_pairs={{0,1},{1,0},{2,3},{3,2},{4,5},{5,4},{6,7},{7,6},{8,9},{9,8},{10,11... | collective-permute-start | bytes 1179656 | tf_op jit(solution)/shard_map/ppermute | solution.py:811
  43.9 14.1 %collective-permute-start.24 = (bf16[192,512]{1,0:T(8,128)(2,1)S(1)}, bf16[192,512]{1,0:T(8,128)(2,1)S(1)}, u32[]{:S(2)}, u32[]{:S(2)}) collective-permute-start(bf16[192,512]{1,0:T(8,128)(2,1)S(1)} %collective-permute-done.3.refs_6_.refs_12_), channel_id=1, source_target_pairs={{16,0},{17,1},{18,2},{19,3},{20,4},{21,5},{22,6},{23,7},{24,8},{25... | collective-permute-start | bytes 589832 | tf_op jit(solution)/shard_map/ppermute | solution.py:811
  45.2 12.9 %collective-permute-start.27 = (bf16[192,512]{1,0:T(8,128)(2,1)S(1)}, bf16[192,512]{1,0:T(8,128)(2,1)S(1)}, u32[]{:S(2)}, u32[]{:S(2)}) collective-permute-start(bf16[192,512]{1,0:T(8,128)(2,1)S(1)} %collective-permute-done.26.refs_32_), channel_id=1, source_target_pairs={{0,1},{1,0},{2,3},{3,2},{4,5},{5,4},{6,7},{7,6},{8,9},{9,8},{10,11... | collective-permute-start | bytes 589832 | tf_op jit(solution)/shard_map/ppermute | solution.py:811
  122.8 27.4 %collective-permute-start.35 = (bf16[3,192,512]{2,1,0:T(8,128)(2,1)S(1)}, bf16[3,192,512]{2,1,0:T(8,128)(2,1)S(1)}, u32[]{:S(2)}, u32[]{:S(2)}) collective-permute-start(bf16[3,192,512]{2,1,0:T(8,128)(2,1)S(1)} %get-tuple-element.111), channel_id=1, source_target_pairs={{0,6},{1,7},{2,4},{3,5},{4,2},{5,3},{6,0},{7,1},{8,14},{9,15},{10,... | collective-permute-start | bytes 1769480 | tf_op jit(solution)/shard_map/ppermute | solution.py:811
  124.6 27.2 %collective-permute-start.34 = (bf16[3,192,512]{2,1,0:T(8,128)(2,1)S(1)}, bf16[3,192,512]{2,1,0:T(8,128)(2,1)S(1)}, u32[]{:S(2)}, u32[]{:S(2)}) collective-permute-start(bf16[3,192,512]{2,1,0:T(8,128)(2,1)S(1)} %get-tuple-element.112), channel_id=1, source_target_pairs={{0,4},{1,5},{2,6},{3,7},{4,0},{5,1},{6,2},{7,3},{8,12},{9,13},{10,... | collective-permute-start | bytes 1769480 | tf_op jit(solution)/shard_map/ppermute | solution.py:811
  125.9 26.1 %collective-permute-start.33 = (bf16[3,192,512]{2,1,0:T(8,128)(2,1)S(1)}, bf16[3,192,512]{2,1,0:T(8,128)(2,1)S(1)}, u32[]{:S(2)}, u32[]{:S(2)}) collective-permute-start(bf16[3,192,512]{2,1,0:T(8,128)(2,1)S(1)} %get-tuple-element.113), channel_id=1, source_target_pairs={{0,2},{1,3},{2,0},{3,1},{4,6},{5,7},{6,4},{7,5},{8,10},{9,11},{10,... | collective-permute-start | bytes 1769480 | tf_op jit(solution)/shard_map/ppermute | solution.py:811
  153.0 24.4 %collective-permute-start.38 = (bf16[192,512]{1,0:T(8,128)(2,1)S(1)}, bf16[192,512]{1,0:T(8,128)(2,1)S(1)}, u32[]{:S(2)}, u32[]{:S(2)}) collective-permute-start(bf16[192,512]{1,0:T(8,128)(2,1)S(1)} %get-tuple-element.119), channel_id=1, source_target_pairs={{0,24},{1,25},{2,26},{3,27},{4,28},{5,29},{6,30},{7,31},{8,16},{9,... | collective-permute-start | bytes 589832 | tf_op jit(solution)/shard_map/ppermute | solution.py:811
  157.6 31.3 %collective-permute-start.36 = (bf16[192,512]{1,0:T(8,128)(2,1)S(1)}, bf16[192,512]{1,0:T(8,128)(2,1)S(1)}, u32[]{:S(2)}, u32[]{:S(2)}) collective-permute-start(bf16[192,512]{1,0:T(8,128)(2,1)S(1)} %get-tuple-element.121), channel_id=1, source_target_pairs={{0,8},{1,9},{2,10},{3,11},{4,12},{5,13},{6,14},{7,15},{16,24},{17,... | collective-permute-start | bytes 589832 | tf_op jit(solution)/shard_map/ppermute | solution.py:811
  160.4 11.3 %collective-permute-start.32 = (bf16[192,512]{1,0:T(8,128)(2,1)S(1)}, bf16[192,512]{1,0:T(8,128)(2,1)S(1)}, u32[]{:S(2)}, u32[]{:S(2)}) collective-permute-start(bf16[192,512]{1,0:T(8,128)(2,1)S(1)} %get-tuple-element.115), channel_id=1, source_target_pairs={{0,6},{1,7},{2,4},{3,5},{4,2},{5,3},{6,0},{7,1},{8,14},{9,15},{10,... | collective-permute-start | bytes 589832 | tf_op jit(solution)/shard_map/ppermute | solution.py:811
  162.1 12.5 %collective-permute-start.31 = (bf16[192,512]{1,0:T(8,128)(2,1)S(1)}, bf16[192,512]{1,0:T(8,128)(2,1)S(1)}, u32[]{:S(2)}, u32[]{:S(2)}) collective-permute-start(bf16[192,512]{1,0:T(8,128)(2,1)S(1)} %get-tuple-element.116), channel_id=1, source_target_pairs={{0,4},{1,5},{2,6},{3,7},{4,0},{5,1},{6,2},{7,3},{8,12},{9,13},{10,... | collective-permute-start | bytes 589832 | tf_op jit(solution)/shard_map/ppermute | solution.py:811
  163.4 11.3 %collective-permute-start.30 = (bf16[192,512]{1,0:T(8,128)(2,1)S(1)}, bf16[192,512]{1,0:T(8,128)(2,1)S(1)}, u32[]{:S(2)}, u32[]{:S(2)}) collective-permute-start(bf16[192,512]{1,0:T(8,128)(2,1)S(1)} %get-tuple-element.117), channel_id=1, source_target_pairs={{0,2},{1,3},{2,0},{3,1},{4,6},{5,7},{6,4},{7,5},{8,10},{9,11},{10,... | collective-permute-start | bytes 589832 | tf_op jit(solution)/shard_map/ppermute | solution.py:811
  171.7 17.2 %collective-permute-start.37 = (bf16[192,512]{1,0:T(8,128)(2,1)S(1)}, bf16[192,512]{1,0:T(8,128)(2,1)S(1)}, u32[]{:S(2)}, u32[]{:S(2)}) collective-permute-start(bf16[192,512]{1,0:T(8,128)(2,1)S(1)} %get-tuple-element.122), channel_id=1, source_target_pairs={{0,16},{1,17},{2,18},{3,19},{4,20},{5,21},{6,22},{7,23},{8,24},{9,... | collective-permute-start | bytes 589832 | tf_op jit(solution)/shard_map/ppermute | solution.py:811
  174.8 14.1 %collective-permute-start.41 = (bf16[192,512]{1,0:T(8,128)(2,1)S(1)}, bf16[192,512]{1,0:T(8,128)(2,1)S(1)}, u32[]{:S(2)}, u32[]{:S(2)}) collective-permute-start(bf16[192,512]{1,0:T(8,128)(2,1)S(1)} %add_convert_fusion.5.refs_4_), channel_id=1, source_target_pairs={{24,0},{25,1},{26,2},{27,3},{28,4},{29,5},{30,6},{31,7},{23,31}} | collective-permute-start | bytes 589832 | tf_op jit(solution)/shard_map/ppermute | solution.py:811
  176.1 12.8 %collective-permute-start.40 = (bf16[192,512]{1,0:T(8,128)(2,1)S(1)}, bf16[192,512]{1,0:T(8,128)(2,1)S(1)}, u32[]{:S(2)}, u32[]{:S(2)}) collective-permute-start(bf16[192,512]{1,0:T(8,128)(2,1)S(1)} %add_convert_fusion.5.refs_4_), channel_id=1, source_target_pairs={{16,0},{17,1},{18,2},{19,3},{20,4},{21,5},{22,6},{23,7},{15,31}} | collective-permute-start | bytes 589832 | tf_op jit(solution)/shard_map/ppermute | solution.py:811
  177.4 15.0 %collective-permute-start.39 = (bf16[192,512]{1,0:T(8,128)(2,1)S(1)}, bf16[192,512]{1,0:T(8,128)(2,1)S(1)}, u32[]{:S(2)}, u32[]{:S(2)}) collective-permute-start(bf16[192,512]{1,0:T(8,128)(2,1)S(1)} %add_convert_fusion.5.refs_4_), channel_id=1, source_target_pairs={{8,0},{9,1},{10,2},{11,3},{12,4},{13,5},{14,6},{15,7},{7,31}} | collective-permute-start | bytes 589832 | tf_op jit(solution)/shard_map/ppermute | solution.py:811
  (55 other events, 503.6 us)

commit v4 on v3

--- a/solution.py
+++ b/solution.py
@@ -307,7 +307,7 @@
     h = (normal * small_ref[12:13, :] + small_ref[13:14, :]).astype(BF16)
     h_ref[0] = h
     turned = dot(turned_ref[0:T_K, :], h, NT)
-    q_ref[0] = turned[0:D].astype(BF16)
+    q_ref[0] = (turned[0:D] * (HEAD**-0.5)).astype(BF16)
     logits = turned[T_R : T_R + 8]
     shifted = jnp.exp(logits - jnp.max(logits, axis=0, keepdims=True))
     prob_ref[0] = shifted / jnp.sum(shifted, axis=0, keepdims=True)
@@ -321,7 +321,7 @@
         keys = k_ref[0, pl.ds(w0, KB), :]
         values = v_ref[0, pl.ds(w0, KB), :]
         pairs = range(EXPERTS // 2)
-        scores = [dot(keys, two_heads(q_ref, pair, q0), NN) * (HEAD**-0.5) + bias for pair in pairs]
+        scores = [dot(keys, two_heads(q_ref, pair, q0), NN) + bias for pair in pairs]
         peak = [jnp.max(part, axis=0, keepdims=True) for part in scores]
         expd = [jnp.exp(part - top) for part, top in zip(scores, peak)]
         summed = [jnp.sum(part, axis=0, keepdims=True) for part in expd]
@@ -652,7 +652,7 @@
         queries = [two_heads(q_ref, pair, q0) for pair in pairs]
         datt = [two_heads(datt_ref, pair, q0) for pair in pairs]
         soft = [
-            jnp.exp(dot(keys, part, NN) * (HEAD**-0.5) + bias - two_rows(lse_ref, pair, q0))
+            jnp.exp(dot(keys, part, NN) + bias - two_rows(lse_ref, pair, q0))
             for pair, part in enumerate(queries)
         ]
         dscores = [
@@ -667,7 +667,7 @@
             for half in range(2):
                 head, part = 2 * pair + half, slice(QB * half, QB * (half + 1))
                 back_ref[0, 64 * head : 64 * (head + 1), pl.ds(q0, QB)] = dq[:, part]
-        dk_ref[pl.ds(w0, KB), :] += dk * (HEAD**-0.5)
+        dk_ref[pl.ds(w0, KB), :] += dk
         dv_ref[pl.ds(w0, KB), :] += dv
         return carry
 
@@ -932,80 +932,48 @@
     return total.astype(BF16)
 
 
-def main_picks(total, my_plane):
-    owned = [total[0]] + [total[z] for z in range(PLANES - 1)]
+def plane_picks(plan, head, main, my_plane, my_lane):
+    low = ROW_S - 16 * plan.first(ALL - 1)
+    small = head[SMALL_AT : SMALL_AT + 16]
+    last = jnp.concatenate([main[-1][:low], small, main[-1][low + 16 :]], axis=0)
+    last = jnp.where(my_lane == LANES - 1, last, main[-1])
+    planes = [head, *(main[z] for z in range(PLANES - 2)), last]
     return [
-        by_plane([owned[mine ^ s] for mine in range(PLANES)], my_plane) for s in range(PLANES)
+        by_plane([planes[mine ^ s] for mine in range(PLANES)], my_plane) for s in range(PLANES)
     ]
 
 
 def to_planes(picks):
     out = [picks[0]]
     for s in range(1, PLANES):
-        pairs = [
-            (z * LANES + f, (z ^ s) * LANES + f)
-            for z in range(PLANES)
-            if z ^ s
-            for f in range(LANES)
-        ]
+        pairs = [(z * LANES + f, (z ^ s) * LANES + f) for z in range(PLANES) for f in range(LANES)]
         out.append(move(picks[s], pairs))
     return out
 
 
-def head_parts(total):
-    out = [total]
-    last = PLANES - 1
-    for s in range(1, PLANES):
-        pairs = [(s * LANES + f, f) for f in range(LANES)]
-        pairs.append(((s - 1) * LANES + LANES - 1, last * LANES + LANES - 1))
-        out.append(move(total, pairs))
-    return out
-
-
-def owned_kernel(plan, at_ref, me_ref, *refs):
-    main, head = refs[:PLANES], refs[PLANES : 2 * PLANES]
-    out_ref, sum_ref, pad_ref = refs[2 * PLANES :]
-
-    def add(parts, low, high):
-        total = parts[0][low:high].astype(F32)
-        for part in parts[1:]:
-            total = total + part[low:high].astype(F32)
-        return total
-
-    @pl.when(me_ref[0] < LANES)
-    def _():
-        sum_ref[...] = add(head, 0, plan.rows)
-
-    @pl.when(me_ref[0] >= LANES)
-    def _():
-        sum_ref[...] = add(main, 0, plan.rows)
-
-    @pl.when(me_ref[0] == ALL - 1)
-    def _():
-        low = ROW_S - 16 * plan.first(ALL - 1)
-        sum_ref[low : low + 16, :] = add(head, SMALL_AT, SMALL_AT + 16)
-
+def owned_kernel(plan, at_ref, *refs):
+    parts, (out_ref, pad_ref) = refs[:PLANES], refs[PLANES:]
+    total = parts[0][...].astype(F32)
+    for part in parts[1:]:
+        total = total + part[...].astype(F32)
     for j in range(4):
-        pad_ref[pl.ds(j, plan.rows, stride=4), :] = sum_ref[:, 128 * j : 128 * (j + 1)]
+        pad_ref[pl.ds(j, plan.rows, stride=4), :] = total[:, 128 * j : 128 * (j + 1)]
     out_ref[...] = pad_ref[pl.ds(at_ref[0], plan.lanes), :]
 
 
-def take_owned(plan, at, me, main, head):
+def take_owned(plan, at, parts):
     out = pl.pallas_call(
         partial(owned_kernel, plan),
         grid_spec=pltpu.PrefetchScalarGridSpec(
-            num_scalar_prefetch=2,
+            num_scalar_prefetch=1,
             grid=(1,),
-            in_specs=[whole(plan.rows, D)] * (2 * PLANES),
+            in_specs=[whole(plan.rows, D)] * PLANES,
             out_specs=whole(plan.lanes, 128),
-            scratch_shapes=[
-                pltpu.VMEM((plan.rows, D), F32),
-                pltpu.VMEM((plan.rows * 4, 128), F32),
-            ],
+            scratch_shapes=[pltpu.VMEM((plan.rows * 4, 128), F32)],
         ),
         out_shape=kind(F32, plan.lanes, 128),
         compiler_params=params(),
-    )(at, me, *main, *head)
+    )(at, *parts)
     return out.reshape(-1)
 
 
@@ -1069,14 +1037,12 @@
         return output, input_grad(x, dmid, back, turned, small), grads
     keep, send = (part[:, 0] for part in packed)
     main = summed(all_after(main, keep))
-    picks = main_picks(main, my_plane)
     parts = core_sum(keep, send)
-    grad_tokens = input_grad(x, dmid, after(back, *parts, *picks), turned, small)
+    grad_tokens = input_grad(x, dmid, after(back, *parts, main), turned, small)
     total = summed(all_after(plane_swap(parts), grad_tokens))
-    output = layer_output(counts, after(mid, total), hid, small, down)
-    me = me.astype(jnp.int32).reshape(1)
-    owned = all_after([*to_planes(picks), *head_parts(total)], output)
-    return output, grad_tokens, take_owned(plan, at, me, owned[:PLANES], owned[PLANES:])
+    picks = plane_picks(plan, total, main, my_plane, my_lane)
+    output = layer_output(counts, after(mid, *picks), hid, small, down)
+    return output, grad_tokens, take_owned(plan, at, all_after(to_planes(picks), output))
 
 
 def solution(mesh):

time: 196 us -> 190 us (0.969)
  starting transfers between devices: 43.5 us -> 34.8 us
  other arithmetic: 5.36 us -> 7.64 us
    ppermute x42 -> x39, starting transfers between devices: 43.5 us -> 34.8 us  [move(): return lax.ppermute(value, AXES, pairs)]
    ppermute x42 -> x39, waiting for transfers between devices: 30.3 us -> 31.5 us  [move(): return lax.ppermute(value, AXES, pairs)]
  transfers between devices with their start and end apart: 42 -> 39, of which waited for: 9 -> 11; matrix products, arithmetic and copies ran while one was open for 2% -> 2% of each run, Pallas kernels for 32% -> 33%
where the time goes in v4:
time: 190 us; the launch traced here: 189 us
  Pallas kernels  111 us (58%)
  starting transfers between devices  34.8 us (18%)
  waiting for transfers between devices  31.5 us (17%)
  other arithmetic  7.64 us (4%)
  local copies, waits for them, and re-layouts  2.55 us (1%)
    pallas_call x1, Pallas kernels, feed_forward(): pl.pallas_call(partial(feed_kernel, plan, gathered, len(wins), pieces), g...  45.8 us
    ppermute x39, starting transfers between devices, move(): return lax.ppermute(value, AXES, pairs)  34.8 us
    ppermute x39, waiting for transfers between devices, move(): return lax.ppermute(value, AXES, pairs)  31.5 us
    pallas_call x1, Pallas kernels, attention_backward(): pl.pallas_call(partial(backward_kernel, pieces), grid_spec=pltpu.Prefetch...  23.3 us
    pallas_call x2, Pallas kernels, attention_forward(): pl.pallas_call(kernel, grid_spec=pltpu.PrefetchScalarGridSpec(num_scalar_...  20.6 us
    pallas_call x1, Pallas kernels, layer_output(): pl.pallas_call(output_kernel, grid_spec=pltpu.PrefetchScalarGridSpec(num_...  10.1 us
    pallas_call x1, Pallas kernels, input_grad(): pl.pallas_call(input_kernel, grid=(rows, length // TB), in_specs=[row_blo...  7.72 us
  transfers between devices with their start and end apart: 39, of which 11 were waited for; matrix products, arithmetic and copies ran while one was open for 2% of the time, Pallas kernels for 33%

profile of v4, /device:TPU:0, one launch (start us, length us, event | category | flops | bytes accessed | tf_op | source)
XLA Modules:
  0.0 189.2 jit_solution(12483370043489528276)
XLA Ops:
  0.7 1.7 shard_map.85.refs_0_.refs_6_
  2.4 3.9 %collective-permute-start.3 = (bf16[192,512]{1,0:T(8,128)(2,1)}, bf16[192,512]{1,0:T(8,128)(2,1)S(1)}, u32[]{:S(2)}, u32[]{:S(2)}) collective-permute-start(bf16[192,512]{1,0:T(8,128)(2,1)} %shard_map.85.refs_0_.refs_6_), channel_id=1, source_target_pairs={{0,6},{1,7},{2,4},{3,5},{4,2},{5,3},{6,0},{7,1},{8,14},{9,15},{10,... | collective-permute-start | bytes 589832 | tf_op jit(solution)/shard_map/ppermute | solution.py:811
  6.3 3.6 %collective-permute-start.2 = (bf16[192,512]{1,0:T(8,128)(2,1)}, bf16[192,512]{1,0:T(8,128)(2,1)S(1)}, u32[]{:S(2)}, u32[]{:S(2)}) collective-permute-start(bf16[192,512]{1,0:T(8,128)(2,1)} %shard_map.85.refs_0_.refs_6_), channel_id=1, source_target_pairs={{0,24},{1,25},{2,26},{3,27},{4,28},{5,29},{6,30},{7,31},{8,16},{9,... | collective-permute-start | bytes 589832 | tf_op jit(solution)/shard_map/ppermute | solution.py:811
  11.4 1.7 collective-permute-start.6
  13.1 3.1 %collective-permute-done.2 = bf16[192,512]{1,0:T(8,128)(2,1)S(1)} collective-permute-done((bf16[192,512]{1,0:T(8,128)(2,1)}, bf16[192,512]{1,0:T(8,128)(2,1)S(1)}, u32[]{:S(2)}, u32[]{:S(2)}) %collective-permute-start.2) | collective-permute-done | bytes 196640 | tf_op jit(solution)/shard_map/ppermute | solution.py:811
  16.2 10.3 %collective-permute-done.1 = bf16[192,512]{1,0:T(8,128)(2,1)S(1)} collective-permute-done((bf16[192,512]{1,0:T(8,128)(2,1)}, bf16[192,512]{1,0:T(8,128)(2,1)S(1)}, u32[]{:S(2)}, u32[]{:S(2)}) %collective-permute-start.1) | collective-permute-done | bytes 196640 | tf_op jit(solution)/shard_map/ppermute | solution.py:811
  28.5 1.5 collective-permute-start.14
  30.1 1.5 collective-permute-start.12
  34.3 5.9 %collective-permute-done.4.refs_28_ = bf16[192,512]{1,0:T(8,128)(2,1)S(1)} collective-permute-done((bf16[192,512]{1,0:T(8,128)(2,1)S(1)}, bf16[192,512]{1,0:T(8,128)(2,1)S(1)}, u32[]{:S(2)}, u32[]{:S(2)}) %collective-permute-start.4) | collective-permute-done | bytes 196640 | tf_op jit(solution)/shard_map/ppermute | solution.py:811
  45.8 11.2 %shard_map.86 = (bf16[2,512,1024]{2,1,0:T(8,128)(2,1)}, bf16[2,1024,64]{2,1,0:T(8,128)(2,1)}, bf16[2,1024,64]{2,1,0:T(8,128)(2,1)}, bf16[2,1024,512]{2,1,0:T(8,1...) custom-call(s32[2]{0:T(128)} %pad_add_fusion.place_ref, ...), custom_call_target="tpu_custom_call" | custom-call | flops 15399999488 | bytes 1400000 | tf_op jit(solution)/shard_map/pallas_call | solution.py:387
  59.0 9.5 %shard_map.87 = (bf16[2,512,1024]{2,1,0:T(8,128)(2,1)}, bf16[2,1024,64]{2,1,0:T(8,128)(2,1)}, bf16[2,1024,64]{2,1,0:T(8,128)(2,1)}, bf16[2,1024,512]{2,1,0:T(8,1...) custom-call(s32[2]{0:T(128)} %pad_add_fusion.place_ref, ...), custom_call_target="tpu_custom_call", output_to_operand_aliasing={{0}: (5, {}), {1}: (6, {}), {2}: (7, {}), {3}: (8, {}), {4}... | custom-call | flops 15399999488 | bytes 1400000 | tf_op jit(solution)/shard_map/pallas_call | solution.py:387
  69.7 45.8 %shard_map.88 = (bf16[2,1024,2048]{2,1,0:T(8,128)(2,1)}, f32[2,1024,512]{2,1,0:T(8,128)}, f32[2,1024,512]{2,1,0:T(8,128)}, bf16[2,512,1024]{2,1,0:T(8,128)(2,1)}...) custom-call(s32[2]{0:T(128)} %pad_add_fusion.place_ref, ...), custom_call_target="tpu_custom_call" | custom-call | flops 54999998464 | bytes 5000000 | tf_op jit(solution)/shard_map/pallas_call | solution.py:565
  115.7 4.6 %collective-permute-done.28 = bf16[4,3,192,512]{3,2,1,0:T(8,128)(2,1)S(1)} collective-permute-done((bf16[4,3,192,512]{3,2,1,0:T(8,128)(2,1)}, bf16[4,3,192,512]{3,2,1,0:T(8,128)(2,1)S(1)}, u32[]{:S(2)}, u32[]{:S(2)}) %collective-permute-start.28) | collective-permute-done | bytes 2359328 | tf_op jit(solution)/shard_map/ppermute | solution.py:811
  120.4 3.1 %fusion.3 = (bf16[3,192,512]{2,1,0:T(8,128)(2,1)}, bf16[3,192,512]{2,1,0:T(8,128)(2,1)S(1)}, bf16[3,192,512]{2,1,0:T(8,128)(2,1)S(1)}, bf16[3,192,512]{2,1,0:T(8,128)(2,1)S(1)}) fusion(bf16[4,3,192,512]{3,2,1,0:T(8,128)(2,1)S(1)} %collective-permute-done.28, bf16[4,3,192,512]{3,2,1,0:T(8,128)(2,1)} %get-tuple-element.69), kind=kLoop, calls=%fused_computation.8 | loop fusion | flops 4718592 | bytes 7077888 | tf_op jit(solution)/shard_map/convert_element_type | solution.py:921
  123.5 1.8 collective-permute-start.31
  127.0 23.3 %shard_map.89 = (bf16[2,656,1024]{2,1,0:T(8,128)(2,1)}, bf16[640,512]{1,0:T(8,128)(2,1)}, bf16[32,512]{1,0:T(8,128)(2,1)}, bf16[4,1,192,512]{3,2,1,0:T(8,128)(2,1)}, bf16[4,1,192,512]{3,2,1,0:T(8,128)(2,1)}) custom-call(s32[2]{0:T(128)} %pad_add_fusion.place_ref, bf16[2,1024,512]{2,1,0:T(8,128)(2,1)} %x_ref.5, ...), custom_call_target="tpu_custom_call" | custom-call | flops 36300001280 | bytes 3300000 | tf_op jit(solution)/shard_map/pallas_call | solution.py:713
  150.4 2.3 %collective-permute-done.30 = bf16[3,192,512]{2,1,0:T(8,128)(2,1)} collective-permute-done((bf16[3,192,512]{2,1,0:T(8,128)(2,1)S(1)}, bf16[3,192,512]{2,1,0:T(8,128)(2,1)}, u32[]{:S(2)}, u32[]{:S(2)}) %collective-permute-start.30) | collective-permute-done | bytes 589856 | tf_op jit(solution)/shard_map/ppermute | solution.py:811
  152.9 1.7 add_convert_fusion
  158.5 7.7 %shard_map.90 = bf16[2,1024,512]{2,1,0:T(8,128)(2,1)} custom-call(bf16[2,1024,512]{2,1,0:T(8,128)(2,1)} %x_ref.5, f32[2,1024,512]{2,1,0:T(8,128)} %get-tuple-element.89.dmid_ref, bf16[2,656,1024]{2,1,0:T(8,128)(2,1)} %get-tuple-element.91.back_ref, bf16[656,512]{1,0:T(8,128)(2,1)} %get-tuple-element.57.turned_ref.refs_10_, ...), custom_call_target="tpu_custom_call" | custom-call | flops 8800000000 | bytes 800000 | tf_op jit(solution)/shard_map/pallas_call | solution.py:765
  167.8 2.8 %collective-permute-start.37 = (bf16[192,512]{1,0:T(8,128)(2,1)S(1)}, bf16[192,512]{1,0:T(8,128)(2,1)S(1)}, u32[]{:S(2)}, u32[]{:S(2)}) collective-permute-start(bf16[192,512]{1,0:T(8,128)(2,1)S(1)} %get-tuple-element.113), channel_id=1, source_target_pairs={{0,16},{1,17},{2,18},{3,19},{4,20},{5,21},{6,22},{7,23},{8,24},{9,... | collective-permute-start | bytes 589832 | tf_op jit(solution)/shard_map/ppermute | solution.py:811
  171.0 2.1 %collective-permute-start.38 = (bf16[192,512]{1,0:T(8,128)(2,1)S(1)}, bf16[192,512]{1,0:T(8,128)(2,1)S(1)}, u32[]{:S(2)}, u32[]{:S(2)}) collective-permute-start(bf16[192,512]{1,0:T(8,128)(2,1)S(1)} %get-tuple-element.103), channel_id=1, source_target_pairs={{0,24},{1,25},{2,26},{3,27},{4,28},{5,29},{6,30},{7,31},{8,16},{9,... | collective-permute-start | bytes 589832 | tf_op jit(solution)/shard_map/ppermute | solution.py:811
  173.1 10.1 %shard_map.91 = bf16[2,1024,512]{2,1,0:T(8,128)(2,1)} custom-call(s32[2]{0:T(128)} %counts_ref.3, f32[2,1024,512]{2,1,0:T(8,128)} %get-tuple-element.96.mid_ref, bf16[2,1024,2048]{2,1,0:T(8,128)(2,1)} %get-tuple-element.97.hid_ref, f32[32,512]{1,0:T(8,128)} %get-tuple-element.58.small_ref.refs_5_, bf16[2048,512]{1,0:T(8,128)(2,1)} %get-tuple-element.98.down_ref), custom_call_target="tpu_custom_call" | custom-call | flops 9900000256 | bytes 900000 | tf_op jit(solution)/shard_map/pallas_call | solution.py:790
  183.3 3.1 %collective-permute-done.38.refs_3_ = bf16[192,512]{1,0:T(8,128)(2,1)S(1)} collective-permute-done((bf16[192,512]{1,0:T(8,128)(2,1)S(1)}, bf16[192,512]{1,0:T(8,128)(2,1)S(1)}, u32[]{:S(2)}, u32[]{:S(2)}) %collective-permute-start.38) | collective-permute-done | bytes 196640 | tf_op jit(solution)/shard_map/ppermute | solution.py:811
  187.1 2.1 %shard_map.92 = f32[659,128]{1,0:T(8,128)} custom-call(s32[1]{0:T(128)} %bitcast.2.at_ref, bf16[192,512]{1,0:T(8,128)(2,1)} %get-tuple-element.99.refs_0_, bf16[192,512]{1,0:T(8,128)(2,1)} %copy-done.4, bf16[192,512]{1,0:T(8,128)(2,1)} %copy-done.3, bf16[192,512]{1,0:T(8,128)(2,1)} %copy-done.5), custom_call_target="tpu_custom_call" | custom-call | tf_op jit(solution)/shard_map/pallas_call | solution.py:965
  (145 shorter events, 23.3 us)
Async XLA Ops:
  9.9 16.6 %collective-permute-start.1 = (bf16[192,512]{1,0:T(8,128)(2,1)}, bf16[192,512]{1,0:T(8,128)(2,1)S(1)}, u32[]{:S(2)}, u32[]{:S(2)}) collective-permute-start(bf16[192,512]{1,0:T(8,128)(2,1)} %shard_map.85.refs_0_.refs_6_), channel_id=1, source_target_pairs={{0,16},{1,17},{2,18},{3,19},{4,20},{5,21},{6,22},{7,23},{8,24},{9,... | collective-permute-start | bytes 589832 | tf_op jit(solution)/shard_map/ppermute | solution.py:811
  9.9 16.6 %collective-permute-start = (bf16[192,512]{1,0:T(8,128)(2,1)}, bf16[192,512]{1,0:T(8,128)(2,1)S(1)}, u32[]{:S(2)}, u32[]{:S(2)}) collective-permute-start(bf16[192,512]{1,0:T(8,128)(2,1)} %shard_map.85.refs_0_.refs_6_), channel_id=1, source_target_pairs={{0,8},{1,9},{2,10},{3,11},{4,12},{5,13},{6,14},{7,15},{8,0},{9,1},... | collective-permute-start | bytes 589832 | tf_op jit(solution)/shard_map/ppermute | solution.py:811
  10.7 16.7 %collective-permute-start.8 = (bf16[192,512]{1,0:T(8,128)(2,1)}, bf16[192,512]{1,0:T(8,128)(2,1)S(1)}, u32[]{:S(2)}, u32[]{:S(2)}) collective-permute-start(bf16[192,512]{1,0:T(8,128)(2,1)} %shard_map.85.refs_0_.refs_6_), channel_id=1, source_target_pairs={{0,4},{1,5},{2,6},{3,7},{4,0},{5,1},{6,2},{7,3},{8,12},{9,13},{10,... | collective-permute-start | bytes 589832 | tf_op jit(solution)/shard_map/ppermute | solution.py:811
  11.4 16.1 %collective-permute-start.6 = (bf16[192,512]{1,0:T(8,128)(2,1)}, bf16[192,512]{1,0:T(8,128)(2,1)S(1)}, u32[]{:S(2)}, u32[]{:S(2)}) collective-permute-start(bf16[192,512]{1,0:T(8,128)(2,1)} %shard_map.85.refs_0_.refs_6_), channel_id=1, source_target_pairs={{0,2},{1,3},{2,0},{3,1},{4,6},{5,7},{6,4},{7,5},{8,10},{9,11},{10,... | collective-permute-start | bytes 589832 | tf_op jit(solution)/shard_map/ppermute | solution.py:811
  16.2 13.9 %collective-permute-start.5 = (bf16[192,512]{1,0:T(8,128)(2,1)}, bf16[192,512]{1,0:T(8,128)(2,1)S(1)}, u32[]{:S(2)}, u32[]{:S(2)}) collective-permute-start(bf16[192,512]{1,0:T(8,128)(2,1)} %shard_map.85.refs_0_.refs_6_), channel_id=1, source_target_pairs={{0,1},{1,0},{2,3},{3,2},{4,5},{5,4},{6,7},{7,6},{8,9},{9,8},{10,11... | collective-permute-start | bytes 589832 | tf_op jit(solution)/shard_map/ppermute | solution.py:811
  28.0 12.2 %collective-permute-start.16 = (bf16[224,512]{1,0:T(8,128)(2,1)S(1)}, bf16[224,512]{1,0:T(8,128)(2,1)S(1)}, u32[]{:S(2)}, u32[]{:S(2)}) collective-permute-start(bf16[224,512]{1,0:T(8,128)(2,1)S(1)} %pad_maximum_fusion.1.refs_8_.refs_14_), channel_id=1, source_target_pairs={{0,6},{1,7},{2,4},{3,5},{4,2},{5,3},{6,0},{7,1},{8,14},{9,15},{10,... | collective-permute-start | bytes 688136 | tf_op jit(solution)/shard_map/ppermute | solution.py:811
  28.5 12.2 %collective-permute-start.14 = (bf16[224,512]{1,0:T(8,128)(2,1)S(1)}, bf16[224,512]{1,0:T(8,128)(2,1)S(1)}, u32[]{:S(2)}, u32[]{:S(2)}) collective-permute-start(bf16[224,512]{1,0:T(8,128)(2,1)S(1)} %pad_maximum_fusion.1.refs_8_.refs_14_), channel_id=1, source_target_pairs={{0,4},{1,5},{2,6},{3,7},{4,0},{5,1},{6,2},{7,3},{8,12},{9,13},{10,... | collective-permute-start | bytes 688136 | tf_op jit(solution)/shard_map/ppermute | solution.py:811
  30.1 10.8 %collective-permute-start.12 = (bf16[224,512]{1,0:T(8,128)(2,1)S(1)}, bf16[224,512]{1,0:T(8,128)(2,1)S(1)}, u32[]{:S(2)}, u32[]{:S(2)}) collective-permute-start(bf16[224,512]{1,0:T(8,128)(2,1)S(1)} %pad_maximum_fusion.1.refs_8_.refs_14_), channel_id=1, source_target_pairs={{0,2},{1,3},{2,0},{3,1},{4,6},{5,7},{6,4},{7,5},{8,10},{9,11},{10,... | collective-permute-start | bytes 688136 | tf_op jit(solution)/shard_map/ppermute | solution.py:811
  42.0 16.5 %collective-permute-start.21 = (bf16[2,192,512]{2,1,0:T(8,128)(2,1)S(1)}, bf16[2,192,512]{2,1,0:T(8,128)(2,1)S(1)}, u32[]{:S(2)}, u32[]{:S(2)}) collective-permute-start(bf16[2,192,512]{2,1,0:T(8,128)(2,1)S(1)} %pad_maximum_fusion.refs_22_), channel_id=1, source_target_pairs={{0,4},{1,5},{2,6},{3,7},{4,0},{5,1},{6,2},{7,3},{8,12},{9,13},{10,... | collective-permute-start | bytes 1179656 | tf_op jit(solution)/shard_map/ppermute | solution.py:811
  43.3 15.3 %collective-permute-start.19 = (bf16[2,192,512]{2,1,0:T(8,128)(2,1)S(1)}, bf16[2,192,512]{2,1,0:T(8,128)(2,1)S(1)}, u32[]{:S(2)}, u32[]{:S(2)}) collective-permute-start(bf16[2,192,512]{2,1,0:T(8,128)(2,1)S(1)} %pad_maximum_fusion.refs_22_), channel_id=1, source_target_pairs={{0,2},{1,3},{2,0},{3,1},{4,6},{5,7},{6,4},{7,5},{8,10},{9,11},{10,... | collective-permute-start | bytes 1179656 | tf_op jit(solution)/shard_map/ppermute | solution.py:811
  43.8 24.8 %collective-permute-start.18 = (bf16[2,192,512]{2,1,0:T(8,128)(2,1)S(1)}, bf16[2,192,512]{2,1,0:T(8,128)(2,1)S(1)}, u32[]{:S(2)}, u32[]{:S(2)}) collective-permute-start(bf16[2,192,512]{2,1,0:T(8,128)(2,1)S(1)} %pad_maximum_fusion.refs_22_), channel_id=1, source_target_pairs={{0,1},{1,0},{2,3},{3,2},{4,5},{5,4},{6,7},{7,6},{8,9},{9,8},{10,11... | collective-permute-start | bytes 1179656 | tf_op jit(solution)/shard_map/ppermute | solution.py:811
  43.8 14.1 %collective-permute-start.24 = (bf16[192,512]{1,0:T(8,128)(2,1)S(1)}, bf16[192,512]{1,0:T(8,128)(2,1)S(1)}, u32[]{:S(2)}, u32[]{:S(2)}) collective-permute-start(bf16[192,512]{1,0:T(8,128)(2,1)S(1)} %collective-permute-done.3.refs_6_.refs_12_), channel_id=1, source_target_pairs={{16,0},{17,1},{18,2},{19,3},{20,4},{21,5},{22,6},{23,7},{24,8},{25... | collective-permute-start | bytes 589832 | tf_op jit(solution)/shard_map/ppermute | solution.py:811
  45.1 12.9 %collective-permute-start.27 = (bf16[192,512]{1,0:T(8,128)(2,1)S(1)}, bf16[192,512]{1,0:T(8,128)(2,1)S(1)}, u32[]{:S(2)}, u32[]{:S(2)}) collective-permute-start(bf16[192,512]{1,0:T(8,128)(2,1)S(1)} %collective-permute-done.26.refs_32_), channel_id=1, source_target_pairs={{0,1},{1,0},{2,3},{3,2},{4,5},{5,4},{6,7},{7,6},{8,9},{9,8},{10,11... | collective-permute-start | bytes 589832 | tf_op jit(solution)/shard_map/ppermute | solution.py:811
  58.0 10.6 %collective-permute-start.23 = (bf16[192,512]{1,0:T(8,128)(2,1)S(1)}, bf16[192,512]{1,0:T(8,128)(2,1)S(1)}, u32[]{:S(2)}, u32[]{:S(2)}) collective-permute-start(bf16[192,512]{1,0:T(8,128)(2,1)S(1)} %collective-permute-done.4.refs_28_), channel_id=1, source_target_pairs={{0,1},{1,0},{2,3},{3,2},{4,5},{5,4},{6,7},{7,6},{8,9},{9,8},{10,11... | collective-permute-start | bytes 589832 | tf_op jit(solution)/shard_map/ppermute | solution.py:811
  58.0 10.5 %collective-permute-start.25 = (bf16[192,512]{1,0:T(8,128)(2,1)S(1)}, bf16[192,512]{1,0:T(8,128)(2,1)S(1)}, u32[]{:S(2)}, u32[]{:S(2)}) collective-permute-start(bf16[192,512]{1,0:T(8,128)(2,1)S(1)} %collective-permute-done.24.refs_30_), channel_id=1, source_target_pairs={{0,1},{1,0},{2,3},{3,2},{4,5},{5,4},{6,7},{7,6},{8,9},{9,8},{10,11... | collective-permute-start | bytes 589832 | tf_op jit(solution)/shard_map/ppermute | solution.py:811
  58.5 10.1 %collective-permute-start.22 = (bf16[2,192,512]{2,1,0:T(8,128)(2,1)S(1)}, bf16[2,192,512]{2,1,0:T(8,128)(2,1)S(1)}, u32[]{:S(2)}, u32[]{:S(2)}) collective-permute-start(bf16[2,192,512]{2,1,0:T(8,128)(2,1)S(1)} %collective-permute-done.21.refs_26_), channel_id=1, source_target_pairs={{0,1},{1,0},{2,3},{3,2},{4,5},{5,4},{6,7},{7,6},{8,9},{9,8},{10,11... | collective-permute-start | bytes 1179656 | tf_op jit(solution)/shard_map/ppermute | solution.py:811
  123.5 26.9 %collective-permute-start.31 = (bf16[3,192,512]{2,1,0:T(8,128)(2,1)}, bf16[3,192,512]{2,1,0:T(8,128)(2,1)}, u32[]{:S(2)}, u32[]{:S(2)}) collective-permute-start(bf16[3,192,512]{2,1,0:T(8,128)(2,1)} %get-tuple-element.105), channel_id=1, source_target_pairs={{0,6},{1,7},{2,4},{3,5},{4,2},{5,3},{6,0},{7,1},{8,14},{9,15},{10,... | collective-permute-start | bytes 1769480 | tf_op jit(solution)/shard_map/ppermute | solution.py:811
  125.3 27.4 %collective-permute-start.30 = (bf16[3,192,512]{2,1,0:T(8,128)(2,1)S(1)}, bf16[3,192,512]{2,1,0:T(8,128)(2,1)}, u32[]{:S(2)}, u32[]{:S(2)}) collective-permute-start(bf16[3,192,512]{2,1,0:T(8,128)(2,1)S(1)} %get-tuple-element.106), channel_id=1, source_target_pairs={{0,4},{1,5},{2,6},{3,7},{4,0},{5,1},{6,2},{7,3},{8,12},{9,13},{10,... | collective-permute-start | bytes 1769480 | tf_op jit(solution)/shard_map/ppermute | solution.py:811
  126.5 26.4 %collective-permute-start.29 = (bf16[3,192,512]{2,1,0:T(8,128)(2,1)S(1)}, bf16[3,192,512]{2,1,0:T(8,128)(2,1)}, u32[]{:S(2)}, u32[]{:S(2)}) collective-permute-start(bf16[3,192,512]{2,1,0:T(8,128)(2,1)S(1)} %get-tuple-element.107), channel_id=1, source_target_pairs={{0,2},{1,3},{2,0},{3,1},{4,6},{5,7},{6,4},{7,5},{8,10},{9,11},{10,... | collective-permute-start | bytes 1769480 | tf_op jit(solution)/shard_map/ppermute | solution.py:811
  154.9 11.3 %collective-permute-start.35 = (bf16[192,512]{1,0:T(8,128)(2,1)S(1)}, bf16[192,512]{1,0:T(8,128)(2,1)S(1)}, u32[]{:S(2)}, u32[]{:S(2)}) collective-permute-start(bf16[192,512]{1,0:T(8,128)(2,1)S(1)} %get-tuple-element.109), channel_id=1, source_target_pairs={{0,6},{1,7},{2,4},{3,5},{4,2},{5,3},{6,0},{7,1},{8,14},{9,15},{10,... | collective-permute-start | bytes 589832 | tf_op jit(solution)/shard_map/ppermute | solution.py:811
  156.3 10.4 %collective-permute-start.34 = (bf16[192,512]{1,0:T(8,128)(2,1)S(1)}, bf16[192,512]{1,0:T(8,128)(2,1)S(1)}, u32[]{:S(2)}, u32[]{:S(2)}) collective-permute-start(bf16[192,512]{1,0:T(8,128)(2,1)S(1)} %get-tuple-element.110), channel_id=1, source_target_pairs={{0,4},{1,5},{2,6},{3,7},{4,0},{5,1},{6,2},{7,3},{8,12},{9,13},{10,... | collective-permute-start | bytes 589832 | tf_op jit(solution)/shard_map/ppermute | solution.py:811
  167.8 15.4 %collective-permute-start.37 = (bf16[192,512]{1,0:T(8,128)(2,1)S(1)}, bf16[192,512]{1,0:T(8,128)(2,1)S(1)}, u32[]{:S(2)}, u32[]{:S(2)}) collective-permute-start(bf16[192,512]{1,0:T(8,128)(2,1)S(1)} %get-tuple-element.113), channel_id=1, source_target_pairs={{0,16},{1,17},{2,18},{3,19},{4,20},{5,21},{6,22},{7,23},{8,24},{9,... | collective-permute-start | bytes 589832 | tf_op jit(solution)/shard_map/ppermute | solution.py:811
  170.6 12.6 %collective-permute-start.36 = (bf16[192,512]{1,0:T(8,128)(2,1)S(1)}, bf16[192,512]{1,0:T(8,128)(2,1)S(1)}, u32[]{:S(2)}, u32[]{:S(2)}) collective-permute-start(bf16[192,512]{1,0:T(8,128)(2,1)S(1)} %get-tuple-element.114), channel_id=1, source_target_pairs={{0,8},{1,9},{2,10},{3,11},{4,12},{5,13},{6,14},{7,15},{8,0},{9,1},... | collective-permute-start | bytes 589832 | tf_op jit(solution)/shard_map/ppermute | solution.py:811
  171.0 15.4 %collective-permute-start.38 = (bf16[192,512]{1,0:T(8,128)(2,1)S(1)}, bf16[192,512]{1,0:T(8,128)(2,1)S(1)}, u32[]{:S(2)}, u32[]{:S(2)}) collective-permute-start(bf16[192,512]{1,0:T(8,128)(2,1)S(1)} %get-tuple-element.103), channel_id=1, source_target_pairs={{0,24},{1,25},{2,26},{3,27},{4,28},{5,29},{6,30},{7,31},{8,16},{9,... | collective-permute-start | bytes 589832 | tf_op jit(solution)/shard_map/ppermute | solution.py:811
  (48 other events, 424.7 us)

commit v5 on v4

--- a/solution.py
+++ b/solution.py
@@ -300,12 +300,11 @@
 
 
 def forward_row(x_ref, code_ref, turned_ref, small_ref, outs, column_ref):
-    q_ref, k_ref, v_ref, h_ref, prob_ref, lse_ref, att_ref = outs
+    q_ref, k_ref, v_ref, prob_ref, lse_ref, att_ref = outs
     length = x_ref.shape[1]
     set_columns(code_ref, column_ref)
     normal, _ = norm(x_ref[0].astype(F32))
     h = (normal * small_ref[12:13, :] + small_ref[13:14, :]).astype(BF16)
-    h_ref[0] = h
     turned = dot(turned_ref[0:T_K, :], h, NT)
     q_ref[0] = (turned[0:D] * (HEAD**-0.5)).astype(BF16)
     logits = turned[T_R : T_R + 8]
@@ -340,13 +339,13 @@
 
 def forward_first(plan, gathered, count, place_ref, x_ref, code_ref, *refs):
     wins, refs = refs[:count], refs[count:]
-    outs, (turned_ref, small_ref), scratch = refs[:7], refs[7:9], refs[9:]
+    outs, (turned_ref, small_ref), scratch = refs[:6], refs[6:8], refs[8:]
     forward_prepare(plan, gathered, place_ref, wins, turned_ref, small_ref, scratch[1:])
     forward_row(x_ref, code_ref, turned_ref, small_ref, outs, scratch[0])
 
 
 def forward_next(place_ref, x_ref, code_ref, turned_ref, small_ref, *refs):
-    forward_row(x_ref, code_ref, turned_ref, small_ref, refs[7:14], refs[14])
+    forward_row(x_ref, code_ref, turned_ref, small_ref, refs[6:12], refs[12])
 
 
 def attention_forward(plan, gathered, place, x, code, row, before):
@@ -356,7 +355,6 @@
         (D, length, BF16),
         (length, HEAD, BF16),
         (length, HEAD, BF16),
-        (length, D, BF16),
         (8, length, F32),
         (8, length, F32),
         (D, length, F32),
@@ -381,9 +379,9 @@
         aliases = {}
     else:
         kernel = forward_next
-        operands = [place, x, code, *before[7:9], *before[:7]]
-        in_specs = in_specs + [whole(T_ALL, D), whole(SMALL, D)] + [ANYWHERE] * 7
-        aliases = {5 + i: i for i in range(7)}
+        operands = [place, x, code, *before[6:8], *before[:6]]
+        in_specs = in_specs + [whole(T_ALL, D), whole(SMALL, D)] + [ANYWHERE] * 6
+        aliases = {5 + i: i for i in range(6)}
     return pl.pallas_call(
         kernel,
         grid_spec=pltpu.PrefetchScalarGridSpec(
@@ -443,8 +441,11 @@
     x_ref, cot_ref, att_ref, prob_ref, experts_ref, small_ref = refs[:6]
     wins = refs[6 : 6 + count]
     hid_ref, mid_ref, dmid_ref, datt_ref, dlog_ref, inner_ref = refs[6 + count : 12 + count]
-    down_ref, gout_ref, gsmall_ref, gup_ref, gdown_ref = refs[12 + count : 17 + count]
-    packed, bias_ref = refs[17 + count : -13], refs[-13]
+    down_out_ref, gout_ref, gsmall_ref, gup_ref = refs[12 + count : 16 + count]
+    packed, gdown_ref = refs[16 + count : 18 + count], refs[18 + count]
+    if not pieces:
+        packed, gdown_ref = [], refs[16 + count]
+    bias_ref, down_ref, down_sem = refs[-15:-12]
     rows_ref, up_ref, flat_ref, tmp_ref, tmp2_ref, wide_ref = refs[-12:-6]
     tdown_ref, tup_ref, tout_ref, sem, sem2, pack_sem = refs[-6:]
 
@@ -465,6 +466,7 @@
                     c, pl.ds(j, D, stride=4), :
                 ].astype(BF16)
         end_rows(plan, ROW_D, ROW_S, down_ref, tmp2_ref, sem2)
+        pltpu.make_async_copy(down_ref, down_out_ref, down_sem.at[0]).start()
 
     amount = x_ref.shape[1]
     prob = prob_ref[0]
@@ -520,6 +522,7 @@
 
     @pl.when(last_step())
     def _():
+        pltpu.make_async_copy(down_ref, down_out_ref, down_sem.at[0]).wait()
         gdown_ref[...] = tdown_ref[...].astype(BF16)
         bias_ref[...] = jnp.concatenate([gsmall_ref[6:7, :], jnp.zeros((15, D), F32)]).astype(BF16)
         ins = [flat_ref, gdown_ref, bias_ref]
@@ -562,6 +565,8 @@
     wins = gathered.arrays(4)
     head = LATE_ROWS if pieces else FF
     packed = [kind(BF16, LANES // 2, PLANES - 1, plan.rows, D)] * 2 if pieces else []
+    plain = [] if pieces else [kind(BF16, FF, D)]
+    held = [pltpu.VMEM((FF, D), BF16)] if pieces else []
     return pl.pallas_call(
         partial(feed_kernel, plan, gathered, len(wins), pieces),
         grid_spec=pltpu.PrefetchScalarGridSpec(
@@ -583,15 +588,18 @@
                 column_block(D),
                 column_block(16),
                 column_block(8),
-                whole(FF, D),
+                ANYWHERE,
                 whole(D, D),
                 whole(8, D),
                 whole(head, D),
-                whole(FF, D),
             ]
+            + [whole(FF, D)] * len(plain)
             + [ANYWHERE] * len(packed),
-            scratch_shapes=[
+            scratch_shapes=held
+            + [
                 pltpu.VMEM((16, D), BF16),
+                pltpu.VMEM((FF, D), BF16),
+                pltpu.SemaphoreType.DMA((1,)),
                 pltpu.VMEM((ROW_D - ROW_O, D), BF16),
                 pltpu.VMEM((D, FF), BF16),
                 pltpu.VMEM((FF, D), BF16),
@@ -617,8 +625,8 @@
             kind(BF16, D, D),
             kind(F32, 8, D),
             kind(BF16, head, D),
-            kind(BF16, FF, D),
         ]
+        + plain
         + packed,
         cost_estimate=cost(50),
         compiler_params=params(60),
@@ -626,8 +634,8 @@
 
 
 def backward_kernel(pieces, place_ref, *refs):
-    x_ref, h_ref, q_ref, k_ref, v_ref, lse_ref, inner_ref, datt_ref, dlog_ref, code_ref = refs[:10]
-    turned_ref, gsmall_ref, gout_ref, gup_ref = refs[10:14]
+    x_ref, q_ref, k_ref, v_ref, lse_ref, inner_ref, datt_ref, dlog_ref, code_ref = refs[:9]
+    turned_ref, small_ref, gsmall_ref, gout_ref, gup_ref = refs[9:14]
     back_ref, ghead_ref, glow_ref = refs[14:17]
     packed = refs[17:-7]
     dk_ref, dv_ref, column_ref, total_ref, gain_ref, shift_ref, pack_sem = refs[-7:]
@@ -677,7 +685,8 @@
     back_ref[0, T_V:T_ALL, :] = dv_ref[...].T.astype(BF16)
     normal, _ = norm(x_ref[0].astype(F32))
     back = back_ref[0]
-    total_ref[...] += dot(back, h_ref[0], NN)
+    h = (normal * small_ref[12:13, :] + small_ref[13:14, :]).astype(BF16)
+    total_ref[...] += dot(back, h, NN)
     gain_ref[...] += dot(back, normal.astype(BF16), NN)
     shift_ref[...] += jnp.sum(back.astype(F32), axis=1, keepdims=True)
 
@@ -704,7 +713,7 @@
 
 
 def attention_backward(
-    plan, place, x, h, q, k, v, lse, inner, datt, dlog, code, turned, gsmall, gout, gup, pieces
+    plan, place, x, q, k, v, lse, inner, datt, dlog, code, turned, small, gsmall, gout, gup, pieces
 ):
     rows, length = x.shape[0], x.shape[1]
     row3 = lambda a, b: pl.BlockSpec((1, a, b), lambda i, *_: (i, 0, 0))
@@ -717,7 +726,6 @@
             grid=(rows,),
             in_specs=[
                 row3(length, D),
-                row3(length, D),
                 row3(D, length),
                 row3(length, HEAD),
                 row3(length, HEAD),
@@ -727,6 +735,7 @@
                 row3(16, length),
                 row3(1, length),
                 whole(T_ALL, D),
+                whole(SMALL, D),
                 whole(8, D),
                 whole(D, D),
                 whole(head, D),
@@ -751,7 +760,7 @@
         + packed,
         cost_estimate=cost(33),
         compiler_params=params(),
-    )(place, x, h, q, k, v, lse, inner, datt, dlog, code, turned, gsmall, gout, gup)
+    )(place, x, q, k, v, lse, inner, datt, dlog, code, turned, small, gsmall, gout, gup)
 
 
 def input_kernel(x_ref, dmid_ref, back_ref, turned_ref, small_ref, gx_ref):
@@ -997,10 +1006,9 @@
     window = make_window(plan, at, shard)
     staged = (planes, lanes, plan.lanes) == (PLANES, LANES, 659)
     main_pieces, head_pieces = [], []
-    first = place
+    waits = []
     if staged:
-        gathered, ready = gather_staged(plan, window, my_plane)
-        first = after(place, *ready)
+        gathered, waits = gather_staged(plan, window, my_plane)
         main_pieces = window_pieces(
             plan, range(LANES, ALL), [(ROW_U, ROW_D), (ROW_D, ROW_S), (ROW_S + 16, ROWS_ALL)], False
         )
@@ -1014,22 +1022,22 @@
     code = jnp.where(places < counts[:, None], segments, -1 - places)
     code = code.astype(F32).reshape(-1, 1, length)
     pairs = jnp.swapaxes(experts, 1, 2)
-    state = attention_forward(plan, gathered, first, x, code, 0, None)
-    turned, small = state[7:9]
+    state = attention_forward(plan, gathered, place, x, after(code, *waits), 0, None)
+    turned, small = state[6:8]
     for row in range(1, rows):
-        before = [*state[:7], turned, small]
+        before = [*state[:6], turned, small]
         state = attention_forward(plan, gathered, place, x, code, row, before)
-    q, k, v, h, prob, lse, att = state[:7]
-    hid, mid, dmid, datt, dlog, inner, down, gout, gsmall, gup, gdown, *packed = feed_forward(
+    q, k, v, prob, lse, att = state[:6]
+    hid, mid, dmid, datt, dlog, inner, down, gout, gsmall, gup, *packed = feed_forward(
         plan, gathered, place, counts, x, cot, att, prob, pairs, small, main_pieces
     )
-    third = place
+    third, gdown = place, packed[0]
     if staged:
         parts = core_sum(*packed)
         third = after(place, *parts)
         main = plane_swap(parts)
     back, ghead, glow, *packed = attention_backward(
-        plan, third, x, h, q, k, v, lse, inner, datt, dlog, code, turned, gsmall, gout, gup, head_pieces
+        plan, third, x, q, k, v, lse, inner, datt, dlog, code, turned, small, gsmall, gout, gup, head_pieces
     )
     if not staged:
         grads = plain_sum(plan, planes, lanes, me, at, ghead, gout, gup, gdown, glow)

time: 190 us -> 188 us (0.989)
  no operation moved by 1% of the time
where the time goes in v5:
time: 188 us
  Pallas kernels  110 us (59%)
  starting transfers between devices  34.6 us (18%)
  waiting for transfers between devices  31.5 us (17%)
  other arithmetic  7.61 us (4%)
  local copies, waits for them, and re-layouts  2.48 us (1%)
    pallas_call x1, Pallas kernels, feed_forward(): pl.pallas_call(partial(feed_kernel, plan, gathered, len(wins), pieces), g...  44.6 us
    ppermute x39, starting transfers between devices, move(): return lax.ppermute(value, AXES, pairs)  34.6 us
    ppermute x39, waiting for transfers between devices, move(): return lax.ppermute(value, AXES, pairs)  31.5 us
    pallas_call x1, Pallas kernels, attention_backward(): pl.pallas_call(partial(backward_kernel, pieces), grid_spec=pltpu.Prefetch...  23.4 us
    pallas_call x2, Pallas kernels, attention_forward(): pl.pallas_call(kernel, grid_spec=pltpu.PrefetchScalarGridSpec(num_scalar_...  20.4 us
    pallas_call x1, Pallas kernels, layer_output(): pl.pallas_call(output_kernel, grid_spec=pltpu.PrefetchScalarGridSpec(num_...  10.1 us
    pallas_call x1, Pallas kernels, input_grad(): pl.pallas_call(input_kernel, grid=(rows, length // TB), in_specs=[row_blo...  7.72 us
  transfers between devices with their start and end apart: 39, of which 11 were waited for; matrix products, arithmetic and copies ran while one was open for 2% of the time, Pallas kernels for 33%

profile of v5, /device:TPU:0, one launch (start us, length us, event | category | flops | bytes accessed | tf_op | source)
XLA Modules:
  0.0 187.6 jit_solution(15846778898574067828)
XLA Ops:
  0.7 1.7 shard_map.85.refs_0_.refs_6_
  2.4 3.9 %collective-permute-start.3 = (bf16[192,512]{1,0:T(8,128)(2,1)}, bf16[192,512]{1,0:T(8,128)(2,1)S(1)}, u32[]{:S(2)}, u32[]{:S(2)}) collective-permute-start(bf16[192,512]{1,0:T(8,128)(2,1)} %shard_map.85.refs_0_.refs_6_), channel_id=1, source_target_pairs={{0,6},{1,7},{2,4},{3,5},{4,2},{5,3},{6,0},{7,1},{8,14},{9,15},{10,... | collective-permute-start | bytes 589832 | tf_op jit(solution)/shard_map/ppermute | solution.py:820
  6.3 3.6 %collective-permute-start.2 = (bf16[192,512]{1,0:T(8,128)(2,1)}, bf16[192,512]{1,0:T(8,128)(2,1)S(1)}, u32[]{:S(2)}, u32[]{:S(2)}) collective-permute-start(bf16[192,512]{1,0:T(8,128)(2,1)} %shard_map.85.refs_0_.refs_6_), channel_id=1, source_target_pairs={{0,24},{1,25},{2,26},{3,27},{4,28},{5,29},{6,30},{7,31},{8,16},{9,... | collective-permute-start | bytes 589832 | tf_op jit(solution)/shard_map/ppermute | solution.py:820
  11.4 1.7 collective-permute-start.6
  13.1 3.1 %collective-permute-done.2 = bf16[192,512]{1,0:T(8,128)(2,1)S(1)} collective-permute-done((bf16[192,512]{1,0:T(8,128)(2,1)}, bf16[192,512]{1,0:T(8,128)(2,1)S(1)}, u32[]{:S(2)}, u32[]{:S(2)}) %collective-permute-start.2) | collective-permute-done | bytes 196640 | tf_op jit(solution)/shard_map/ppermute | solution.py:820
  16.2 10.3 %collective-permute-done.1 = bf16[192,512]{1,0:T(8,128)(2,1)S(1)} collective-permute-done((bf16[192,512]{1,0:T(8,128)(2,1)}, bf16[192,512]{1,0:T(8,128)(2,1)S(1)}, u32[]{:S(2)}, u32[]{:S(2)}) %collective-permute-start.1) | collective-permute-done | bytes 196640 | tf_op jit(solution)/shard_map/ppermute | solution.py:820
  28.5 1.5 collective-permute-start.14
  30.1 1.5 collective-permute-start.12
  34.3 5.9 %collective-permute-done.4.refs_28_ = bf16[192,512]{1,0:T(8,128)(2,1)S(1)} collective-permute-done((bf16[192,512]{1,0:T(8,128)(2,1)S(1)}, bf16[192,512]{1,0:T(8,128)(2,1)S(1)}, u32[]{:S(2)}, u32[]{:S(2)}) %collective-permute-start.4) | collective-permute-done | bytes 196640 | tf_op jit(solution)/shard_map/ppermute | solution.py:820
  45.8 11.0 %shard_map.86 = (bf16[2,512,1024]{2,1,0:T(8,128)(2,1)}, bf16[2,1024,64]{2,1,0:T(8,128)(2,1)}, bf16[2,1024,64]{2,1,0:T(8,128)(2,1)}, f32[2,8,1024]{2,1,0:T(8,128)...) custom-call(s32[2]{0:T(128)} %pad_add_fusion.place_ref, ...), custom_call_target="tpu_custom_call" | custom-call | flops 15399999488 | bytes 1400000 | tf_op jit(solution)/shard_map/pallas_call | solution.py:385
  58.9 9.3 %shard_map.87 = (bf16[2,512,1024]{2,1,0:T(8,128)(2,1)}, bf16[2,1024,64]{2,1,0:T(8,128)(2,1)}, bf16[2,1024,64]{2,1,0:T(8,128)(2,1)}, f32[2,8,1024]{2,1,0:T(8,128)...) custom-call(s32[2]{0:T(128)} %pad_add_fusion.place_ref, ...), custom_call_target="tpu_custom_call", output_to_operand_aliasing={{0}: (5, {}), {1}: (6, {}), {2}: (7, {}), {3}: (8, {}), {4}... | custom-call | flops 15399999488 | bytes 1400000 | tf_op jit(solution)/shard_map/pallas_call | solution.py:385
  69.5 44.6 %shard_map.88 = (bf16[2,1024,2048]{2,1,0:T(8,128)(2,1)}, f32[2,1024,512]{2,1,0:T(8,128)}, f32[2,1024,512]{2,1,0:T(8,128)}, bf16[2,512,1024]{2,1,0:T(8,128)(2,1)}...) custom-call(s32[2]{0:T(128)} %pad_add_fusion.place_ref, ...), custom_call_target="tpu_custom_call" | custom-call | flops 54999998464 | bytes 5000000 | tf_op jit(solution)/shard_map/pallas_call | solution.py:570
  114.3 4.6 %collective-permute-done.28 = bf16[4,3,192,512]{3,2,1,0:T(8,128)(2,1)S(1)} collective-permute-done((bf16[4,3,192,512]{3,2,1,0:T(8,128)(2,1)}, bf16[4,3,192,512]{3,2,1,0:T(8,128)(2,1)S(1)}, u32[]{:S(2)}, u32[]{:S(2)}) %collective-permute-start.28) | collective-permute-done | bytes 2359328 | tf_op jit(solution)/shard_map/ppermute | solution.py:820
  118.9 3.2 %fusion.3 = (bf16[3,192,512]{2,1,0:T(8,128)(2,1)}, bf16[3,192,512]{2,1,0:T(8,128)(2,1)S(1)}, bf16[3,192,512]{2,1,0:T(8,128)(2,1)S(1)}, bf16[3,192,512]{2,1,0:T(8,128)(2,1)S(1)}) fusion(bf16[4,3,192,512]{3,2,1,0:T(8,128)(2,1)S(1)} %collective-permute-done.28, bf16[4,3,192,512]{3,2,1,0:T(8,128)(2,1)} %get-tuple-element.66), kind=kLoop, calls=%fused_computation.8 | loop fusion | flops 4718592 | bytes 7077888 | tf_op jit(solution)/shard_map/convert_element_type | solution.py:930
  122.1 1.8 collective-permute-start.31
  125.6 23.4 %shard_map.89 = (bf16[2,656,1024]{2,1,0:T(8,128)(2,1)}, bf16[640,512]{1,0:T(8,128)(2,1)}, bf16[32,512]{1,0:T(8,128)(2,1)}, bf16[4,1,192,512]{3,2,1,0:T(8,128)(2,1)}, bf16[4,1,192,512]{3,2,1,0:T(8,128)(2,1)}) custom-call(s32[2]{0:T(128)} %pad_add_fusion.place_ref, bf16[2,1024,512]{2,1,0:T(8,128)(2,1)} %x_ref.5, ...), custom_call_target="tpu_custom_call" | custom-call | flops 36300001280 | bytes 3300000 | tf_op jit(solution)/shard_map/pallas_call | solution.py:722
  149.1 2.2 %collective-permute-done.30 = bf16[3,192,512]{2,1,0:T(8,128)(2,1)} collective-permute-done((bf16[3,192,512]{2,1,0:T(8,128)(2,1)S(1)}, bf16[3,192,512]{2,1,0:T(8,128)(2,1)}, u32[]{:S(2)}, u32[]{:S(2)}) %collective-permute-start.30) | collective-permute-done | bytes 589856 | tf_op jit(solution)/shard_map/ppermute | solution.py:820
  151.5 1.7 add_convert_fusion
  157.0 7.7 %shard_map.90 = bf16[2,1024,512]{2,1,0:T(8,128)(2,1)} custom-call(bf16[2,1024,512]{2,1,0:T(8,128)(2,1)} %x_ref.5, f32[2,1024,512]{2,1,0:T(8,128)} %get-tuple-element.85.dmid_ref, bf16[2,656,1024]{2,1,0:T(8,128)(2,1)} %get-tuple-element.87.back_ref, bf16[656,512]{1,0:T(8,128)(2,1)} %get-tuple-element.55.turned_ref.refs_9_, ...), custom_call_target="tpu_custom_call" | custom-call | flops 8800000000 | bytes 800000 | tf_op jit(solution)/shard_map/pallas_call | solution.py:774
  166.4 2.6 %collective-permute-start.37 = (bf16[192,512]{1,0:T(8,128)(2,1)S(1)}, bf16[192,512]{1,0:T(8,128)(2,1)S(1)}, u32[]{:S(2)}, u32[]{:S(2)}) collective-permute-start(bf16[192,512]{1,0:T(8,128)(2,1)S(1)} %get-tuple-element.109), channel_id=1, source_target_pairs={{0,16},{1,17},{2,18},{3,19},{4,20},{5,21},{6,22},{7,23},{8,24},{9,... | collective-permute-start | bytes 589832 | tf_op jit(solution)/shard_map/ppermute | solution.py:820
  169.4 2.1 %collective-permute-start.38 = (bf16[192,512]{1,0:T(8,128)(2,1)S(1)}, bf16[192,512]{1,0:T(8,128)(2,1)S(1)}, u32[]{:S(2)}, u32[]{:S(2)}) collective-permute-start(bf16[192,512]{1,0:T(8,128)(2,1)S(1)} %get-tuple-element.99), channel_id=1, source_target_pairs={{0,24},{1,25},{2,26},{3,27},{4,28},{5,29},{6,30},{7,31},{8,16},{9,... | collective-permute-start | bytes 589832 | tf_op jit(solution)/shard_map/ppermute | solution.py:820
  171.5 10.1 %shard_map.91 = bf16[2,1024,512]{2,1,0:T(8,128)(2,1)} custom-call(s32[2]{0:T(128)} %counts_ref.3, f32[2,1024,512]{2,1,0:T(8,128)} %get-tuple-element.92.mid_ref, bf16[2,1024,2048]{2,1,0:T(8,128)(2,1)} %get-tuple-element.93.hid_ref, f32[32,512]{1,0:T(8,128)} %get-tuple-element.56.small_ref.refs_5_.refs_10_, bf16[2048,512]{1,0:T(8,128)(2,1)} %get-tuple-element.94.down_ref), custom_call_target="tpu_custom_call" | custom-call | flops 9900000256 | bytes 900000 | tf_op jit(solution)/shard_map/pallas_call | solution.py:799
  181.7 3.1 %collective-permute-done.38.refs_3_ = bf16[192,512]{1,0:T(8,128)(2,1)S(1)} collective-permute-done((bf16[192,512]{1,0:T(8,128)(2,1)S(1)}, bf16[192,512]{1,0:T(8,128)(2,1)S(1)}, u32[]{:S(2)}, u32[]{:S(2)}) %collective-permute-start.38) | collective-permute-done | bytes 196640 | tf_op jit(solution)/shard_map/ppermute | solution.py:820
  185.5 2.1 %shard_map.92 = f32[659,128]{1,0:T(8,128)} custom-call(s32[1]{0:T(128)} %bitcast.2.at_ref, bf16[192,512]{1,0:T(8,128)(2,1)} %get-tuple-element.95.refs_0_, bf16[192,512]{1,0:T(8,128)(2,1)} %copy-done.4, bf16[192,512]{1,0:T(8,128)(2,1)} %copy-done.3, bf16[192,512]{1,0:T(8,128)(2,1)} %copy-done.5), custom_call_target="tpu_custom_call" | custom-call | tf_op jit(solution)/shard_map/pallas_call | solution.py:974
  (145 shorter events, 23.3 us)
Async XLA Ops:
  9.9 16.6 %collective-permute-start.1 = (bf16[192,512]{1,0:T(8,128)(2,1)}, bf16[192,512]{1,0:T(8,128)(2,1)S(1)}, u32[]{:S(2)}, u32[]{:S(2)}) collective-permute-start(bf16[192,512]{1,0:T(8,128)(2,1)} %shard_map.85.refs_0_.refs_6_), channel_id=1, source_target_pairs={{0,16},{1,17},{2,18},{3,19},{4,20},{5,21},{6,22},{7,23},{8,24},{9,... | collective-permute-start | bytes 589832 | tf_op jit(solution)/shard_map/ppermute | solution.py:820
  9.9 16.6 %collective-permute-start = (bf16[192,512]{1,0:T(8,128)(2,1)}, bf16[192,512]{1,0:T(8,128)(2,1)S(1)}, u32[]{:S(2)}, u32[]{:S(2)}) collective-permute-start(bf16[192,512]{1,0:T(8,128)(2,1)} %shard_map.85.refs_0_.refs_6_), channel_id=1, source_target_pairs={{0,8},{1,9},{2,10},{3,11},{4,12},{5,13},{6,14},{7,15},{8,0},{9,1},... | collective-permute-start | bytes 589832 | tf_op jit(solution)/shard_map/ppermute | solution.py:820
  10.7 16.7 %collective-permute-start.8 = (bf16[192,512]{1,0:T(8,128)(2,1)}, bf16[192,512]{1,0:T(8,128)(2,1)S(1)}, u32[]{:S(2)}, u32[]{:S(2)}) collective-permute-start(bf16[192,512]{1,0:T(8,128)(2,1)} %shard_map.85.refs_0_.refs_6_), channel_id=1, source_target_pairs={{0,4},{1,5},{2,6},{3,7},{4,0},{5,1},{6,2},{7,3},{8,12},{9,13},{10,... | collective-permute-start | bytes 589832 | tf_op jit(solution)/shard_map/ppermute | solution.py:820
  11.4 16.1 %collective-permute-start.6 = (bf16[192,512]{1,0:T(8,128)(2,1)}, bf16[192,512]{1,0:T(8,128)(2,1)S(1)}, u32[]{:S(2)}, u32[]{:S(2)}) collective-permute-start(bf16[192,512]{1,0:T(8,128)(2,1)} %shard_map.85.refs_0_.refs_6_), channel_id=1, source_target_pairs={{0,2},{1,3},{2,0},{3,1},{4,6},{5,7},{6,4},{7,5},{8,10},{9,11},{10,... | collective-permute-start | bytes 589832 | tf_op jit(solution)/shard_map/ppermute | solution.py:820
  16.2 13.9 %collective-permute-start.5 = (bf16[192,512]{1,0:T(8,128)(2,1)}, bf16[192,512]{1,0:T(8,128)(2,1)S(1)}, u32[]{:S(2)}, u32[]{:S(2)}) collective-permute-start(bf16[192,512]{1,0:T(8,128)(2,1)} %shard_map.85.refs_0_.refs_6_), channel_id=1, source_target_pairs={{0,1},{1,0},{2,3},{3,2},{4,5},{5,4},{6,7},{7,6},{8,9},{9,8},{10,11... | collective-permute-start | bytes 589832 | tf_op jit(solution)/shard_map/ppermute | solution.py:820
  28.0 12.2 %collective-permute-start.16 = (bf16[224,512]{1,0:T(8,128)(2,1)S(1)}, bf16[224,512]{1,0:T(8,128)(2,1)S(1)}, u32[]{:S(2)}, u32[]{:S(2)}) collective-permute-start(bf16[224,512]{1,0:T(8,128)(2,1)S(1)} %pad_maximum_fusion.1.refs_8_.refs_14_), channel_id=1, source_target_pairs={{0,6},{1,7},{2,4},{3,5},{4,2},{5,3},{6,0},{7,1},{8,14},{9,15},{10,... | collective-permute-start | bytes 688136 | tf_op jit(solution)/shard_map/ppermute | solution.py:820
  28.5 12.2 %collective-permute-start.14 = (bf16[224,512]{1,0:T(8,128)(2,1)S(1)}, bf16[224,512]{1,0:T(8,128)(2,1)S(1)}, u32[]{:S(2)}, u32[]{:S(2)}) collective-permute-start(bf16[224,512]{1,0:T(8,128)(2,1)S(1)} %pad_maximum_fusion.1.refs_8_.refs_14_), channel_id=1, source_target_pairs={{0,4},{1,5},{2,6},{3,7},{4,0},{5,1},{6,2},{7,3},{8,12},{9,13},{10,... | collective-permute-start | bytes 688136 | tf_op jit(solution)/shard_map/ppermute | solution.py:820
  30.1 10.8 %collective-permute-start.12 = (bf16[224,512]{1,0:T(8,128)(2,1)S(1)}, bf16[224,512]{1,0:T(8,128)(2,1)S(1)}, u32[]{:S(2)}, u32[]{:S(2)}) collective-permute-start(bf16[224,512]{1,0:T(8,128)(2,1)S(1)} %pad_maximum_fusion.1.refs_8_.refs_14_), channel_id=1, source_target_pairs={{0,2},{1,3},{2,0},{3,1},{4,6},{5,7},{6,4},{7,5},{8,10},{9,11},{10,... | collective-permute-start | bytes 688136 | tf_op jit(solution)/shard_map/ppermute | solution.py:820
  41.9 16.5 %collective-permute-start.21 = (bf16[2,192,512]{2,1,0:T(8,128)(2,1)S(1)}, bf16[2,192,512]{2,1,0:T(8,128)(2,1)S(1)}, u32[]{:S(2)}, u32[]{:S(2)}) collective-permute-start(bf16[2,192,512]{2,1,0:T(8,128)(2,1)S(1)} %pad_maximum_fusion.refs_22_), channel_id=1, source_target_pairs={{0,4},{1,5},{2,6},{3,7},{4,0},{5,1},{6,2},{7,3},{8,12},{9,13},{10,... | collective-permute-start | bytes 1179656 | tf_op jit(solution)/shard_map/ppermute | solution.py:820
  43.2 15.3 %collective-permute-start.19 = (bf16[2,192,512]{2,1,0:T(8,128)(2,1)S(1)}, bf16[2,192,512]{2,1,0:T(8,128)(2,1)S(1)}, u32[]{:S(2)}, u32[]{:S(2)}) collective-permute-start(bf16[2,192,512]{2,1,0:T(8,128)(2,1)S(1)} %pad_maximum_fusion.refs_22_), channel_id=1, source_target_pairs={{0,2},{1,3},{2,0},{3,1},{4,6},{5,7},{6,4},{7,5},{8,10},{9,11},{10,... | collective-permute-start | bytes 1179656 | tf_op jit(solution)/shard_map/ppermute | solution.py:820
  43.7 24.6 %collective-permute-start.18 = (bf16[2,192,512]{2,1,0:T(8,128)(2,1)S(1)}, bf16[2,192,512]{2,1,0:T(8,128)(2,1)S(1)}, u32[]{:S(2)}, u32[]{:S(2)}) collective-permute-start(bf16[2,192,512]{2,1,0:T(8,128)(2,1)S(1)} %pad_maximum_fusion.refs_22_), channel_id=1, source_target_pairs={{0,1},{1,0},{2,3},{3,2},{4,5},{5,4},{6,7},{7,6},{8,9},{9,8},{10,11... | collective-permute-start | bytes 1179656 | tf_op jit(solution)/shard_map/ppermute | solution.py:820
  43.8 14.1 %collective-permute-start.24 = (bf16[192,512]{1,0:T(8,128)(2,1)S(1)}, bf16[192,512]{1,0:T(8,128)(2,1)S(1)}, u32[]{:S(2)}, u32[]{:S(2)}) collective-permute-start(bf16[192,512]{1,0:T(8,128)(2,1)S(1)} %collective-permute-done.3.refs_6_.refs_12_), channel_id=1, source_target_pairs={{16,0},{17,1},{18,2},{19,3},{20,4},{21,5},{22,6},{23,7},{24,8},{25... | collective-permute-start | bytes 589832 | tf_op jit(solution)/shard_map/ppermute | solution.py:820
  45.1 12.9 %collective-permute-start.27 = (bf16[192,512]{1,0:T(8,128)(2,1)S(1)}, bf16[192,512]{1,0:T(8,128)(2,1)S(1)}, u32[]{:S(2)}, u32[]{:S(2)}) collective-permute-start(bf16[192,512]{1,0:T(8,128)(2,1)S(1)} %collective-permute-done.26.refs_32_), channel_id=1, source_target_pairs={{0,1},{1,0},{2,3},{3,2},{4,5},{5,4},{6,7},{7,6},{8,9},{9,8},{10,11... | collective-permute-start | bytes 589832 | tf_op jit(solution)/shard_map/ppermute | solution.py:820
  57.9 10.4 %collective-permute-start.23 = (bf16[192,512]{1,0:T(8,128)(2,1)S(1)}, bf16[192,512]{1,0:T(8,128)(2,1)S(1)}, u32[]{:S(2)}, u32[]{:S(2)}) collective-permute-start(bf16[192,512]{1,0:T(8,128)(2,1)S(1)} %collective-permute-done.4.refs_28_), channel_id=1, source_target_pairs={{0,1},{1,0},{2,3},{3,2},{4,5},{5,4},{6,7},{7,6},{8,9},{9,8},{10,11... | collective-permute-start | bytes 589832 | tf_op jit(solution)/shard_map/ppermute | solution.py:820
  58.0 10.3 %collective-permute-start.25 = (bf16[192,512]{1,0:T(8,128)(2,1)S(1)}, bf16[192,512]{1,0:T(8,128)(2,1)S(1)}, u32[]{:S(2)}, u32[]{:S(2)}) collective-permute-start(bf16[192,512]{1,0:T(8,128)(2,1)S(1)} %collective-permute-done.24.refs_30_), channel_id=1, source_target_pairs={{0,1},{1,0},{2,3},{3,2},{4,5},{5,4},{6,7},{7,6},{8,9},{9,8},{10,11... | collective-permute-start | bytes 589832 | tf_op jit(solution)/shard_map/ppermute | solution.py:820
  58.4 9.9 %collective-permute-start.22 = (bf16[2,192,512]{2,1,0:T(8,128)(2,1)S(1)}, bf16[2,192,512]{2,1,0:T(8,128)(2,1)S(1)}, u32[]{:S(2)}, u32[]{:S(2)}) collective-permute-start(bf16[2,192,512]{2,1,0:T(8,128)(2,1)S(1)} %collective-permute-done.21.refs_26_), channel_id=1, source_target_pairs={{0,1},{1,0},{2,3},{3,2},{4,5},{5,4},{6,7},{7,6},{8,9},{9,8},{10,11... | collective-permute-start | bytes 1179656 | tf_op jit(solution)/shard_map/ppermute | solution.py:820
  122.1 27.0 %collective-permute-start.31 = (bf16[3,192,512]{2,1,0:T(8,128)(2,1)}, bf16[3,192,512]{2,1,0:T(8,128)(2,1)}, u32[]{:S(2)}, u32[]{:S(2)}) collective-permute-start(bf16[3,192,512]{2,1,0:T(8,128)(2,1)} %get-tuple-element.101), channel_id=1, source_target_pairs={{0,6},{1,7},{2,4},{3,5},{4,2},{5,3},{6,0},{7,1},{8,14},{9,15},{10,... | collective-permute-start | bytes 1769480 | tf_op jit(solution)/shard_map/ppermute | solution.py:820
  123.9 27.4 %collective-permute-start.30 = (bf16[3,192,512]{2,1,0:T(8,128)(2,1)S(1)}, bf16[3,192,512]{2,1,0:T(8,128)(2,1)}, u32[]{:S(2)}, u32[]{:S(2)}) collective-permute-start(bf16[3,192,512]{2,1,0:T(8,128)(2,1)S(1)} %get-tuple-element.102), channel_id=1, source_target_pairs={{0,4},{1,5},{2,6},{3,7},{4,0},{5,1},{6,2},{7,3},{8,12},{9,13},{10,... | collective-permute-start | bytes 1769480 | tf_op jit(solution)/shard_map/ppermute | solution.py:820
  125.0 26.4 %collective-permute-start.29 = (bf16[3,192,512]{2,1,0:T(8,128)(2,1)S(1)}, bf16[3,192,512]{2,1,0:T(8,128)(2,1)}, u32[]{:S(2)}, u32[]{:S(2)}) collective-permute-start(bf16[3,192,512]{2,1,0:T(8,128)(2,1)S(1)} %get-tuple-element.103), channel_id=1, source_target_pairs={{0,2},{1,3},{2,0},{3,1},{4,6},{5,7},{6,4},{7,5},{8,10},{9,11},{10,... | collective-permute-start | bytes 1769480 | tf_op jit(solution)/shard_map/ppermute | solution.py:820
  153.5 11.3 %collective-permute-start.35 = (bf16[192,512]{1,0:T(8,128)(2,1)S(1)}, bf16[192,512]{1,0:T(8,128)(2,1)S(1)}, u32[]{:S(2)}, u32[]{:S(2)}) collective-permute-start(bf16[192,512]{1,0:T(8,128)(2,1)S(1)} %get-tuple-element.105), channel_id=1, source_target_pairs={{0,6},{1,7},{2,4},{3,5},{4,2},{5,3},{6,0},{7,1},{8,14},{9,15},{10,... | collective-permute-start | bytes 589832 | tf_op jit(solution)/shard_map/ppermute | solution.py:820
  154.9 10.4 %collective-permute-start.34 = (bf16[192,512]{1,0:T(8,128)(2,1)S(1)}, bf16[192,512]{1,0:T(8,128)(2,1)S(1)}, u32[]{:S(2)}, u32[]{:S(2)}) collective-permute-start(bf16[192,512]{1,0:T(8,128)(2,1)S(1)} %get-tuple-element.106), channel_id=1, source_target_pairs={{0,4},{1,5},{2,6},{3,7},{4,0},{5,1},{6,2},{7,3},{8,12},{9,13},{10,... | collective-permute-start | bytes 589832 | tf_op jit(solution)/shard_map/ppermute | solution.py:820
  166.4 15.2 %collective-permute-start.37 = (bf16[192,512]{1,0:T(8,128)(2,1)S(1)}, bf16[192,512]{1,0:T(8,128)(2,1)S(1)}, u32[]{:S(2)}, u32[]{:S(2)}) collective-permute-start(bf16[192,512]{1,0:T(8,128)(2,1)S(1)} %get-tuple-element.109), channel_id=1, source_target_pairs={{0,16},{1,17},{2,18},{3,19},{4,20},{5,21},{6,22},{7,23},{8,24},{9,... | collective-permute-start | bytes 589832 | tf_op jit(solution)/shard_map/ppermute | solution.py:820
  169.0 12.6 %collective-permute-start.36 = (bf16[192,512]{1,0:T(8,128)(2,1)S(1)}, bf16[192,512]{1,0:T(8,128)(2,1)S(1)}, u32[]{:S(2)}, u32[]{:S(2)}) collective-permute-start(bf16[192,512]{1,0:T(8,128)(2,1)S(1)} %get-tuple-element.110), channel_id=1, source_target_pairs={{0,8},{1,9},{2,10},{3,11},{4,12},{5,13},{6,14},{7,15},{8,0},{9,1},... | collective-permute-start | bytes 589832 | tf_op jit(solution)/shard_map/ppermute | solution.py:820
  169.4 15.4 %collective-permute-start.38 = (bf16[192,512]{1,0:T(8,128)(2,1)S(1)}, bf16[192,512]{1,0:T(8,128)(2,1)S(1)}, u32[]{:S(2)}, u32[]{:S(2)}) collective-permute-start(bf16[192,512]{1,0:T(8,128)(2,1)S(1)} %get-tuple-element.99), channel_id=1, source_target_pairs={{0,24},{1,25},{2,26},{3,27},{4,28},{5,29},{6,30},{7,31},{8,16},{9,... | collective-permute-start | bytes 589832 | tf_op jit(solution)/shard_map/ppermute | solution.py:820
  (48 other events, 422.3 us)

commit v6 on v5

--- a/solution.py
+++ b/solution.py
@@ -334,7 +334,7 @@
                 lse_ref[0, head : head + 1, pl.ds(q0, QB)] = total[:, part]
         return carry
 
-    lax.fori_loop(0, length // QB, block_step, 0, unroll=2)
+    lax.fori_loop(0, length // QB, block_step, 0, unroll=4)
 
 
 def forward_first(plan, gathered, count, place_ref, x_ref, code_ref, *refs):
@@ -679,7 +679,7 @@
         dv_ref[pl.ds(w0, KB), :] += dv
         return carry
 
-    lax.fori_loop(0, length // QB, block_step, 0, unroll=2)
+    lax.fori_loop(0, length // QB, block_step, 0, unroll=4)
     back_ref[0, T_R:T_K, :] = dlog_ref[0]
     back_ref[0, T_K:T_V, :] = dk_ref[...].T.astype(BF16)
     back_ref[0, T_V:T_ALL, :] = dv_ref[...].T.astype(BF16)

time: 188 us -> 188 us (level)
  transfers between devices with their start and end apart: 39 -> 39, of which waited for: 11 -> 11; matrix products, arithmetic and copies ran while one was open for 2% -> 2% of each run, Pallas kernels for 33% -> 32%
where the time goes in v6:
time: 188 us; the launch traced here: 187 us
  Pallas kernels  109 us (58%)
  starting transfers between devices  34.3 us (18%)
  waiting for transfers between devices  32.3 us (17%)
  other arithmetic  7.61 us (4%)
  local copies, waits for them, and re-layouts  2.48 us (1%)
    pallas_call x1, Pallas kernels, feed_forward(): pl.pallas_call(partial(feed_kernel, plan, gathered, len(wins), pieces), g...  44.7 us
    ppermute x39, starting transfers between devices, move(): return lax.ppermute(value, AXES, pairs)  34.3 us
    ppermute x39, waiting for transfers between devices, move(): return lax.ppermute(value, AXES, pairs)  32.3 us
    pallas_call x1, Pallas kernels, attention_backward(): pl.pallas_call(partial(backward_kernel, pieces), grid_spec=pltpu.Prefetch...  22.9 us
    pallas_call x2, Pallas kernels, attention_forward(): pl.pallas_call(kernel, grid_spec=pltpu.PrefetchScalarGridSpec(num_scalar_...  19.8 us
    pallas_call x1, Pallas kernels, layer_output(): pl.pallas_call(output_kernel, grid_spec=pltpu.PrefetchScalarGridSpec(num_...  10.1 us
    pallas_call x1, Pallas kernels, input_grad(): pl.pallas_call(input_kernel, grid=(rows, length // TB), in_specs=[row_blo...  7.72 us
  transfers between devices with their start and end apart: 39, of which 11 were waited for; matrix products, arithmetic and copies ran while one was open for 2% of the time, Pallas kernels for 32%

profile of v6, /device:TPU:0, one launch (start us, length us, event | category | flops | bytes accessed | tf_op | source)
XLA Modules:
  0.0 187.0 jit_solution(10530872576870039946)
XLA Ops:
  0.7 1.7 shard_map.85.refs_0_.refs_6_
  2.4 3.9 %collective-permute-start.3 = (bf16[192,512]{1,0:T(8,128)(2,1)}, bf16[192,512]{1,0:T(8,128)(2,1)S(1)}, u32[]{:S(2)}, u32[]{:S(2)}) collective-permute-start(bf16[192,512]{1,0:T(8,128)(2,1)} %shard_map.85.refs_0_.refs_6_), channel_id=1, source_target_pairs={{0,6},{1,7},{2,4},{3,5},{4,2},{5,3},{6,0},{7,1},{8,14},{9,15},{10,... | collective-permute-start | bytes 589832 | tf_op jit(solution)/shard_map/ppermute | solution.py:820
  6.3 3.6 %collective-permute-start.2 = (bf16[192,512]{1,0:T(8,128)(2,1)}, bf16[192,512]{1,0:T(8,128)(2,1)S(1)}, u32[]{:S(2)}, u32[]{:S(2)}) collective-permute-start(bf16[192,512]{1,0:T(8,128)(2,1)} %shard_map.85.refs_0_.refs_6_), channel_id=1, source_target_pairs={{0,24},{1,25},{2,26},{3,27},{4,28},{5,29},{6,30},{7,31},{8,16},{9,... | collective-permute-start | bytes 589832 | tf_op jit(solution)/shard_map/ppermute | solution.py:820
  11.4 1.7 collective-permute-start.6
  13.1 3.1 %collective-permute-done.2 = bf16[192,512]{1,0:T(8,128)(2,1)S(1)} collective-permute-done((bf16[192,512]{1,0:T(8,128)(2,1)}, bf16[192,512]{1,0:T(8,128)(2,1)S(1)}, u32[]{:S(2)}, u32[]{:S(2)}) %collective-permute-start.2) | collective-permute-done | bytes 196640 | tf_op jit(solution)/shard_map/ppermute | solution.py:820
  16.2 10.3 %collective-permute-done.1 = bf16[192,512]{1,0:T(8,128)(2,1)S(1)} collective-permute-done((bf16[192,512]{1,0:T(8,128)(2,1)}, bf16[192,512]{1,0:T(8,128)(2,1)S(1)}, u32[]{:S(2)}, u32[]{:S(2)}) %collective-permute-start.1) | collective-permute-done | bytes 196640 | tf_op jit(solution)/shard_map/ppermute | solution.py:820
  28.5 1.5 collective-permute-start.14
  30.1 1.5 collective-permute-start.12
  34.3 5.9 %collective-permute-done.4.refs_28_ = bf16[192,512]{1,0:T(8,128)(2,1)S(1)} collective-permute-done((bf16[192,512]{1,0:T(8,128)(2,1)S(1)}, bf16[192,512]{1,0:T(8,128)(2,1)S(1)}, u32[]{:S(2)}, u32[]{:S(2)}) %collective-permute-start.4) | collective-permute-done | bytes 196640 | tf_op jit(solution)/shard_map/ppermute | solution.py:820
  45.8 10.7 %shard_map.86 = (bf16[2,512,1024]{2,1,0:T(8,128)(2,1)}, bf16[2,1024,64]{2,1,0:T(8,128)(2,1)}, bf16[2,1024,64]{2,1,0:T(8,128)(2,1)}, f32[2,8,1024]{2,1,0:T(8,128)...) custom-call(s32[2]{0:T(128)} %pad_add_fusion.place_ref, ...), custom_call_target="tpu_custom_call" | custom-call | flops 15399999488 | bytes 1400000 | tf_op jit(solution)/shard_map/pallas_call | solution.py:385
  58.9 9.0 %shard_map.87 = (bf16[2,512,1024]{2,1,0:T(8,128)(2,1)}, bf16[2,1024,64]{2,1,0:T(8,128)(2,1)}, bf16[2,1024,64]{2,1,0:T(8,128)(2,1)}, f32[2,8,1024]{2,1,0:T(8,128)...) custom-call(s32[2]{0:T(128)} %pad_add_fusion.place_ref, ...), custom_call_target="tpu_custom_call", output_to_operand_aliasing={{0}: (5, {}), {1}: (6, {}), {2}: (7, {}), {3}: (8, {}), {4}... | custom-call | flops 15399999488 | bytes 1400000 | tf_op jit(solution)/shard_map/pallas_call | solution.py:385
  69.2 44.7 %shard_map.88 = (bf16[2,1024,2048]{2,1,0:T(8,128)(2,1)}, f32[2,1024,512]{2,1,0:T(8,128)}, f32[2,1024,512]{2,1,0:T(8,128)}, bf16[2,512,1024]{2,1,0:T(8,128)(2,1)}...) custom-call(s32[2]{0:T(128)} %pad_add_fusion.place_ref, ...), custom_call_target="tpu_custom_call" | custom-call | flops 54999998464 | bytes 5000000 | tf_op jit(solution)/shard_map/pallas_call | solution.py:570
  114.0 4.6 %collective-permute-done.28 = bf16[4,3,192,512]{3,2,1,0:T(8,128)(2,1)S(1)} collective-permute-done((bf16[4,3,192,512]{3,2,1,0:T(8,128)(2,1)}, bf16[4,3,192,512]{3,2,1,0:T(8,128)(2,1)S(1)}, u32[]{:S(2)}, u32[]{:S(2)}) %collective-permute-start.28) | collective-permute-done | bytes 2359328 | tf_op jit(solution)/shard_map/ppermute | solution.py:820
  118.6 3.2 %fusion.3 = (bf16[3,192,512]{2,1,0:T(8,128)(2,1)}, bf16[3,192,512]{2,1,0:T(8,128)(2,1)S(1)}, bf16[3,192,512]{2,1,0:T(8,128)(2,1)S(1)}, bf16[3,192,512]{2,1,0:T(8,128)(2,1)S(1)}) fusion(bf16[4,3,192,512]{3,2,1,0:T(8,128)(2,1)S(1)} %collective-permute-done.28, bf16[4,3,192,512]{3,2,1,0:T(8,128)(2,1)} %get-tuple-element.66), kind=kLoop, calls=%fused_computation.8 | loop fusion | flops 4718592 | bytes 7077888 | tf_op jit(solution)/shard_map/convert_element_type | solution.py:930
  121.8 1.8 collective-permute-start.31
  125.3 22.9 %shard_map.89 = (bf16[2,656,1024]{2,1,0:T(8,128)(2,1)}, bf16[640,512]{1,0:T(8,128)(2,1)}, bf16[32,512]{1,0:T(8,128)(2,1)}, bf16[4,1,192,512]{3,2,1,0:T(8,128)(2,1)}, bf16[4,1,192,512]{3,2,1,0:T(8,128)(2,1)}) custom-call(s32[2]{0:T(128)} %pad_add_fusion.place_ref, bf16[2,1024,512]{2,1,0:T(8,128)(2,1)} %x_ref.5, ...), custom_call_target="tpu_custom_call" | custom-call | flops 36300001280 | bytes 3300000 | tf_op jit(solution)/shard_map/pallas_call | solution.py:722
  148.3 2.7 %collective-permute-done.30 = bf16[3,192,512]{2,1,0:T(8,128)(2,1)} collective-permute-done((bf16[3,192,512]{2,1,0:T(8,128)(2,1)S(1)}, bf16[3,192,512]{2,1,0:T(8,128)(2,1)}, u32[]{:S(2)}, u32[]{:S(2)}) %collective-permute-start.30) | collective-permute-done | bytes 589856 | tf_op jit(solution)/shard_map/ppermute | solution.py:820
  151.2 1.7 add_convert_fusion
  156.7 7.7 %shard_map.90 = bf16[2,1024,512]{2,1,0:T(8,128)(2,1)} custom-call(bf16[2,1024,512]{2,1,0:T(8,128)(2,1)} %x_ref.5, f32[2,1024,512]{2,1,0:T(8,128)} %get-tuple-element.85.dmid_ref, bf16[2,656,1024]{2,1,0:T(8,128)(2,1)} %get-tuple-element.87.back_ref, bf16[656,512]{1,0:T(8,128)(2,1)} %get-tuple-element.55.turned_ref.refs_9_, ...), custom_call_target="tpu_custom_call" | custom-call | flops 8800000000 | bytes 800000 | tf_op jit(solution)/shard_map/pallas_call | solution.py:774
  166.1 2.3 %collective-permute-start.37 = (bf16[192,512]{1,0:T(8,128)(2,1)S(1)}, bf16[192,512]{1,0:T(8,128)(2,1)S(1)}, u32[]{:S(2)}, u32[]{:S(2)}) collective-permute-start(bf16[192,512]{1,0:T(8,128)(2,1)S(1)} %get-tuple-element.109), channel_id=1, source_target_pairs={{0,16},{1,17},{2,18},{3,19},{4,20},{5,21},{6,22},{7,23},{8,24},{9,... | collective-permute-start | bytes 589832 | tf_op jit(solution)/shard_map/ppermute | solution.py:820
  168.8 2.1 %collective-permute-start.38 = (bf16[192,512]{1,0:T(8,128)(2,1)S(1)}, bf16[192,512]{1,0:T(8,128)(2,1)S(1)}, u32[]{:S(2)}, u32[]{:S(2)}) collective-permute-start(bf16[192,512]{1,0:T(8,128)(2,1)S(1)} %get-tuple-element.99), channel_id=1, source_target_pairs={{0,24},{1,25},{2,26},{3,27},{4,28},{5,29},{6,30},{7,31},{8,16},{9,... | collective-permute-start | bytes 589832 | tf_op jit(solution)/shard_map/ppermute | solution.py:820
  170.9 10.1 %shard_map.91 = bf16[2,1024,512]{2,1,0:T(8,128)(2,1)} custom-call(s32[2]{0:T(128)} %counts_ref.3, f32[2,1024,512]{2,1,0:T(8,128)} %get-tuple-element.92.mid_ref, bf16[2,1024,2048]{2,1,0:T(8,128)(2,1)} %get-tuple-element.93.hid_ref, f32[32,512]{1,0:T(8,128)} %get-tuple-element.56.small_ref.refs_5_.refs_10_, bf16[2048,512]{1,0:T(8,128)(2,1)} %get-tuple-element.94.down_ref), custom_call_target="tpu_custom_call" | custom-call | flops 9900000256 | bytes 900000 | tf_op jit(solution)/shard_map/pallas_call | solution.py:799
  181.0 3.1 %collective-permute-done.38.refs_3_ = bf16[192,512]{1,0:T(8,128)(2,1)S(1)} collective-permute-done((bf16[192,512]{1,0:T(8,128)(2,1)S(1)}, bf16[192,512]{1,0:T(8,128)(2,1)S(1)}, u32[]{:S(2)}, u32[]{:S(2)}) %collective-permute-start.38) | collective-permute-done | bytes 196640 | tf_op jit(solution)/shard_map/ppermute | solution.py:820
  184.8 2.1 %shard_map.92 = f32[659,128]{1,0:T(8,128)} custom-call(s32[1]{0:T(128)} %bitcast.2.at_ref, bf16[192,512]{1,0:T(8,128)(2,1)} %get-tuple-element.95.refs_0_, bf16[192,512]{1,0:T(8,128)(2,1)} %copy-done.4, bf16[192,512]{1,0:T(8,128)(2,1)} %copy-done.3, bf16[192,512]{1,0:T(8,128)(2,1)} %copy-done.5), custom_call_target="tpu_custom_call" | custom-call | tf_op jit(solution)/shard_map/pallas_call | solution.py:974
  (145 shorter events, 23.7 us)
Async XLA Ops:
  6.3 9.9 %collective-permute-start.2 = (bf16[192,512]{1,0:T(8,128)(2,1)}, bf16[192,512]{1,0:T(8,128)(2,1)S(1)}, u32[]{:S(2)}, u32[]{:S(2)}) collective-permute-start(bf16[192,512]{1,0:T(8,128)(2,1)} %shard_map.85.refs_0_.refs_6_), channel_id=1, source_target_pairs={{0,24},{1,25},{2,26},{3,27},{4,28},{5,29},{6,30},{7,31},{8,16},{9,... | collective-permute-start | bytes 589832 | tf_op jit(solution)/shard_map/ppermute | solution.py:820
  9.9 16.6 %collective-permute-start.1 = (bf16[192,512]{1,0:T(8,128)(2,1)}, bf16[192,512]{1,0:T(8,128)(2,1)S(1)}, u32[]{:S(2)}, u32[]{:S(2)}) collective-permute-start(bf16[192,512]{1,0:T(8,128)(2,1)} %shard_map.85.refs_0_.refs_6_), channel_id=1, source_target_pairs={{0,16},{1,17},{2,18},{3,19},{4,20},{5,21},{6,22},{7,23},{8,24},{9,... | collective-permute-start | bytes 589832 | tf_op jit(solution)/shard_map/ppermute | solution.py:820
  9.9 16.6 %collective-permute-start = (bf16[192,512]{1,0:T(8,128)(2,1)}, bf16[192,512]{1,0:T(8,128)(2,1)S(1)}, u32[]{:S(2)}, u32[]{:S(2)}) collective-permute-start(bf16[192,512]{1,0:T(8,128)(2,1)} %shard_map.85.refs_0_.refs_6_), channel_id=1, source_target_pairs={{0,8},{1,9},{2,10},{3,11},{4,12},{5,13},{6,14},{7,15},{8,0},{9,1},... | collective-permute-start | bytes 589832 | tf_op jit(solution)/shard_map/ppermute | solution.py:820
  10.7 16.7 %collective-permute-start.8 = (bf16[192,512]{1,0:T(8,128)(2,1)}, bf16[192,512]{1,0:T(8,128)(2,1)S(1)}, u32[]{:S(2)}, u32[]{:S(2)}) collective-permute-start(bf16[192,512]{1,0:T(8,128)(2,1)} %shard_map.85.refs_0_.refs_6_), channel_id=1, source_target_pairs={{0,4},{1,5},{2,6},{3,7},{4,0},{5,1},{6,2},{7,3},{8,12},{9,13},{10,... | collective-permute-start | bytes 589832 | tf_op jit(solution)/shard_map/ppermute | solution.py:820
  11.4 16.1 %collective-permute-start.6 = (bf16[192,512]{1,0:T(8,128)(2,1)}, bf16[192,512]{1,0:T(8,128)(2,1)S(1)}, u32[]{:S(2)}, u32[]{:S(2)}) collective-permute-start(bf16[192,512]{1,0:T(8,128)(2,1)} %shard_map.85.refs_0_.refs_6_), channel_id=1, source_target_pairs={{0,2},{1,3},{2,0},{3,1},{4,6},{5,7},{6,4},{7,5},{8,10},{9,11},{10,... | collective-permute-start | bytes 589832 | tf_op jit(solution)/shard_map/ppermute | solution.py:820
  16.2 13.9 %collective-permute-start.5 = (bf16[192,512]{1,0:T(8,128)(2,1)}, bf16[192,512]{1,0:T(8,128)(2,1)S(1)}, u32[]{:S(2)}, u32[]{:S(2)}) collective-permute-start(bf16[192,512]{1,0:T(8,128)(2,1)} %shard_map.85.refs_0_.refs_6_), channel_id=1, source_target_pairs={{0,1},{1,0},{2,3},{3,2},{4,5},{5,4},{6,7},{7,6},{8,9},{9,8},{10,11... | collective-permute-start | bytes 589832 | tf_op jit(solution)/shard_map/ppermute | solution.py:820
  28.0 12.2 %collective-permute-start.16 = (bf16[224,512]{1,0:T(8,128)(2,1)S(1)}, bf16[224,512]{1,0:T(8,128)(2,1)S(1)}, u32[]{:S(2)}, u32[]{:S(2)}) collective-permute-start(bf16[224,512]{1,0:T(8,128)(2,1)S(1)} %pad_maximum_fusion.1.refs_8_.refs_14_), channel_id=1, source_target_pairs={{0,6},{1,7},{2,4},{3,5},{4,2},{5,3},{6,0},{7,1},{8,14},{9,15},{10,... | collective-permute-start | bytes 688136 | tf_op jit(solution)/shard_map/ppermute | solution.py:820
  28.5 12.2 %collective-permute-start.14 = (bf16[224,512]{1,0:T(8,128)(2,1)S(1)}, bf16[224,512]{1,0:T(8,128)(2,1)S(1)}, u32[]{:S(2)}, u32[]{:S(2)}) collective-permute-start(bf16[224,512]{1,0:T(8,128)(2,1)S(1)} %pad_maximum_fusion.1.refs_8_.refs_14_), channel_id=1, source_target_pairs={{0,4},{1,5},{2,6},{3,7},{4,0},{5,1},{6,2},{7,3},{8,12},{9,13},{10,... | collective-permute-start | bytes 688136 | tf_op jit(solution)/shard_map/ppermute | solution.py:820
  30.1 10.8 %collective-permute-start.12 = (bf16[224,512]{1,0:T(8,128)(2,1)S(1)}, bf16[224,512]{1,0:T(8,128)(2,1)S(1)}, u32[]{:S(2)}, u32[]{:S(2)}) collective-permute-start(bf16[224,512]{1,0:T(8,128)(2,1)S(1)} %pad_maximum_fusion.1.refs_8_.refs_14_), channel_id=1, source_target_pairs={{0,2},{1,3},{2,0},{3,1},{4,6},{5,7},{6,4},{7,5},{8,10},{9,11},{10,... | collective-permute-start | bytes 688136 | tf_op jit(solution)/shard_map/ppermute | solution.py:820
  41.9 16.5 %collective-permute-start.21 = (bf16[2,192,512]{2,1,0:T(8,128)(2,1)S(1)}, bf16[2,192,512]{2,1,0:T(8,128)(2,1)S(1)}, u32[]{:S(2)}, u32[]{:S(2)}) collective-permute-start(bf16[2,192,512]{2,1,0:T(8,128)(2,1)S(1)} %pad_maximum_fusion.refs_22_), channel_id=1, source_target_pairs={{0,4},{1,5},{2,6},{3,7},{4,0},{5,1},{6,2},{7,3},{8,12},{9,13},{10,... | collective-permute-start | bytes 1179656 | tf_op jit(solution)/shard_map/ppermute | solution.py:820
  43.2 15.3 %collective-permute-start.19 = (bf16[2,192,512]{2,1,0:T(8,128)(2,1)S(1)}, bf16[2,192,512]{2,1,0:T(8,128)(2,1)S(1)}, u32[]{:S(2)}, u32[]{:S(2)}) collective-permute-start(bf16[2,192,512]{2,1,0:T(8,128)(2,1)S(1)} %pad_maximum_fusion.refs_22_), channel_id=1, source_target_pairs={{0,2},{1,3},{2,0},{3,1},{4,6},{5,7},{6,4},{7,5},{8,10},{9,11},{10,... | collective-permute-start | bytes 1179656 | tf_op jit(solution)/shard_map/ppermute | solution.py:820
  43.7 24.3 %collective-permute-start.18 = (bf16[2,192,512]{2,1,0:T(8,128)(2,1)S(1)}, bf16[2,192,512]{2,1,0:T(8,128)(2,1)S(1)}, u32[]{:S(2)}, u32[]{:S(2)}) collective-permute-start(bf16[2,192,512]{2,1,0:T(8,128)(2,1)S(1)} %pad_maximum_fusion.refs_22_), channel_id=1, source_target_pairs={{0,1},{1,0},{2,3},{3,2},{4,5},{5,4},{6,7},{7,6},{8,9},{9,8},{10,11... | collective-permute-start | bytes 1179656 | tf_op jit(solution)/shard_map/ppermute | solution.py:820
  43.8 14.1 %collective-permute-start.24 = (bf16[192,512]{1,0:T(8,128)(2,1)S(1)}, bf16[192,512]{1,0:T(8,128)(2,1)S(1)}, u32[]{:S(2)}, u32[]{:S(2)}) collective-permute-start(bf16[192,512]{1,0:T(8,128)(2,1)S(1)} %collective-permute-done.3.refs_6_.refs_12_), channel_id=1, source_target_pairs={{16,0},{17,1},{18,2},{19,3},{20,4},{21,5},{22,6},{23,7},{24,8},{25... | collective-permute-start | bytes 589832 | tf_op jit(solution)/shard_map/ppermute | solution.py:820
  45.1 12.9 %collective-permute-start.27 = (bf16[192,512]{1,0:T(8,128)(2,1)S(1)}, bf16[192,512]{1,0:T(8,128)(2,1)S(1)}, u32[]{:S(2)}, u32[]{:S(2)}) collective-permute-start(bf16[192,512]{1,0:T(8,128)(2,1)S(1)} %collective-permute-done.26.refs_32_), channel_id=1, source_target_pairs={{0,1},{1,0},{2,3},{3,2},{4,5},{5,4},{6,7},{7,6},{8,9},{9,8},{10,11... | collective-permute-start | bytes 589832 | tf_op jit(solution)/shard_map/ppermute | solution.py:820
  57.9 10.1 %collective-permute-start.23 = (bf16[192,512]{1,0:T(8,128)(2,1)S(1)}, bf16[192,512]{1,0:T(8,128)(2,1)S(1)}, u32[]{:S(2)}, u32[]{:S(2)}) collective-permute-start(bf16[192,512]{1,0:T(8,128)(2,1)S(1)} %collective-permute-done.4.refs_28_), channel_id=1, source_target_pairs={{0,1},{1,0},{2,3},{3,2},{4,5},{5,4},{6,7},{7,6},{8,9},{9,8},{10,11... | collective-permute-start | bytes 589832 | tf_op jit(solution)/shard_map/ppermute | solution.py:820
  58.0 10.0 %collective-permute-start.25 = (bf16[192,512]{1,0:T(8,128)(2,1)S(1)}, bf16[192,512]{1,0:T(8,128)(2,1)S(1)}, u32[]{:S(2)}, u32[]{:S(2)}) collective-permute-start(bf16[192,512]{1,0:T(8,128)(2,1)S(1)} %collective-permute-done.24.refs_30_), channel_id=1, source_target_pairs={{0,1},{1,0},{2,3},{3,2},{4,5},{5,4},{6,7},{7,6},{8,9},{9,8},{10,11... | collective-permute-start | bytes 589832 | tf_op jit(solution)/shard_map/ppermute | solution.py:820
  121.8 26.5 %collective-permute-start.31 = (bf16[3,192,512]{2,1,0:T(8,128)(2,1)}, bf16[3,192,512]{2,1,0:T(8,128)(2,1)}, u32[]{:S(2)}, u32[]{:S(2)}) collective-permute-start(bf16[3,192,512]{2,1,0:T(8,128)(2,1)} %get-tuple-element.101), channel_id=1, source_target_pairs={{0,6},{1,7},{2,4},{3,5},{4,2},{5,3},{6,0},{7,1},{8,14},{9,15},{10,... | collective-permute-start | bytes 1769480 | tf_op jit(solution)/shard_map/ppermute | solution.py:820
  123.6 27.4 %collective-permute-start.30 = (bf16[3,192,512]{2,1,0:T(8,128)(2,1)S(1)}, bf16[3,192,512]{2,1,0:T(8,128)(2,1)}, u32[]{:S(2)}, u32[]{:S(2)}) collective-permute-start(bf16[3,192,512]{2,1,0:T(8,128)(2,1)S(1)} %get-tuple-element.102), channel_id=1, source_target_pairs={{0,4},{1,5},{2,6},{3,7},{4,0},{5,1},{6,2},{7,3},{8,12},{9,13},{10,... | collective-permute-start | bytes 1769480 | tf_op jit(solution)/shard_map/ppermute | solution.py:820
  124.7 26.4 %collective-permute-start.29 = (bf16[3,192,512]{2,1,0:T(8,128)(2,1)S(1)}, bf16[3,192,512]{2,1,0:T(8,128)(2,1)}, u32[]{:S(2)}, u32[]{:S(2)}) collective-permute-start(bf16[3,192,512]{2,1,0:T(8,128)(2,1)S(1)} %get-tuple-element.103), channel_id=1, source_target_pairs={{0,2},{1,3},{2,0},{3,1},{4,6},{5,7},{6,4},{7,5},{8,10},{9,11},{10,... | collective-permute-start | bytes 1769480 | tf_op jit(solution)/shard_map/ppermute | solution.py:820
  153.2 11.3 %collective-permute-start.35 = (bf16[192,512]{1,0:T(8,128)(2,1)S(1)}, bf16[192,512]{1,0:T(8,128)(2,1)S(1)}, u32[]{:S(2)}, u32[]{:S(2)}) collective-permute-start(bf16[192,512]{1,0:T(8,128)(2,1)S(1)} %get-tuple-element.105), channel_id=1, source_target_pairs={{0,6},{1,7},{2,4},{3,5},{4,2},{5,3},{6,0},{7,1},{8,14},{9,15},{10,... | collective-permute-start | bytes 589832 | tf_op jit(solution)/shard_map/ppermute | solution.py:820
  154.6 10.4 %collective-permute-start.34 = (bf16[192,512]{1,0:T(8,128)(2,1)S(1)}, bf16[192,512]{1,0:T(8,128)(2,1)S(1)}, u32[]{:S(2)}, u32[]{:S(2)}) collective-permute-start(bf16[192,512]{1,0:T(8,128)(2,1)S(1)} %get-tuple-element.106), channel_id=1, source_target_pairs={{0,4},{1,5},{2,6},{3,7},{4,0},{5,1},{6,2},{7,3},{8,12},{9,13},{10,... | collective-permute-start | bytes 589832 | tf_op jit(solution)/shard_map/ppermute | solution.py:820
  166.1 14.9 %collective-permute-start.37 = (bf16[192,512]{1,0:T(8,128)(2,1)S(1)}, bf16[192,512]{1,0:T(8,128)(2,1)S(1)}, u32[]{:S(2)}, u32[]{:S(2)}) collective-permute-start(bf16[192,512]{1,0:T(8,128)(2,1)S(1)} %get-tuple-element.109), channel_id=1, source_target_pairs={{0,16},{1,17},{2,18},{3,19},{4,20},{5,21},{6,22},{7,23},{8,24},{9,... | collective-permute-start | bytes 589832 | tf_op jit(solution)/shard_map/ppermute | solution.py:820
  168.4 12.6 %collective-permute-start.36 = (bf16[192,512]{1,0:T(8,128)(2,1)S(1)}, bf16[192,512]{1,0:T(8,128)(2,1)S(1)}, u32[]{:S(2)}, u32[]{:S(2)}) collective-permute-start(bf16[192,512]{1,0:T(8,128)(2,1)S(1)} %get-tuple-element.110), channel_id=1, source_target_pairs={{0,8},{1,9},{2,10},{3,11},{4,12},{5,13},{6,14},{7,15},{8,0},{9,1},... | collective-permute-start | bytes 589832 | tf_op jit(solution)/shard_map/ppermute | solution.py:820
  168.8 15.4 %collective-permute-start.38 = (bf16[192,512]{1,0:T(8,128)(2,1)S(1)}, bf16[192,512]{1,0:T(8,128)(2,1)S(1)}, u32[]{:S(2)}, u32[]{:S(2)}) collective-permute-start(bf16[192,512]{1,0:T(8,128)(2,1)S(1)} %get-tuple-element.99), channel_id=1, source_target_pairs={{0,24},{1,25},{2,26},{3,27},{4,28},{5,29},{6,30},{7,31},{8,16},{9,... | collective-permute-start | bytes 589832 | tf_op jit(solution)/shard_map/ppermute | solution.py:820
  (48 other events, 420.8 us)
